TPU v7x, 128 devices: a whole 4x4x4 slice. The times are simulated.
128 devices in a mesh: gx: 16 (over y, x), gy: 8 (over z, core).
Axes of the slice: x: 4, y: 4, z: 4, core: 2. Of those that a mesh axis runs over, the one named last changes fastest.
Arguments:
- concentration: float32 [24, 10, 256, 1024], P(None, None, 'gx', 'gy'), may hold values from -4 to 4
- base_volume: float32 [10, 256, 1024], P(None, 'gx', 'gy'), may hold values from 1 to 2
- flow_x: float32 [10, 256, 1024], P(None, 'gx', 'gy'), may hold values from -3 to 3
- flow_y: float32 [10, 256, 1024], P(None, 'gx', 'gy'), may hold values from -3 to 3
- face_wet_x: int32 [10, 256, 1024], P(None, 'gx', 'gy'), may hold values 0 or 1
- face_wet_y: int32 [10, 256, 1024], P(None, 'gx', 'gy'), may hold values 0 or 1
- diffusivity: float32 [9, 256, 1024], P(None, 'gx', 'gy'), may hold values from 0.05 to 2
- decay_rates: float32 [23], replicated, may hold values from 0.05 to 1.5
- inflow: float32 [24], replicated, may hold values from -2 to 2
- fine_volume: float32 [10, 4194304], P(None, ('gx', 'gy')), may hold values from 0.02 to 0.12
- fine_discharge: float32 [10, 4194304], P(None, ('gx', 'gy')), may hold values from 0 to 0.04
- cell_wet: int32 [4194304], P(('gx', 'gy')), may hold values from 0 to 1
- seg_local: int32 [4194304], P(('gx', 'gy')), may hold values from 0 to 2047
Outputs:
- updated: float32 [24, 10, 256, 1024], P(None, None, 'gx', 'gy')
All inputs are finite; a program needn't handle non-finite values. No bound on the sum of `face_wet_x` or of `face_wet_y` on one device may be relied on, other than what follows from the above.
Results may differ from a plain program's by a relative error of at most 0.0003.
Values sent between devices are 32-bit elements; how exact they have to be, the bound alone decides.
No kernel may reach another device: no remote copies, remote signals or barrier semaphores. Data moves between devices by JAX's collectives and lax.ppermute only.
A program may use at most 192 MiB of HBM per device.

v0:
```python
import functools

import jax
import jax.numpy as jnp
from jax import lax
from jax.experimental import pallas as pl
from jax.experimental.pallas import tpu as pltpu
from jax.sharding import PartitionSpec as P

SUBSTEPS = 3
STEP = 1.0 / SUBSTEPS
VMEM_BYTES = 48 * 1024 * 1024
F32 = jnp.float32
BF16 = jnp.bfloat16

VMEM = pl.BlockSpec(memory_space=pltpu.VMEM)
SMEM = pl.BlockSpec(memory_space=pltpu.SMEM)


def half_minmod(left, right):
    return jnp.minimum(
        jnp.maximum(left, jnp.minimum(right, 0.0)), jnp.maximum(right, 0.0)
    )


def roll(values, shift):
    return pltpu.roll(values, shift % values.shape[-1], values.ndim - 1)


def lanes(shape):
    return lax.broadcasted_iota(jnp.int32, shape, len(shape) - 1)


def pack_kernel(volume, discharge, wet, segment, out):
    layers = volume.shape[0]
    rows = 2 * layers + 1
    groups = wet.shape[0]
    missing = 16 * 128
    label = jnp.where(wet[...] == 1, segment[...], missing).astype(F32)
    for k in range(groups):
        out[k * rows : k * rows + layers, :] = volume[:, k * 128 : (k + 1) * 128]
        out[k * rows + layers : k * rows + 2 * layers, :] = discharge[:, k * 128 : (k + 1) * 128]
        out[k * rows + 2 * layers : (k + 1) * rows, :] = label[k : k + 1, :]


def pack_slots(volume, discharge, wet, segment):
    layers, fine = volume.shape
    groups = fine // 128
    rows = 2 * layers + 1
    step = 32 if groups % 32 == 0 else 8
    return pl.pallas_call(
        pack_kernel,
        grid=(groups // step,),
        in_specs=[
            pl.BlockSpec((layers, step * 128), lambda i: (0, i)),
            pl.BlockSpec((layers, step * 128), lambda i: (0, i)),
            pl.BlockSpec((step, 128), lambda i: (i, 0)),
            pl.BlockSpec((step, 128), lambda i: (i, 0)),
        ],
        out_specs=pl.BlockSpec((step * rows, 128), lambda i: (i, 0)),
        out_shape=jax.ShapeDtypeStruct((groups * rows, 128), F32),
        compiler_params=pltpu.CompilerParams(vmem_limit_bytes=VMEM_BYTES),
        cost_estimate=pl.CostEstimate(flops=0, bytes_accessed=8 * 10**6, transcendentals=0),
        name="pack_slots",
    )(volume, discharge, wet.reshape(groups, 128), segment.reshape(groups, 128))


def pack_columns(load, count, tile):
    packed = None
    for par in range(2):
        for row in range(16):
            k = par * 16 + row
            moved = roll(load(tile * 2 + par, row), 4 * k + 2)
            if packed is None:
                packed = moved
            else:
                packed = jnp.where(lanes(moved.shape) // 4 == k, moved, packed)
    return packed


def start_kernel(
    last, conc, flow_x, flow_y, wet_x, wet_y, state, low_x, high_x, edges_y, qx, qy
):
    layers, rows = flow_x.shape[0], flow_x.shape[1]
    subs = conc.shape[0] // (layers * rows)
    row = lax.broadcasted_iota(jnp.int32, flow_x.shape, 1)
    col = lax.broadcasted_iota(jnp.int32, flow_x.shape, 2)
    keep_x = jnp.where((row == rows - 1) & (last[0] == 1), 0.0, 1.0)
    keep_y = jnp.where((col == 127) & (last[1] == 1), 0.0, 1.0)
    qx[...] = flow_x[...] * wet_x[...].astype(F32) * keep_x
    qy[...] = flow_y[...] * wet_y[...].astype(F32) * keep_y
    high_x[...] = jnp.zeros_like(high_x)
    edges_y[...] = jnp.zeros_like(edges_y)

    def layer(l, carry):
        for i in range(rows):
            c = conc[pl.ds(l * rows + i, subs, stride=layers * rows), :]
            state[l, i] = c
            if i < 2:
                low_x[l, i] = c
            if i >= rows - 2:
                high_x[l, i - rows + 2] = c
        high_x[layers, 0, pl.ds(l, 1), :] = qx[l, rows - 1 :, :]
        return carry

    lax.fori_loop(0, layers, layer, 0)

    def tile(t, carry):
        edges_y[t] = pack_columns(lambda l, i: state[l, i], subs, t)
        flows = pack_columns(lambda l, i: roll(qy[l, i : i + 1, :], -1), 1, t)
        edges_y[layers // 2, pl.ds(t, 1), :] = flows
        return carry

    lax.fori_loop(0, layers // 2, tile, 0)


def start(last, conc, flow_x, flow_y, wet_x, wet_y):
    subs, layers, rows, cols = conc.shape
    flows = jax.ShapeDtypeStruct(flow_x.shape, F32)
    return pl.pallas_call(
        start_kernel,
        in_specs=[SMEM] + [VMEM] * 5,
        out_specs=[VMEM] * 6,
        out_shape=[
            jax.ShapeDtypeStruct((layers, rows, subs, cols), F32),
            jax.ShapeDtypeStruct((layers, 2, subs, cols), F32),
            jax.ShapeDtypeStruct((layers + 1, 2, subs, cols), F32),
            jax.ShapeDtypeStruct((layers // 2 + 1, subs, cols), F32),
            flows,
            flows,
        ],
        compiler_params=pltpu.CompilerParams(vmem_limit_bytes=VMEM_BYTES),
        cost_estimate=pl.CostEstimate(flops=10**6, bytes_accessed=8 * 10**6, transcendentals=0),
        name="start_state",
    )(last, conc.reshape(subs * layers * rows, cols), flow_x, flow_y, wet_x, wet_y)


def edge_fluxes(own, left, right, flows_own, flows_left, inserts, fluxes):
    shape = own.shape
    place = lanes(shape) % 4

    def flux(four, flows):
        steps = 0.5 * (roll(four, -1) - four)
        slope = half_minmod(steps, roll(steps, -1))
        before = roll(four, -1) + slope
        after = roll(four, -2) - roll(slope, -1)
        return jnp.maximum(flows, 0.0) * before + jnp.minimum(flows, 0.0) * after

    first = jnp.where(place < 2, left, own)
    last = jnp.where(place < 2, own, right)
    inserts[...] = jnp.where(place == 0, roll(last, -2), first)
    fluxes[...] = jnp.where(place == 0, flux(last, flows_own), roll(flux(first, flows_left), 1))


def edge_pass(edges, edges_left, edges_right, flow_edges, flow_left, inserts, fluxes):
    tiles = inserts.shape[0]
    edge_fluxes(
        edges[:tiles],
        edges_left[:tiles],
        edges_right[:tiles],
        flow_edges[tiles, :tiles, :][:, None, :],
        flow_left[tiles, :tiles, :][:, None, :],
        inserts,
        fluxes,
    )


def divergence_layer(state, west, east, inserts, fluxes, qx, qx_west, qy, tile, par, emit):
    l = tile * 2 + par
    rows = qx.shape[1]
    lane = lanes(state.shape[2:])

    def get(i):
        if i < 0:
            return west[l, i + 2]
        if i >= rows:
            return east[l, i - rows]
        return state[l, i]

    before, here = (get(-2), get(-1))
    step = 0.5 * (here - before)
    flux = None
    left = None
    for i in range(-1, rows + 1):
        after = get(i + 1)
        step_after = 0.5 * (after - here)
        slope = half_minmod(step, step_after)
        right = here - slope
        if i >= 0:
            q = qx_west if i == 0 else qx[l, i - 1 : i, :]
            new_flux = jnp.maximum(q, 0.0) * left + jnp.minimum(q, 0.0) * right
            if i >= 1:
                c = before
                edge = 127 - 4 * (par * 16 + i - 1)
                insert = roll(inserts[tile], edge)
                cl = jnp.where(lane == 0, insert, roll(c, 1))
                cr = jnp.where(lane == 127, insert, roll(c, -1))
                slope_y = half_minmod(0.5 * (c - cl), 0.5 * (cr - c))
                qr = qy[l, i - 1 : i, :]
                fy = jnp.maximum(qr, 0.0) * (c + slope_y) + jnp.minimum(qr, 0.0) * roll(
                    c - slope_y, -1
                )
                flux_edge = roll(fluxes[tile], edge)
                fm = jnp.where(lane == 0, flux_edge, roll(fy, 1))
                fy = jnp.where(lane == 127, flux_edge, fy)
                emit(l, i - 1, c, (new_flux - flux) + (fy - fm))
            flux = new_flux
        left = here + slope
        before, here, step = (here, after, step_after)


def first_divergence_kernel(
    state, west, east, edges, edges_left, edges_right, qx, qy, div, inserts, fluxes
):
    layers = qx.shape[0]
    edge_pass(edges, edges_left, edges_right, edges, edges_left, inserts, fluxes)

    def emit(l, i, c, value):
        div[l, i] = value

    def tile(t, carry):
        for par in range(2):
            qx_west = west[layers, 0, pl.ds(t * 2 + par, 1), :]
            divergence_layer(
                state, west, east, inserts, fluxes, qx, qx_west, qy, t, par, emit
            )
        return carry

    lax.fori_loop(0, layers // 2, tile, 0)


def first_divergence(state, west, east, edges, edges_left, edges_right, qx, qy):
    layers, rows, subs, cols = state.shape
    tiles = pltpu.VMEM((layers // 2, subs, cols), F32)
    return pl.pallas_call(
        first_divergence_kernel,
        in_specs=[VMEM] * 8,
        out_specs=VMEM,
        out_shape=jax.ShapeDtypeStruct(state.shape, F32),
        scratch_shapes=[tiles, tiles],
        compiler_params=pltpu.CompilerParams(vmem_limit_bytes=VMEM_BYTES),
        cost_estimate=pl.CostEstimate(flops=2 * 10**7, bytes_accessed=10**7, transcendentals=0),
        name="first_divergence",
    )(state, west, east, edges, edges_left, edges_right, qx, qy)


def explicit_value(c, div, rates, rates_before, inflow, renewal, scale):
    carried = pltpu.roll(c, 1, 0)
    return (
        c
        + ((renewal * (inflow - c) - scale * div) + (rates_before * carried - rates * c))
    )


def solve_row(star, row, coef, out, emit):
    layers = coef.shape[1]

    def get(which, l):
        return coef[which, l, pl.ds(row, 1), :]

    forward = [star[0, row]]
    for l in range(1, layers):
        forward.append(star[l, row] - get(0, l) * forward[l - 1])
    value = forward[layers - 1] * get(1, layers - 1)
    emit(layers - 1, row, value)
    for l in range(layers - 2, -1, -1):
        value = (forward[l] + get(2, l) * value) * get(1, l)
        emit(l, row, value)


def emit_edges(state, low_x, high_x, edges_y):
    layers, rows = state.shape[0], state.shape[1]
    low_x[...] = state[:, :2]
    high_x[...] = state[:, rows - 2 :]

    def tile(t, carry):
        edges_y[t] = pack_columns(lambda l, i: state[l, i], 0, t)
        return carry

    lax.fori_loop(0, layers // 2, tile, 0)


def aggregate(slots, spread, hot, total):
    rows = 21
    groups = slots.shape[0] // rows
    step = 8
    sub8 = lax.broadcasted_iota(jnp.int32, (8, 128), 0)
    column = lax.broadcasted_iota(jnp.int32, (128, 128), 0)
    total[...] = jnp.zeros_like(total)

    def chunk(it, carry):
        base = pl.multiple_of(it * (step * rows), 8)
        for j in range(step):
            at = base + j * rows
            label = slots[pl.ds(at + 20, 1), :].astype(jnp.int32)
            mask = jnp.where(jnp.broadcast_to((label >> 7) & 7, (8, 128)) == sub8, 1.0, 0.0)
            mask = jnp.concatenate([mask, mask], axis=0).astype(BF16)
            for ch in range(20):
                value = jnp.broadcast_to(slots[pl.ds(at + ch, 1), :], (8, 128))
                high = value.astype(BF16).astype(F32)
                both = jnp.concatenate([high, value - high], axis=0).astype(BF16)
                spread[ch * 16 : (ch + 1) * 16, j * 128 : (j + 1) * 128] = both * mask
            same = (label & 127) == column
            half = label >> 10
            for h in range(2):
                hit = jnp.where(same, jnp.where(half == h, 1.0, 0.0), 0.0).astype(BF16)
                hot[h * 128 : (h + 1) * 128, j * 128 : (j + 1) * 128] = hit
        total[...] += lax.dot_general(
            spread[...], hot[...], (((1,), (1,)), ((), ())), preferred_element_type=F32
        )
        return carry

    lax.fori_loop(0, groups // step, chunk, 0)


def first_step_kernel(
    slots,
    base_volume,
    diffusivity,
    state,
    div,
    rates,
    rates_before,
    inflow,
    new,
    low_x,
    high_x,
    edges_y,
    coef,
    spread,
    hot,
    total,
    star,
):
    layers, rows = base_volume.shape[0], base_volume.shape[1]
    aggregate(slots, spread, hot, total)
    uppers, downs = ([], [])
    for l in range(layers):
        parts = []
        for ch in (l, layers + l):
            parts.append(
                jnp.concatenate(
                    [
                        total[ch * 16 : ch * 16 + 8, h * 128 : (h + 1) * 128]
                        + total[ch * 16 + 8 : ch * 16 + 16, h * 128 : (h + 1) * 128]
                        for h in range(2)
                    ],
                    axis=0,
                )
            )
        scale = STEP / (base_volume[l] + parts[0])
        coef[3, l] = scale
        coef[4, l] = scale * parts[1]
        uppers.append(scale * diffusivity[l] if l < layers - 1 else jnp.zeros_like(scale))
        downs.append(scale * diffusivity[l - 1] if l > 0 else jnp.zeros_like(scale))
    pivot = 1.0 + uppers[0]
    coef[0, 0] = jnp.zeros_like(pivot)
    for l in range(layers):
        inverse = 1.0 / pivot
        coef[1, l] = inverse
        coef[2, l] = uppers[l]
        if l + 1 < layers:
            factor = -downs[l + 1] * inverse
            coef[0, l + 1] = factor
            pivot = 1.0 + uppers[l + 1] + downs[l + 1] + factor * uppers[l]

    def explicit(l, carry):
        for i in range(rows):
            star[l, i] = explicit_value(
                state[l, i],
                div[l, i],
                rates[...],
                rates_before[...],
                inflow[...],
                coef[4, l, i : i + 1, :],
                coef[3, l, i : i + 1, :],
            )
        return carry

    lax.fori_loop(0, layers, explicit, 0)

    def emit(l, i, value):
        new[l, i] = value

    def row(i, carry):
        solve_row(star, i, coef, new, emit)
        return carry

    lax.fori_loop(0, rows, row, 0)
    emit_edges(new, low_x, high_x, edges_y)


def state_shapes(shape):
    layers, rows, subs, cols = shape
    return [
        jax.ShapeDtypeStruct(shape, F32),
        jax.ShapeDtypeStruct((layers, 2, subs, cols), F32),
        jax.ShapeDtypeStruct((layers, 2, subs, cols), F32),
        jax.ShapeDtypeStruct((layers // 2, subs, cols), F32),
    ]


def first_step(slots, base_volume, diffusivity, state, div, rates, rates_before, inflow):
    layers, rows, subs, cols = state.shape
    return pl.pallas_call(
        first_step_kernel,
        in_specs=[VMEM] * 8,
        out_specs=[VMEM] * 5,
        out_shape=state_shapes(state.shape)
        + [jax.ShapeDtypeStruct((5, layers, rows, cols), F32)],
        scratch_shapes=[
            pltpu.VMEM((2 * layers * 16, 1024), BF16),
            pltpu.VMEM((256, 1024), BF16),
            pltpu.VMEM((2 * layers * 16, 256), F32),
            pltpu.VMEM(state.shape, F32),
        ],
        compiler_params=pltpu.CompilerParams(vmem_limit_bytes=VMEM_BYTES),
        cost_estimate=pl.CostEstimate(flops=10**9, bytes_accessed=10**7, transcendentals=0),
        name="aggregate_and_first_step",
    )(slots, base_volume, diffusivity, state, div, rates, rates_before, inflow)


def later_step_kernel(
    final,
    state,
    west,
    east,
    edges,
    edges_left,
    edges_right,
    flow_west,
    flow_edges,
    flow_left,
    qx,
    qy,
    coef,
    rates,
    rates_before,
    inflow,
    *refs,
):
    layers, rows = qx.shape[0], qx.shape[1]
    if final:
        out, inserts, fluxes, star = refs
        subs = out.shape[0] // (layers * rows)
    else:
        new, low_x, high_x, edges_y, inserts, fluxes, star = refs
    edge_pass(edges, edges_left, edges_right, flow_edges, flow_left, inserts, fluxes)

    def explicit(l, i, c, div):
        star[l, i] = explicit_value(
            c,
            div,
            rates[...],
            rates_before[...],
            inflow[...],
            coef[4, l, i : i + 1, :],
            coef[3, l, i : i + 1, :],
        )

    def tile(t, carry):
        for par in range(2):
            qx_west = flow_west[layers, 0, pl.ds(t * 2 + par, 1), :]
            divergence_layer(
                state, west, east, inserts, fluxes, qx, qx_west, qy, t, par, explicit
            )
        return carry

    lax.fori_loop(0, layers // 2, tile, 0)

    def emit(l, i, value):
        if final:
            out[pl.ds(l * rows + i, subs, stride=layers * rows), :] = value
        else:
            new[l, i] = value

    def row(i, carry):
        solve_row(star, i, coef, None, emit)
        return carry

    lax.fori_loop(0, rows, row, 0)
    if not final:
        emit_edges(new, low_x, high_x, edges_y)


def later_step(final, state, *args):
    layers, rows, subs, cols = state.shape
    tiles = pltpu.VMEM((layers // 2, subs, cols), F32)
    if final:
        shapes = jax.ShapeDtypeStruct((subs * layers * rows, cols), F32)
        specs = VMEM
    else:
        shapes = state_shapes(state.shape)
        specs = [VMEM] * 4
    return pl.pallas_call(
        functools.partial(later_step_kernel, final),
        in_specs=[VMEM] * 15,
        out_specs=specs,
        out_shape=shapes,
        scratch_shapes=[tiles, tiles, pltpu.VMEM(state.shape, F32)],
        compiler_params=pltpu.CompilerParams(vmem_limit_bytes=VMEM_BYTES),
        cost_estimate=pl.CostEstimate(flops=3 * 10**7, bytes_accessed=10**7, transcendentals=0),
        name="last_step" if final else "middle_step",
    )(state, *args)


def to_next(values, axis):
    size = lax.axis_size(axis)
    return lax.ppermute(values, axis, [(i, i + 1) for i in range(size - 1)])


def to_previous(values, axis):
    size = lax.axis_size(axis)
    return lax.ppermute(values, axis, [(i + 1, i) for i in range(size - 1)])


def exchange(low_x, high_x, edges_y):
    west = to_next(high_x, "gx")
    east = to_previous(low_x, "gx")
    left = to_next(edges_y, "gy")
    right = to_previous(edges_y, "gy")
    return (west, east, left, right)


def local(
    concentration,
    base_volume,
    flow_x,
    flow_y,
    face_wet_x,
    face_wet_y,
    diffusivity,
    decay_rates,
    inflow,
    fine_volume,
    fine_discharge,
    cell_wet,
    seg_local,
):
    subs, layers, rows, cols = concentration.shape
    size_x, size_y = (lax.axis_size("gx"), lax.axis_size("gy"))
    owners = size_x * size_y
    sent = pack_slots(fine_volume, fine_discharge, cell_wet, seg_local)
    arrived = lax.all_to_all(
        sent.reshape(owners, 1, -1), ("gx", "gy"), split_axis=0, concat_axis=0, tiled=True
    ).reshape(sent.shape)

    last = jnp.stack(
        [
            (lax.axis_index("gx") == size_x - 1).astype(jnp.int32),
            (lax.axis_index("gy") == size_y - 1).astype(jnp.int32),
        ]
    )
    rates = jnp.concatenate([jnp.zeros((1,), F32), decay_rates]) * STEP
    rates_before = jnp.concatenate([jnp.zeros((1,), F32), rates[:-1]])
    rates, rates_before, inflow = (
        jnp.broadcast_to(v[:, None], (subs, cols)) for v in (rates, rates_before, inflow)
    )
    state, low_x, high_x, edges, qx, qy = start(
        last, concentration, flow_x, flow_y, face_wet_x, face_wet_y
    )
    west, east, left, right = exchange(low_x, high_x, edges)
    flow_west, flow_edges, flow_left = (west, edges, left)
    div = first_divergence(state, west, east, edges, left, right, qx, qy)
    state, low_x, high_x, edges, coef = first_step(
        arrived, base_volume, diffusivity, state, div, rates, rates_before, inflow
    )
    for step in range(1, SUBSTEPS):
        final = step == SUBSTEPS - 1
        halos = exchange(low_x, high_x, edges)
        result = later_step(
            final,
            state,
            halos[0],
            halos[1],
            edges,
            halos[2],
            halos[3],
            flow_west,
            flow_edges,
            flow_left,
            qx,
            qy,
            coef,
            rates,
            rates_before,
            inflow,
        )
        if not final:
            state, low_x, high_x, edges = result
    return result.reshape(concentration.shape)


def solution(mesh):
    fine = P(None, ("gx", "gy"))
    block = P(None, "gx", "gy")
    return jax.shard_map(
        local,
        mesh=mesh,
        in_specs=(
            P(None, None, "gx", "gy"),
            block,
            block,
            block,
            block,
            block,
            block,
            P(),
            P(),
            fine,
            fine,
            P(("gx", "gy")),
            P(("gx", "gy")),
        ),
        out_specs=P(None, None, "gx", "gy"),
        check_vma=False,
    )
```

profile of v0, /device:TPU:56, one launch (start us, length us, event | category | flops | bytes accessed | tf_op | source)
XLA Modules:
  0.0 171.5 jit_solution(847007105745542838)
XLA Ops:
  5.0 3.4 %pack_slots.1 = f32[5376,128]{1,0:T(8,128)} custom-call(f32[10,32768]{1,0:T(8,128)S(1)} %copy-done.1, f32[10,32768]{1,0:T(8,128)S(1)} %copy-done.2, s32[256,128]{1,0:T(8,128)S(1)} %bitcast.10, s32[256,128]{1,0:T(8,128)S(1)} %bitcast.11), custom_call_target="tpu_custom_call" | custom-call | bytes 8000000 | tf_op jit(solution)/shard_map/pack_slots/pallas_call | solution.py:51
  8.4 10.5 %all-to-all-start = ((f32[128,1,5376]{2,1,0:T(1,128)}), f32[128,1,5376]{2,1,0:T(1,128)}, u32[]{:S(2)}, u32[]{:S(2)}) async-start(f32[128,1,5376]{2,1,0:T(1,128)} %bitcast.12), calls=%async_computation | async-start | bytes 5505024 | tf_op jit(solution)/shard_map/all_to_all | solution.py:544
  20.6 3.1 %start_state.1 = (f32[10,16,24,128]{3,2,1,0:T(8,128)S(1)}, f32[10,2,24,128]{3,2,1,0:T(8,128)S(1)}, f32[11,2,24,128]{3,2,1,0:T(8,128)S(1)}, f32[6,24,128]{2,1,0:T...) custom-call(s32[2]{0:T(128)S(1)} %add_convert_fusion.last, f32[3840,128]{1,0:T(8,128)S(1)} %bitcast.9, ...), custom_call_target="tpu_custom_call" | custom-call | flops 1000000 | bytes 8000000 | tf_op jit(solution)/shard_map/start_state/pallas_call | solution.py:120
  23.7 3.4 %collective-permute-start = (f32[11,2,24,128]{3,2,1,0:T(8,128)S(1)}, f32[11,2,24,128]{3,2,1,0:T(8,128)S(1)}, u32[]{:S(2)}, u32[]{:S(2)}) collective-permute-start(f32[11,2,24,128]{3,2,1,0:T(8,128)S(1)} %get-tuple-element.21), channel_id=1, source_target_pairs={{0,8},{8,16},{16,24},{24,32},{32,40},{40,48},{48,56},{56,64},{64,7... | collective-permute-start | bytes 811016 | tf_op jit(solution)/shard_map/ppermute | solution.py:509
  27.1 4.6 %collective-permute-start.1 = (f32[10,2,24,128]{3,2,1,0:T(8,128)S(1)}, f32[10,2,24,128]{3,2,1,0:T(8,128)S(1)}, u32[]{:S(2)}, u32[]{:S(2)}) collective-permute-start(f32[10,2,24,128]{3,2,1,0:T(8,128)S(1)} %get-tuple-element.22), channel_id=1, source_target_pairs={{8,0},{16,8},{24,16},{32,24},{40,32},{48,40},{56,48},{64,56},{72,6... | collective-permute-start | bytes 737288 | tf_op jit(solution)/shard_map/ppermute | solution.py:514
  31.7 1.9 %collective-permute-start.3 = (f32[6,24,128]{2,1,0:T(8,128)S(1)}, f32[6,24,128]{2,1,0:T(8,128)S(1)}, u32[]{:S(2)}, u32[]{:S(2)}) collective-permute-start(f32[6,24,128]{2,1,0:T(8,128)S(1)} %get-tuple-element.23.edges.flow_edges), channel_id=1, source_target_pairs={{1,0},{2,1},{3,2},{4,3},{5,4},{6,5},{7,6},{9,8},{10,9},{11,10},{12... | collective-permute-start | bytes 221192 | tf_op jit(solution)/shard_map/ppermute | solution.py:514
  33.6 2.4 %collective-permute-start.2 = (f32[6,24,128]{2,1,0:T(8,128)S(1)}, f32[6,24,128]{2,1,0:T(8,128)S(1)}, u32[]{:S(2)}, u32[]{:S(2)}) collective-permute-start(f32[6,24,128]{2,1,0:T(8,128)S(1)} %get-tuple-element.23.edges.flow_edges), channel_id=1, source_target_pairs={{0,1},{1,2},{2,3},{3,4},{4,5},{5,6},{6,7},{8,9},{9,10},{10,11},{11... | collective-permute-start | bytes 221192 | tf_op jit(solution)/shard_map/ppermute | solution.py:509
  36.2 2.4 %collective-permute-done.3.edges_right = f32[6,24,128]{2,1,0:T(8,128)S(1)} collective-permute-done((f32[6,24,128]{2,1,0:T(8,128)S(1)}, f32[6,24,128]{2,1,0:T(8,128)S(1)}, u32[]{:S(2)}, u32[]{:S(2)}) %collective-permute-start.3) | collective-permute-done | bytes 73760 | tf_op jit(solution)/shard_map/ppermute | solution.py:514
  38.6 11.5 %collective-permute-done.2.edges_left.flow_left = f32[6,24,128]{2,1,0:T(8,128)S(1)} collective-permute-done((f32[6,24,128]{2,1,0:T(8,128)S(1)}, f32[6,24,128]{2,1,0:T(8,128)S(1)}, u32[]{:S(2)}, u32[]{:S(2)}) %collective-permute-start.2) | collective-permute-done | bytes 73760 | tf_op jit(solution)/shard_map/ppermute | solution.py:509
  50.0 5.1 %collective-permute-done.1.east = f32[10,2,24,128]{3,2,1,0:T(8,128)S(1)} collective-permute-done((f32[10,2,24,128]{3,2,1,0:T(8,128)S(1)}, f32[10,2,24,128]{3,2,1,0:T(8,128)S(1)}, u32[]{:S(2)}, u32[]{:S(2)}) %collective-permute-start.1) | collective-permute-done | bytes 245792 | tf_op jit(solution)/shard_map/ppermute | solution.py:514
  55.1 2.0 %collective-permute-done.west.flow_west = f32[11,2,24,128]{3,2,1,0:T(8,128)S(1)} collective-permute-done((f32[11,2,24,128]{3,2,1,0:T(8,128)S(1)}, f32[11,2,24,128]{3,2,1,0:T(8,128)S(1)}, u32[]{:S(2)}, u32[]{:S(2)}) %collective-permute-start) | collective-permute-done | bytes 270368 | tf_op jit(solution)/shard_map/ppermute | solution.py:509
  57.1 17.9 %first_divergence.1.div = f32[10,16,24,128]{3,2,1,0:T(8,128)S(1)} custom-call(f32[10,16,24,128]{3,2,1,0:T(8,128)S(1)} %get-tuple-element.20.state, f32[11,2,24,128]{3,2,1,0:T(8,128)S(1)} %collective-permute-done.west.flow_west, f32[10,2,24,128]{3,2,1,0:T(8,128)S(1)} %collective-permute-done.1.east, f32[6,24,128]{2,1,0:T(8,128)S(1)} %get-tuple-element.23.edges.flow_edges, ...), custom_call_target="tpu_custom_call" | custom-call | flops 20000000 | bytes 10000000 | tf_op jit(solution)/shard_map/first_divergence/pallas_call | solution.py:235
  76.5 23.8 %aggregate_and_first_step.1 = (f32[10,16,24,128]{3,2,1,0:T(8,128)S(1)}, f32[10,2,24,128]{3,2,1,0:T(8,128)S(1)}, f32[10,2,24,128]{3,2,1,0:T(8,128)S(1)}, f32[5,24,128]{2,1,0:T(8,128)S(1)}, f32[5,10,16,128]{3,2,1,0:T(8,128)S(1)}) custom-call(f32[5376,128]{1,0:T(8,128)} %bitcast.3.slots, f32[10,16,128]{2,1,0:T(8,128)S(1)} %copy-done.10, ...), custom_call_target="tpu_custom_call" | custom-call | flops 1000000000 | bytes 10000000 | tf_op jit(solution)/shard_map/aggregate_and_first_step/pallas_call | solution.py:405
  100.3 1.9 %collective-permute-start.4 = (f32[10,2,24,128]{3,2,1,0:T(8,128)S(1)}, f32[10,2,24,128]{3,2,1,0:T(8,128)S(1)}, u32[]{:S(2)}, u32[]{:S(2)}) collective-permute-start(f32[10,2,24,128]{3,2,1,0:T(8,128)S(1)} %get-tuple-element.27), channel_id=1, source_target_pairs={{0,8},{8,16},{16,24},{24,32},{32,40},{40,48},{48,56},{56,64},{64,7... | collective-permute-start | bytes 737288 | tf_op jit(solution)/shard_map/ppermute | solution.py:509
  102.2 6.0 %collective-permute-start.5 = (f32[10,2,24,128]{3,2,1,0:T(8,128)S(1)}, f32[10,2,24,128]{3,2,1,0:T(8,128)S(1)}, u32[]{:S(2)}, u32[]{:S(2)}) collective-permute-start(f32[10,2,24,128]{3,2,1,0:T(8,128)S(1)} %get-tuple-element.28), channel_id=1, source_target_pairs={{8,0},{16,8},{24,16},{32,24},{40,32},{48,40},{56,48},{64,56},{72,6... | collective-permute-start | bytes 737288 | tf_op jit(solution)/shard_map/ppermute | solution.py:514
  108.3 1.9 %collective-permute-start.7 = (f32[5,24,128]{2,1,0:T(8,128)S(1)}, f32[5,24,128]{2,1,0:T(8,128)S(1)}, u32[]{:S(2)}, u32[]{:S(2)}) collective-permute-start(f32[5,24,128]{2,1,0:T(8,128)S(1)} %get-tuple-element.29.edges), channel_id=1, source_target_pairs={{1,0},{2,1},{3,2},{4,3},{5,4},{6,5},{7,6},{9,8},{10,9},{11,10},{12... | collective-permute-start | bytes 184328 | tf_op jit(solution)/shard_map/ppermute | solution.py:514
  110.2 2.4 %collective-permute-start.6 = (f32[5,24,128]{2,1,0:T(8,128)S(1)}, f32[5,24,128]{2,1,0:T(8,128)S(1)}, u32[]{:S(2)}, u32[]{:S(2)}) collective-permute-start(f32[5,24,128]{2,1,0:T(8,128)S(1)} %get-tuple-element.29.edges), channel_id=1, source_target_pairs={{0,1},{1,2},{2,3},{3,4},{4,5},{5,6},{6,7},{8,9},{9,10},{10,11},{11... | collective-permute-start | bytes 184328 | tf_op jit(solution)/shard_map/ppermute | solution.py:509
  112.6 3.1 %collective-permute-done.6.edges_left = f32[5,24,128]{2,1,0:T(8,128)S(1)} collective-permute-done((f32[5,24,128]{2,1,0:T(8,128)S(1)}, f32[5,24,128]{2,1,0:T(8,128)S(1)}, u32[]{:S(2)}, u32[]{:S(2)}) %collective-permute-start.6) | collective-permute-done | bytes 61472 | tf_op jit(solution)/shard_map/ppermute | solution.py:509
  115.7 19.3 %middle_step.1 = (f32[10,16,24,128]{3,2,1,0:T(8,128)S(1)}, f32[10,2,24,128]{3,2,1,0:T(8,128)S(1)}, f32[10,2,24,128]{3,2,1,0:T(8,128)S(1)}, f32[5,24,128]{2,1,0:T(8,128)S(1)}) custom-call(f32[10,16,24,128]{3,2,1,0:T(8,128)S(1)} %get-tuple-element.26.state, f32[10,2,24,128]{3,2,1,0:T(8,128)S(1)} %collective-permute-done.4.west, ...), custom_call_target="tpu_custom_call" | custom-call | flops 30000000 | bytes 10000000 | tf_op jit(solution)/shard_map/middle_step/pallas_call | solution.py:495
  135.1 1.9 %collective-permute-start.8 = (f32[10,2,24,128]{3,2,1,0:T(8,128)S(1)}, f32[10,2,24,128]{3,2,1,0:T(8,128)S(1)}, u32[]{:S(2)}, u32[]{:S(2)}) collective-permute-start(f32[10,2,24,128]{3,2,1,0:T(8,128)S(1)} %get-tuple-element.32), channel_id=1, source_target_pairs={{0,8},{8,16},{16,24},{24,32},{32,40},{40,48},{48,56},{56,64},{64,7... | collective-permute-start | bytes 737288 | tf_op jit(solution)/shard_map/ppermute | solution.py:509
  137.0 6.0 %collective-permute-start.9 = (f32[10,2,24,128]{3,2,1,0:T(8,128)S(1)}, f32[10,2,24,128]{3,2,1,0:T(8,128)S(1)}, u32[]{:S(2)}, u32[]{:S(2)}) collective-permute-start(f32[10,2,24,128]{3,2,1,0:T(8,128)S(1)} %get-tuple-element.33), channel_id=1, source_target_pairs={{8,0},{16,8},{24,16},{32,24},{40,32},{48,40},{56,48},{64,56},{72,6... | collective-permute-start | bytes 737288 | tf_op jit(solution)/shard_map/ppermute | solution.py:514
  145.0 2.4 %collective-permute-start.10 = (f32[5,24,128]{2,1,0:T(8,128)S(1)}, f32[5,24,128]{2,1,0:T(8,128)S(1)}, u32[]{:S(2)}, u32[]{:S(2)}) collective-permute-start(f32[5,24,128]{2,1,0:T(8,128)S(1)} %get-tuple-element.34.edges), channel_id=1, source_target_pairs={{0,1},{1,2},{2,3},{3,4},{4,5},{5,6},{6,7},{8,9},{9,10},{10,11},{11... | collective-permute-start | bytes 184328 | tf_op jit(solution)/shard_map/ppermute | solution.py:509
  147.4 3.1 %collective-permute-done.10.edges_left = f32[5,24,128]{2,1,0:T(8,128)S(1)} collective-permute-done((f32[5,24,128]{2,1,0:T(8,128)S(1)}, f32[5,24,128]{2,1,0:T(8,128)S(1)}, u32[]{:S(2)}, u32[]{:S(2)}) %collective-permute-start.10) | collective-permute-done | bytes 61472 | tf_op jit(solution)/shard_map/ppermute | solution.py:509
  150.5 21.0 %last_step.1 = f32[3840,128]{1,0:T(8,128)} custom-call(f32[10,16,24,128]{3,2,1,0:T(8,128)S(1)} %get-tuple-element.31.state, f32[10,2,24,128]{3,2,1,0:T(8,128)S(1)} %collective-permute-done.8.west, f32[10,2,24,128]{3,2,1,0:T(8,128)S(1)} %collective-permute-done.9.east, f32[5,24,128]{2,1,0:T(8,128)S(1)} %get-tuple-element.34.edges, ...), custom_call_target="tpu_custom_call" | custom-call | flops 30000000 | bytes 10000000 | tf_op jit(solution)/shard_map/last_step/pallas_call | solution.py:495
  (42 shorter events, 10.2 us)
Async XLA Ops:
  0.0 1.6 copy-start.1
  1.6 1.6 copy-start.2
  8.4 10.6 %copy-start.6 = (f32[10,16,128]{2,1,0:T(8,128)S(1)}, f32[10,16,128]{2,1,0:T(8,128)}, u32[]{:S(2)}) copy-start(f32[10,16,128]{2,1,0:T(8,128)} %flow_x.1) | copy-start | bytes 245764
  8.4 10.6 %copy-start.7 = (f32[10,16,128]{2,1,0:T(8,128)S(1)}, f32[10,16,128]{2,1,0:T(8,128)}, u32[]{:S(2)}) copy-start(f32[10,16,128]{2,1,0:T(8,128)} %flow_y.1) | copy-start | bytes 245764
  8.4 10.6 %copy-start.8 = (s32[10,16,128]{2,1,0:T(8,128)S(1)}, s32[10,16,128]{2,1,0:T(8,128)}, u32[]{:S(2)}) copy-start(s32[10,16,128]{2,1,0:T(8,128)} %wet_x.1) | copy-start | bytes 245764
  8.4 10.6 %copy-start.9 = (s32[10,16,128]{2,1,0:T(8,128)S(1)}, s32[10,16,128]{2,1,0:T(8,128)}, u32[]{:S(2)}) copy-start(s32[10,16,128]{2,1,0:T(8,128)} %wet_y.1) | copy-start | bytes 245764
  8.4 67.8 %all-to-all-start = ((f32[128,1,5376]{2,1,0:T(1,128)}), f32[128,1,5376]{2,1,0:T(1,128)}, u32[]{:S(2)}, u32[]{:S(2)}) async-start(f32[128,1,5376]{2,1,0:T(1,128)} %bitcast.12), calls=%async_computation | async-start | bytes 5505024 | tf_op jit(solution)/shard_map/all_to_all | solution.py:544
  18.9 17.1 %copy-start.13 = (f32[23]{0:T(128)S(1)}, f32[23]{0:T(128)}, u32[]{:S(2)}) copy-start(f32[23]{0:T(128)} %param.20) | copy-start | bytes 280
  19.1 1.5 copy-start.3
  23.7 33.4 %collective-permute-start = (f32[11,2,24,128]{3,2,1,0:T(8,128)S(1)}, f32[11,2,24,128]{3,2,1,0:T(8,128)S(1)}, u32[]{:S(2)}, u32[]{:S(2)}) collective-permute-start(f32[11,2,24,128]{3,2,1,0:T(8,128)S(1)} %get-tuple-element.21), channel_id=1, source_target_pairs={{0,8},{8,16},{16,24},{24,32},{32,40},{40,48},{48,56},{56,64},{64,7... | collective-permute-start | bytes 811016 | tf_op jit(solution)/shard_map/ppermute | solution.py:509
  27.1 28.0 %collective-permute-start.1 = (f32[10,2,24,128]{3,2,1,0:T(8,128)S(1)}, f32[10,2,24,128]{3,2,1,0:T(8,128)S(1)}, u32[]{:S(2)}, u32[]{:S(2)}) collective-permute-start(f32[10,2,24,128]{3,2,1,0:T(8,128)S(1)} %get-tuple-element.22), channel_id=1, source_target_pairs={{8,0},{16,8},{24,16},{32,24},{40,32},{48,40},{56,48},{64,56},{72,6... | collective-permute-start | bytes 737288 | tf_op jit(solution)/shard_map/ppermute | solution.py:514
  31.7 6.9 %collective-permute-start.3 = (f32[6,24,128]{2,1,0:T(8,128)S(1)}, f32[6,24,128]{2,1,0:T(8,128)S(1)}, u32[]{:S(2)}, u32[]{:S(2)}) collective-permute-start(f32[6,24,128]{2,1,0:T(8,128)S(1)} %get-tuple-element.23.edges.flow_edges), channel_id=1, source_target_pairs={{1,0},{2,1},{3,2},{4,3},{5,4},{6,5},{7,6},{9,8},{10,9},{11,10},{12... | collective-permute-start | bytes 221192 | tf_op jit(solution)/shard_map/ppermute | solution.py:514
  33.6 16.4 %collective-permute-start.2 = (f32[6,24,128]{2,1,0:T(8,128)S(1)}, f32[6,24,128]{2,1,0:T(8,128)S(1)}, u32[]{:S(2)}, u32[]{:S(2)}) collective-permute-start(f32[6,24,128]{2,1,0:T(8,128)S(1)} %get-tuple-element.23.edges.flow_edges), channel_id=1, source_target_pairs={{0,1},{1,2},{2,3},{3,4},{4,5},{5,6},{6,7},{8,9},{9,10},{10,11},{11... | collective-permute-start | bytes 221192 | tf_op jit(solution)/shard_map/ppermute | solution.py:509
  57.1 19.3 %copy-start.12 = (f32[24]{0:T(128)S(1)}, f32[24]{0:T(128)}, u32[]{:S(2)}) copy-start(f32[24]{0:T(128)} %param.21) | copy-start | bytes 292
  57.1 19.4 %copy-start.10 = (f32[10,16,128]{2,1,0:T(8,128)S(1)}, f32[10,16,128]{2,1,0:T(8,128)}, u32[]{:S(2)}) copy-start(f32[10,16,128]{2,1,0:T(8,128)} %base_volume.1) | copy-start | bytes 245764
  57.1 19.4 %copy-start.11 = (f32[9,16,128]{2,1,0:T(8,128)S(1)}, f32[9,16,128]{2,1,0:T(8,128)}, u32[]{:S(2)}) copy-start(f32[9,16,128]{2,1,0:T(8,128)} %diffusivity.1) | copy-start | bytes 221188
  100.3 15.4 %collective-permute-start.4 = (f32[10,2,24,128]{3,2,1,0:T(8,128)S(1)}, f32[10,2,24,128]{3,2,1,0:T(8,128)S(1)}, u32[]{:S(2)}, u32[]{:S(2)}) collective-permute-start(f32[10,2,24,128]{3,2,1,0:T(8,128)S(1)} %get-tuple-element.27), channel_id=1, source_target_pairs={{0,8},{8,16},{16,24},{24,32},{32,40},{40,48},{48,56},{56,64},{64,7... | collective-permute-start | bytes 737288 | tf_op jit(solution)/shard_map/ppermute | solution.py:509
  102.2 13.5 %collective-permute-start.5 = (f32[10,2,24,128]{3,2,1,0:T(8,128)S(1)}, f32[10,2,24,128]{3,2,1,0:T(8,128)S(1)}, u32[]{:S(2)}, u32[]{:S(2)}) collective-permute-start(f32[10,2,24,128]{3,2,1,0:T(8,128)S(1)} %get-tuple-element.28), channel_id=1, source_target_pairs={{8,0},{16,8},{24,16},{32,24},{40,32},{48,40},{56,48},{64,56},{72,6... | collective-permute-start | bytes 737288 | tf_op jit(solution)/shard_map/ppermute | solution.py:514
  108.3 4.3 %collective-permute-start.7 = (f32[5,24,128]{2,1,0:T(8,128)S(1)}, f32[5,24,128]{2,1,0:T(8,128)S(1)}, u32[]{:S(2)}, u32[]{:S(2)}) collective-permute-start(f32[5,24,128]{2,1,0:T(8,128)S(1)} %get-tuple-element.29.edges), channel_id=1, source_target_pairs={{1,0},{2,1},{3,2},{4,3},{5,4},{6,5},{7,6},{9,8},{10,9},{11,10},{12... | collective-permute-start | bytes 184328 | tf_op jit(solution)/shard_map/ppermute | solution.py:514
  110.2 5.5 %collective-permute-start.6 = (f32[5,24,128]{2,1,0:T(8,128)S(1)}, f32[5,24,128]{2,1,0:T(8,128)S(1)}, u32[]{:S(2)}, u32[]{:S(2)}) collective-permute-start(f32[5,24,128]{2,1,0:T(8,128)S(1)} %get-tuple-element.29.edges), channel_id=1, source_target_pairs={{0,1},{1,2},{2,3},{3,4},{4,5},{5,6},{6,7},{8,9},{9,10},{10,11},{11... | collective-permute-start | bytes 184328 | tf_op jit(solution)/shard_map/ppermute | solution.py:509
  135.1 15.4 %collective-permute-start.8 = (f32[10,2,24,128]{3,2,1,0:T(8,128)S(1)}, f32[10,2,24,128]{3,2,1,0:T(8,128)S(1)}, u32[]{:S(2)}, u32[]{:S(2)}) collective-permute-start(f32[10,2,24,128]{3,2,1,0:T(8,128)S(1)} %get-tuple-element.32), channel_id=1, source_target_pairs={{0,8},{8,16},{16,24},{24,32},{32,40},{40,48},{48,56},{56,64},{64,7... | collective-permute-start | bytes 737288 | tf_op jit(solution)/shard_map/ppermute | solution.py:509
  137.0 13.5 %collective-permute-start.9 = (f32[10,2,24,128]{3,2,1,0:T(8,128)S(1)}, f32[10,2,24,128]{3,2,1,0:T(8,128)S(1)}, u32[]{:S(2)}, u32[]{:S(2)}) collective-permute-start(f32[10,2,24,128]{3,2,1,0:T(8,128)S(1)} %get-tuple-element.33), channel_id=1, source_target_pairs={{8,0},{16,8},{24,16},{32,24},{40,32},{48,40},{56,48},{64,56},{72,6... | collective-permute-start | bytes 737288 | tf_op jit(solution)/shard_map/ppermute | solution.py:514
  143.0 4.3 %collective-permute-start.11 = (f32[5,24,128]{2,1,0:T(8,128)S(1)}, f32[5,24,128]{2,1,0:T(8,128)S(1)}, u32[]{:S(2)}, u32[]{:S(2)}) collective-permute-start(f32[5,24,128]{2,1,0:T(8,128)S(1)} %get-tuple-element.34.edges), channel_id=1, source_target_pairs={{1,0},{2,1},{3,2},{4,3},{5,4},{6,5},{7,6},{9,8},{10,9},{11,10},{12... | collective-permute-start | bytes 184328 | tf_op jit(solution)/shard_map/ppermute | solution.py:514
  145.0 5.5 %collective-permute-start.10 = (f32[5,24,128]{2,1,0:T(8,128)S(1)}, f32[5,24,128]{2,1,0:T(8,128)S(1)}, u32[]{:S(2)}, u32[]{:S(2)}) collective-permute-start(f32[5,24,128]{2,1,0:T(8,128)S(1)} %get-tuple-element.34.edges), channel_id=1, source_target_pairs={{0,1},{1,2},{2,3},{3,4},{4,5},{5,6},{6,7},{8,9},{9,10},{10,11},{11... | collective-permute-start | bytes 184328 | tf_op jit(solution)/shard_map/ppermute | solution.py:509
  (3 other events, 3.1 us)
where the time goes:
time: 172 us
  Pallas kernels  88.5 us (51%)
  starting transfers between devices  47.3 us (28%)
  waiting for transfers between devices  27.2 us (16%)
  local copies, waits for them, and re-layouts  8.04 us (5%)
    pallas_call x2, Pallas kernels, later_step(): pl.pallas_call(functools.partial(later_step_kernel, final), in_specs=[VME...  40.3 us
    pallas_call x1, Pallas kernels, first_step(): pl.pallas_call(first_step_kernel, in_specs=[VMEM] * 8, out_specs=[VMEM] *...  23.8 us
    ppermute x6, starting transfers between devices, to_previous(): return lax.ppermute(values, axis, [(i + 1, i) for i in range(size - 1)])  22.4 us
    ppermute x6, waiting for transfers between devices, to_next(): return lax.ppermute(values, axis, [(i, i + 1) for i in range(size - 1)])  19.7 us
    pallas_call x1, Pallas kernels, first_divergence(): pl.pallas_call(first_divergence_kernel, in_specs=[VMEM] * 8, out_specs=VM...  17.9 us
    ppermute x6, starting transfers between devices, to_next(): return lax.ppermute(values, axis, [(i, i + 1) for i in range(size - 1)])  14.4 us
    all_to_all x1, starting transfers between devices, local(): lax.all_to_all(sent.reshape(owners, 1, -1), ('gx', 'gy'), split_axis=0, c...  10.5 us
    unnamed x28, local copies, waits for them, and re-layouts  7.83 us
  transfers between devices with their start and end apart: 13, of which 6 were waited for; matrix products, arithmetic and copies ran while one was open for 0% of the time, Pallas kernels for 12%

commit v1 on v0

v1 whole, which is shorter than its diff:
```python
import functools

import jax
import jax.numpy as jnp
from jax import lax
from jax.experimental import pallas as pl
from jax.experimental.pallas import tpu as pltpu
from jax.sharding import PartitionSpec as P

SUBSTEPS = 3
STEP = 1.0 / SUBSTEPS
VMEM_BYTES = 48 * 1024 * 1024
PACK_VMEM_BYTES = 62 * 1024 * 1024
F32 = jnp.float32
BF16 = jnp.bfloat16

VMEM = pl.BlockSpec(memory_space=pltpu.VMEM)
SMEM = pl.BlockSpec(memory_space=pltpu.SMEM)


def half_minmod(left, right):
    return jnp.minimum(
        jnp.maximum(left, jnp.minimum(right, 0.0)), jnp.maximum(right, 0.0)
    )


def roll(values, shift):
    return pltpu.roll(values, shift % values.shape[-1], values.ndim - 1)


def lanes(shape):
    return lax.broadcasted_iota(jnp.int32, shape, len(shape) - 1)


def pack_kernel(volume, discharge, wet, segment, out):
    layers = volume.shape[0]
    rows = 2 * layers + 1
    groups = wet.shape[0]
    missing = 16 * 128
    label = jnp.where(wet[...] == 1, segment[...], missing).astype(F32)
    for k in range(groups):
        out[k * rows : k * rows + layers, :] = volume[:, k * 128 : (k + 1) * 128]
        out[k * rows + layers : k * rows + 2 * layers, :] = discharge[:, k * 128 : (k + 1) * 128]
        out[k * rows + 2 * layers : (k + 1) * rows, :] = label[k : k + 1, :]


def pack_slots(volume, discharge, wet, segment):
    layers, fine = volume.shape
    groups = fine // 128
    rows = 2 * layers + 1
    step = 32 if groups % 32 == 0 else 8
    return pl.pallas_call(
        pack_kernel,
        grid=(groups // step,),
        in_specs=[
            pl.BlockSpec((layers, step * 128), lambda i: (0, i)),
            pl.BlockSpec((layers, step * 128), lambda i: (0, i)),
            pl.BlockSpec((step, 128), lambda i: (i, 0)),
            pl.BlockSpec((step, 128), lambda i: (i, 0)),
        ],
        out_specs=pl.BlockSpec((step * rows, 128), lambda i: (i, 0)),
        out_shape=jax.ShapeDtypeStruct((groups * rows, 128), F32),
        compiler_params=pltpu.CompilerParams(vmem_limit_bytes=PACK_VMEM_BYTES),
        cost_estimate=pl.CostEstimate(flops=0, bytes_accessed=8 * 10**6, transcendentals=0),
        name="pack_slots",
    )(volume, discharge, wet.reshape(groups, 128), segment.reshape(groups, 128))


def places(shape):
    return lanes(shape) % 8


def pack_layer(rows_of_layer):
    packed = None
    for i, values in enumerate(rows_of_layer):
        moved = roll(values, 8 * i + 4)
        packed = moved if i == 0 else jnp.where(lanes(moved.shape) // 8 == i, moved, packed)
    return packed


def narrow(edges, low, high):
    even, odd = (edges[low], edges[high])
    place = places(even.shape)
    return jnp.where((place >= 2) & (place < 6), even, roll(odd, 4))


def widen(sent, layer):
    tile = sent[layer // 2]
    return tile if layer % 2 == 0 else roll(tile, -4)


def edge_divergence(own, left, right, flows_own, flows_left):
    place = places(own.shape)

    def divergence(four, flows):
        step = 0.5 * (roll(four, -1) - four)
        slope = half_minmod(roll(step, 1), step)
        flux = jnp.maximum(flows, 0.0) * (four + slope) + jnp.minimum(flows, 0.0) * roll(
            four - slope, -1
        )
        return flux - roll(flux, 1)

    first = divergence(
        jnp.where(place >= 4, own, left),
        jnp.where(places(flows_own.shape) >= 4, flows_own, flows_left),
    )
    last = divergence(jnp.where(place < 4, own, right), flows_own)
    return jnp.where(place < 4, last, first)


def edge_pass(edges, left, right, flow_edges, flow_left, fixes):
    layers = fixes.shape[0]
    flows_sent = layers // 2
    for l in range(layers):
        flow = flow_edges[layers, l : l + 1, :]
        other = flow_left[flows_sent, l // 2 : l // 2 + 1, :]
        fixes[l] = edge_divergence(
            edges[l],
            widen(left, l),
            widen(right, l),
            flow,
            other if l % 2 == 0 else roll(other, -4),
        )


def at_edges(shape):
    lane = lanes(shape)
    return (lane < 2) | (lane >= 126)


def emit_sent(edges, sent, with_flows):
    layers = edges.shape[0] - (1 if with_flows else 0)
    for t in range(layers // 2):
        sent[t] = narrow(edges, 2 * t, 2 * t + 1)
        if with_flows:
            even = edges[layers, 2 * t : 2 * t + 1, :]
            odd = edges[layers, 2 * t + 1 : 2 * t + 2, :]
            place = places(even.shape)
            sent[layers // 2, t : t + 1, :] = jnp.where(
                (place >= 2) & (place < 6), even, roll(odd, 4)
            )


def start_kernel(
    last, conc, flow_x, flow_y, wet_x, wet_y, state, low_x, high_x, edges, sent, qx, qy
):
    layers, rows = flow_x.shape[0], flow_x.shape[1]
    subs = conc.shape[0] // (layers * rows)
    row = lax.broadcasted_iota(jnp.int32, flow_x.shape, 1)
    col = lax.broadcasted_iota(jnp.int32, flow_x.shape, 2)
    keep_x = jnp.where((row == rows - 1) & (last[0] == 1), 0.0, 1.0)
    keep_y = jnp.where((col == 127) & (last[1] == 1), 0.0, 1.0)
    qx[...] = flow_x[...] * wet_x[...].astype(F32) * keep_x
    qy[...] = flow_y[...] * wet_y[...].astype(F32) * keep_y
    high_x[layers] = jnp.zeros_like(high_x[layers])
    edges[layers] = jnp.zeros_like(edges[layers])
    sent[layers // 2] = jnp.zeros_like(sent[layers // 2])

    def layer(l, carry):
        values = []
        for i in range(rows):
            c = conc[pl.ds(l * rows + i, subs, stride=layers * rows), :]
            values.append(c)
            state[l, i] = c
            if i < 2:
                low_x[l, i] = c
            if i >= rows - 2:
                high_x[l, i - rows + 2] = c
        edges[l] = pack_layer(values)
        edges[layers, pl.ds(l, 1), :] = pack_layer([qy[l, i : i + 1, :] for i in range(rows)])
        high_x[layers, 0, pl.ds(l, 1), :] = qx[l, rows - 1 :, :]
        return carry

    lax.fori_loop(0, layers, layer, 0)
    emit_sent(edges, sent, True)


def start(last, conc, flow_x, flow_y, wet_x, wet_y):
    subs, layers, rows, cols = conc.shape
    flows = jax.ShapeDtypeStruct(flow_x.shape, F32)
    return pl.pallas_call(
        start_kernel,
        in_specs=[SMEM] + [VMEM] * 5,
        out_specs=[VMEM] * 7,
        out_shape=[
            jax.ShapeDtypeStruct((layers, rows, subs, cols), F32),
            jax.ShapeDtypeStruct((layers, 2, subs, cols), F32),
            jax.ShapeDtypeStruct((layers + 1, 2, subs, cols), F32),
            jax.ShapeDtypeStruct((layers + 1, subs, cols), F32),
            jax.ShapeDtypeStruct((layers // 2 + 1, subs, cols), F32),
            flows,
            flows,
        ],
        compiler_params=pltpu.CompilerParams(vmem_limit_bytes=VMEM_BYTES),
        cost_estimate=pl.CostEstimate(flops=10**6, bytes_accessed=8 * 10**6, transcendentals=0),
        name="start_state",
    )(last, conc.reshape(subs * layers * rows, cols), flow_x, flow_y, wet_x, wet_y)


def y_divergence(c, flows):
    before = [roll(v, 1) for v in c]
    after = [roll(v, -1) for v in c]
    slope = [0.5 * half_minmod(v - b, a - v) for v, b, a in zip(c, before, after)]
    right = [roll(v - s, -1) for v, s in zip(c, slope)]
    flux = [
        jnp.maximum(q, 0.0) * (v + s) + jnp.minimum(q, 0.0) * r
        for q, v, s, r in zip(flows, c, slope, right)
    ]
    return [f - roll(f, 1) for f in flux]


def x_faces(get, flow, first, last):
    here = get(first)
    step = 0.5 * (here - get(first - 1))
    fluxes = []
    left = None
    for i in range(first, last + 2):
        after = get(i + 1)
        step_after = 0.5 * (after - here)
        slope = half_minmod(step, step_after)
        if i > first:
            q = flow(i - 1)
            fluxes.append(
                jnp.maximum(q, 0.0) * left + jnp.minimum(q, 0.0) * (here - slope)
            )
        left = here + slope
        here, step = (after, step_after)
    return fluxes


def x_rows(state, west, east, l, rows):
    def get(i):
        if i < 0:
            return west[l, i + 2]
        if i >= rows:
            return east[l, i - rows]
        return state[l, i]

    return get


def x_flows(qx, qx_west, l):
    return lambda i: qx_west if i < 0 else qx[l, i : i + 1, :]


def first_divergence_kernel(state, qx, qy, div):
    layers, rows = qx.shape[0], qx.shape[1]
    edge = at_edges(state.shape[2:])

    def layer(l, carry):
        c = [state[l, i] for i in range(rows)]
        parts = y_divergence(c, [qy[l, i : i + 1, :] for i in range(rows)])
        faces = x_faces(x_rows(state, None, None, l, rows), x_flows(qx, None, l), 1, rows - 3)
        for i in range(rows):
            value = jnp.where(edge, 0.0, parts[i])
            if 2 <= i < rows - 2:
                value = value + (faces[i - 1] - faces[i - 2])
            div[l, i] = value
        return carry

    lax.fori_loop(0, layers, layer, 0)


def first_divergence(state, qx, qy):
    return pl.pallas_call(
        first_divergence_kernel,
        in_specs=[VMEM] * 3,
        out_specs=VMEM,
        out_shape=jax.ShapeDtypeStruct(state.shape, F32),
        compiler_params=pltpu.CompilerParams(vmem_limit_bytes=VMEM_BYTES),
        cost_estimate=pl.CostEstimate(flops=2 * 10**7, bytes_accessed=10**7, transcendentals=0),
        name="first_divergence",
    )(state, qx, qy)


def explicit_value(c, div, rates, rates_before, inflow, renewal, scale):
    carried = pltpu.roll(c, 1, 0)
    return (
        c
        + ((renewal * (inflow - c) - scale * div) + (rates_before * carried - rates * c))
    )


def solve(star, coef, emit):
    layers, rows = star.shape[0], star.shape[1]
    batch = 4

    def some(b, carry):
        ids = [b * batch + j for j in range(batch)]

        def get(which, l, i):
            return coef[which, l, pl.ds(i, 1), :]

        value = [star[0, i] for i in ids]
        for l in range(1, layers):
            value = [star[l, i] - get(0, l, i) * v for i, v in zip(ids, value)]
            for i, v in zip(ids, value):
                star[l, i] = v
        value = [v * get(1, layers - 1, i) for i, v in zip(ids, value)]
        for i, v in zip(ids, value):
            emit(layers - 1, i, v)
        for l in range(layers - 2, -1, -1):
            value = [
                (star[l, i] + get(2, l, i) * v) * get(1, l, i) for i, v in zip(ids, value)
            ]
            for i, v in zip(ids, value):
                emit(l, i, v)
        return carry

    lax.fori_loop(0, rows // batch, some, 0)


def emit_edges(state, low_x, high_x, edges, sent):
    layers, rows = state.shape[0], state.shape[1]
    low_x[...] = state[:, :2]
    high_x[...] = state[:, rows - 2 :]

    def layer(l, carry):
        edges[l] = pack_layer([state[l, i] for i in range(rows)])
        return carry

    lax.fori_loop(0, layers, layer, 0)
    emit_sent(edges, sent, False)


def spread_slots(slots, chunk, terms, spread, hot):
    rows = 21
    halves = spread.shape[1] // 128
    sub8 = lax.broadcasted_iota(jnp.int32, (8, 128), 0)
    column = lax.broadcasted_iota(jnp.int32, (128, 128), 0).astype(F32).astype(BF16)
    base = pl.multiple_of(chunk * (halves * rows), 8)
    values = slots[pl.ds(base, halves * rows), :]
    high = values.astype(BF16).astype(F32)
    terms[0] = high
    terms[1] = values - high
    for j in range(halves):
        to = slice(j * 128, (j + 1) * 128)

        def term(which, ch):
            at = j * rows + ch
            return terms[which, at : at + 1, :]

        label = (term(0, 20) + term(1, 20)).astype(jnp.int32)
        mask = jnp.where(jnp.broadcast_to((label >> 7) & 7, (8, 128)) == sub8, 1.0, 0.0)
        mask = jnp.concatenate([mask, mask], axis=0).astype(BF16)
        for ch in range(20):
            both = [jnp.broadcast_to(term(which, ch), (8, 128)) for which in range(2)]
            both = jnp.concatenate(both, axis=0).astype(BF16)
            spread[ch * 16 : (ch + 1) * 16, to] = both * mask
        place = jnp.broadcast_to((label & 127).astype(F32), (16, 128)).astype(BF16)
        half = label >> 10
        hits = [
            jnp.broadcast_to(jnp.where(half == h, 1.0, 0.0), (16, 128)).astype(BF16)
            for h in range(2)
        ]
        zero = jnp.zeros((16, 128), BF16)
        for g in range(8):
            same = column[g * 16 : (g + 1) * 16] == place
            for h in range(2):
                at = h * 128 + g * 16
                hot[at : at + 16, to] = jnp.where(same, hits[h], zero)


def aggregate(slots, terms, spread, hot, total):
    total[...] = jnp.zeros_like(total)

    def chunk(i, carry):
        spread_slots(slots, i, terms, spread, hot)
        total[...] += lax.dot_general(
            spread[...], hot[...], (((1,), (1,)), ((), ())), preferred_element_type=F32
        )
        return carry

    lax.fori_loop(0, slots.shape[0] // terms.shape[1], chunk, 0)


def factorize(total, base_volume, diffusivity, coef):
    layers = base_volume.shape[0]
    uppers, downs = ([], [])
    for l in range(layers):
        parts = []
        for ch in (l, layers + l):
            parts.append(
                jnp.concatenate(
                    [
                        total[ch * 16 : ch * 16 + 8, h * 128 : (h + 1) * 128]
                        + total[ch * 16 + 8 : ch * 16 + 16, h * 128 : (h + 1) * 128]
                        for h in range(2)
                    ],
                    axis=0,
                )
            )
        scale = STEP / (base_volume[l] + parts[0])
        coef[3, l] = scale
        coef[4, l] = scale * parts[1]
        uppers.append(scale * diffusivity[l] if l < layers - 1 else jnp.zeros_like(scale))
        downs.append(scale * diffusivity[l - 1] if l > 0 else jnp.zeros_like(scale))
    pivot = 1.0 + uppers[0]
    coef[0, 0] = jnp.zeros_like(pivot)
    for l in range(layers):
        inverse = 1.0 / pivot
        coef[1, l] = inverse
        coef[2, l] = uppers[l]
        if l + 1 < layers:
            factor = -downs[l + 1] * inverse
            coef[0, l + 1] = factor
            pivot = 1.0 + uppers[l + 1] + downs[l + 1] + factor * uppers[l]


def first_step_kernel(
    slots,
    base_volume,
    diffusivity,
    state,
    div,
    west,
    east,
    edges_before,
    left,
    right,
    qx,
    rates,
    rates_before,
    inflow,
    new,
    low_x,
    high_x,
    edges,
    sent,
    coef,
    terms,
    spread,
    hot,
    total,
    fixes,
    star,
):
    layers, rows = base_volume.shape[0], base_volume.shape[1]
    aggregate(slots, terms, spread, hot, total)
    factorize(total, base_volume, diffusivity, coef)
    edge_pass(edges_before, left, right, edges_before, left, fixes)
    edge = at_edges(state.shape[2:])

    def explicit(l, carry):
        get = x_rows(state, west, east, l, rows)
        flow = x_flows(qx, west[layers, 0, pl.ds(l, 1), :], l)
        low = x_faces(get, flow, -1, 1)
        high = x_faces(get, flow, rows - 3, rows - 1)
        fix = [roll(fixes[l], 124 - 8 * i) for i in range(rows)]
        for i in range(rows):
            value = div[l, i] + jnp.where(edge, fix[i], 0.0)
            if i < 2:
                value = value + (low[i + 1] - low[i])
            if i >= rows - 2:
                j = i - rows + 3
                value = value + (high[j] - high[j - 1])
            star[l, i] = explicit_value(
                state[l, i],
                value,
                rates[...],
                rates_before[...],
                inflow[...],
                coef[4, l, i : i + 1, :],
                coef[3, l, i : i + 1, :],
            )
        return carry

    lax.fori_loop(0, layers, explicit, 0)

    def emit(l, i, value):
        new[l, i] = value

    solve(star, coef, emit)
    emit_edges(new, low_x, high_x, edges, sent)


def state_shapes(shape):
    layers, rows, subs, cols = shape
    return [
        jax.ShapeDtypeStruct(shape, F32),
        jax.ShapeDtypeStruct((layers, 2, subs, cols), F32),
        jax.ShapeDtypeStruct((layers, 2, subs, cols), F32),
        jax.ShapeDtypeStruct((layers, subs, cols), F32),
        jax.ShapeDtypeStruct((layers // 2, subs, cols), F32),
    ]


def first_step(slots, base_volume, diffusivity, state, *args):
    layers, rows, subs, cols = state.shape
    depth = min(2048, slots.shape[0] // 21 * 128)
    return pl.pallas_call(
        first_step_kernel,
        in_specs=[VMEM] * 14,
        out_specs=[VMEM] * 6,
        out_shape=state_shapes(state.shape)
        + [jax.ShapeDtypeStruct((5, layers, rows, cols), F32)],
        scratch_shapes=[
            pltpu.VMEM((2, depth // 128 * 21, 128), F32),
            pltpu.VMEM((2 * layers * 16, depth), BF16),
            pltpu.VMEM((256, depth), BF16),
            pltpu.VMEM((2 * layers * 16, 256), F32),
            pltpu.VMEM((layers, subs, cols), F32),
            pltpu.VMEM(state.shape, F32),
        ],
        compiler_params=pltpu.CompilerParams(vmem_limit_bytes=VMEM_BYTES),
        cost_estimate=pl.CostEstimate(flops=10**9, bytes_accessed=10**7, transcendentals=0),
        name="aggregate_and_first_step",
    )(slots, base_volume, diffusivity, state, *args)


def later_step_kernel(
    final,
    state,
    west,
    east,
    edges_before,
    left,
    right,
    flow_west,
    flow_edges,
    flow_left,
    qx,
    qy,
    coef,
    rates,
    rates_before,
    inflow,
    *refs,
):
    layers, rows = qx.shape[0], qx.shape[1]
    if final:
        out, fixes, star = refs
        subs = out.shape[0] // (layers * rows)
    else:
        new, low_x, high_x, edges, sent, fixes, star = refs
    edge_pass(edges_before, left, right, flow_edges, flow_left, fixes)
    edge = at_edges(state.shape[2:])

    def layer(l, carry):
        c = [state[l, i] for i in range(rows)]
        fix = [roll(fixes[l], 124 - 8 * i) for i in range(rows)]
        parts = y_divergence(c, [qy[l, i : i + 1, :] for i in range(rows)])
        parts = [jnp.where(edge, f, p) for f, p in zip(fix, parts)]
        flow = x_flows(qx, flow_west[layers, 0, pl.ds(l, 1), :], l)
        faces = x_faces(x_rows(state, west, east, l, rows), flow, -1, rows - 1)
        for i in range(rows):
            star[l, i] = explicit_value(
                state[l, i],
                parts[i] + (faces[i + 1] - faces[i]),
                rates[...],
                rates_before[...],
                inflow[...],
                coef[4, l, i : i + 1, :],
                coef[3, l, i : i + 1, :],
            )
        return carry

    lax.fori_loop(0, layers, layer, 0)

    def emit(l, i, value):
        if final:
            out[pl.ds(l * rows + i, subs, stride=layers * rows), :] = value
        else:
            new[l, i] = value

    solve(star, coef, emit)
    if not final:
        emit_edges(new, low_x, high_x, edges, sent)


def later_step(final, state, *args):
    layers, rows, subs, cols = state.shape
    if final:
        shapes = jax.ShapeDtypeStruct((subs * layers * rows, cols), F32)
        specs = VMEM
    else:
        shapes = state_shapes(state.shape)
        specs = [VMEM] * 5
    return pl.pallas_call(
        functools.partial(later_step_kernel, final),
        in_specs=[VMEM] * 15,
        out_specs=specs,
        out_shape=shapes,
        scratch_shapes=[pltpu.VMEM((layers, subs, cols), F32), pltpu.VMEM(state.shape, F32)],
        compiler_params=pltpu.CompilerParams(vmem_limit_bytes=VMEM_BYTES),
        cost_estimate=pl.CostEstimate(flops=3 * 10**7, bytes_accessed=10**7, transcendentals=0),
        name="last_step" if final else "middle_step",
    )(state, *args)


def to_next(values, axis):
    size = lax.axis_size(axis)
    return lax.ppermute(values, axis, [(i, i + 1) for i in range(size - 1)])


def to_previous(values, axis):
    size = lax.axis_size(axis)
    return lax.ppermute(values, axis, [(i + 1, i) for i in range(size - 1)])


def exchange(low_x, high_x, sent):
    west = to_next(high_x, "gx")
    east = to_previous(low_x, "gx")
    left = to_next(sent, "gy")
    right = to_previous(sent, "gy")
    return (west, east, left, right)


def local(
    concentration,
    base_volume,
    flow_x,
    flow_y,
    face_wet_x,
    face_wet_y,
    diffusivity,
    decay_rates,
    inflow,
    fine_volume,
    fine_discharge,
    cell_wet,
    seg_local,
):
    subs, layers, rows, cols = concentration.shape
    size_x, size_y = (lax.axis_size("gx"), lax.axis_size("gy"))
    owners = size_x * size_y
    slots = pack_slots(fine_volume, fine_discharge, cell_wet, seg_local)
    arrived = lax.all_to_all(
        slots.reshape(owners, 1, -1), ("gx", "gy"), split_axis=0, concat_axis=0, tiled=True
    ).reshape(slots.shape)

    last = jnp.stack(
        [
            (lax.axis_index("gx") == size_x - 1).astype(jnp.int32),
            (lax.axis_index("gy") == size_y - 1).astype(jnp.int32),
        ]
    )
    rates = jnp.concatenate([jnp.zeros((1,), F32), decay_rates]) * STEP
    rates_before = jnp.concatenate([jnp.zeros((1,), F32), rates[:-1]])
    rates, rates_before, inflow = (
        jnp.broadcast_to(v[:, None], (subs, cols)) for v in (rates, rates_before, inflow)
    )
    state, low_x, high_x, edges, sent, qx, qy = start(
        last, concentration, flow_x, flow_y, face_wet_x, face_wet_y
    )
    west, east, left, right = exchange(low_x, high_x, sent)
    flow_west, flow_edges, flow_left = (west, edges, left)
    div = first_divergence(state, qx, qy)
    constants = (rates, rates_before, inflow)
    state, low_x, high_x, edges, sent, coef = first_step(
        arrived, base_volume, diffusivity, state, div, west, east, edges, left, right, qx, *constants
    )
    for step in range(1, SUBSTEPS):
        final = step == SUBSTEPS - 1
        west, east, left, right = exchange(low_x, high_x, sent)
        flows = (flow_west, flow_edges, flow_left, qx, qy, coef)
        result = later_step(final, state, west, east, edges, left, right, *flows, *constants)
        if not final:
            state, low_x, high_x, edges, sent = result
    return result.reshape(concentration.shape)


def solution(mesh):
    fine = P(None, ("gx", "gy"))
    block = P(None, "gx", "gy")
    return jax.shard_map(
        local,
        mesh=mesh,
        in_specs=(
            P(None, None, "gx", "gy"),
            block,
            block,
            block,
            block,
            block,
            block,
            P(),
            P(),
            fine,
            fine,
            P(("gx", "gy")),
            P(("gx", "gy")),
        ),
        out_specs=P(None, None, "gx", "gy"),
        check_vma=False,
    )
```

time: 172 us -> 124 us (0.72)
  Pallas kernels: 88.5 us -> 48.3 us
  waiting for transfers between devices: 27.2 us -> 23.2 us
  local copies, waits for them, and re-layouts: 8.04 us -> 4.32 us
    pallas_call x2, Pallas kernels: 40.3 us -> 17 us  [later_step(): pl.pallas_call(functools.partial(later_step_kernel, final), in_specs=[VME...]
    pallas_call x2, Pallas kernels: 41.7 us -> 22.5 us  [the longest x1 19.3 us: first_step(): pl.pallas_call(first_step_kernel, in_specs=[VMEM] * 14, out_specs=[VMEM]...]
    unnamed x28 -> x22, local copies, waits for them, and re-layouts: 7.83 us -> 4.12 us
    pallas_call x1, Pallas kernels: 3.44 us -> 6.3 us  [pack_slots(): pl.pallas_call(pack_kernel, grid=(groups // step,), in_specs=[pl.BlockSpe...]
    ppermute x6, waiting for transfers between devices: 7.47 us -> 5.11 us  [to_previous(): return lax.ppermute(values, axis, [(i + 1, i) for i in range(size - 1)])]
  transfers between devices with their start and end apart: 13 -> 13, of which waited for: 6 -> 5; matrix products, arithmetic and copies ran while one was open for 0% -> 0% of each run, Pallas kernels for 12% -> 5%
where the time goes in v1:
time: 124 us
  Pallas kernels  48.3 us (39%)
  starting transfers between devices  47.3 us (38%)
  waiting for transfers between devices  23.2 us (19%)
  local copies, waits for them, and re-layouts  4.32 us (3%)
    ppermute x6, starting transfers between devices, to_previous(): return lax.ppermute(values, axis, [(i + 1, i) for i in range(size - 1)])  22.4 us
    pallas_call x1, Pallas kernels, first_step(): pl.pallas_call(first_step_kernel, in_specs=[VMEM] * 14, out_specs=[VMEM]...  19.3 us
    ppermute x6, waiting for transfers between devices, to_next(): return lax.ppermute(values, axis, [(i, i + 1) for i in range(size - 1)])  18.1 us
    pallas_call x2, Pallas kernels, later_step(): pl.pallas_call(functools.partial(later_step_kernel, final), in_specs=[VME...  17 us
    ppermute x6, starting transfers between devices, to_next(): return lax.ppermute(values, axis, [(i, i + 1) for i in range(size - 1)])  14.4 us
    all_to_all x1, starting transfers between devices, local(): lax.all_to_all(slots.reshape(owners, 1, -1), ('gx', 'gy'), split_axis=0,...  10.5 us
    pallas_call x1, Pallas kernels, pack_slots(): pl.pallas_call(pack_kernel, grid=(groups // step,), in_specs=[pl.BlockSpe...  6.3 us
    ppermute x6, waiting for transfers between devices, to_previous(): return lax.ppermute(values, axis, [(i + 1, i) for i in range(size - 1)])  5.11 us
  transfers between devices with their start and end apart: 13, of which 5 were waited for; matrix products, arithmetic and copies ran while one was open for 0% of the time, Pallas kernels for 5%

profile of v1, /device:TPU:56, one launch (start us, length us, event | category | flops | bytes accessed | tf_op | source)
XLA Modules:
  0.0 123.6 jit_solution(13236260864808496377)
XLA Ops:
  0.0 6.3 %pack_slots.1 = f32[5376,128]{1,0:T(8,128)} custom-call(f32[10,32768]{1,0:T(8,128)} %volume.1, f32[10,32768]{1,0:T(8,128)} %discharge.1, s32[256,128]{1,0:T(8,128)} %bitcast.11, s32[256,128]{1,0:T(8,128)} %bitcast.12), custom_call_target="tpu_custom_call" | custom-call | bytes 8000000 | tf_op jit(solution)/shard_map/pack_slots/pallas_call | solution.py:52
  6.3 10.5 %all-to-all-start = ((f32[128,1,5376]{2,1,0:T(1,128)}), f32[128,1,5376]{2,1,0:T(1,128)}, u32[]{:S(2)}, u32[]{:S(2)}) async-start(f32[128,1,5376]{2,1,0:T(1,128)} %bitcast.10), calls=%async_computation | async-start | bytes 5505024 | tf_op jit(solution)/shard_map/all_to_all | solution.py:628
  18.5 2.5 %start_state.1 = (f32[10,16,24,128]{3,2,1,0:T(8,128)S(1)}, f32[10,2,24,128]{3,2,1,0:T(8,128)S(1)}, f32[11,2,24,128]{3,2,1,0:T(8,128)S(1)}, f32[11,24,128]{2,1,0:...) custom-call(s32[2]{0:T(128)S(1)} %add_convert_fusion.last, ...), custom_call_target="tpu_custom_call" | custom-call | flops 1000000 | bytes 8000000 | tf_op jit(solution)/shard_map/start_state/pallas_call | solution.py:181
  21.0 3.4 %collective-permute-start = (f32[11,2,24,128]{3,2,1,0:T(8,128)S(1)}, f32[11,2,24,128]{3,2,1,0:T(8,128)S(1)}, u32[]{:S(2)}, u32[]{:S(2)}) collective-permute-start(f32[11,2,24,128]{3,2,1,0:T(8,128)S(1)} %get-tuple-element.26), channel_id=1, source_target_pairs={{0,8},{8,16},{16,24},{24,32},{32,40},{40,48},{48,56},{56,64},{64,7... | collective-permute-start | bytes 811016 | tf_op jit(solution)/shard_map/ppermute | solution.py:593
  24.4 4.6 %collective-permute-start.1 = (f32[10,2,24,128]{3,2,1,0:T(8,128)S(1)}, f32[10,2,24,128]{3,2,1,0:T(8,128)S(1)}, u32[]{:S(2)}, u32[]{:S(2)}) collective-permute-start(f32[10,2,24,128]{3,2,1,0:T(8,128)S(1)} %get-tuple-element.27), channel_id=1, source_target_pairs={{8,0},{16,8},{24,16},{32,24},{40,32},{48,40},{56,48},{64,56},{72,6... | collective-permute-start | bytes 737288 | tf_op jit(solution)/shard_map/ppermute | solution.py:598
  29.0 1.9 %collective-permute-start.3 = (f32[6,24,128]{2,1,0:T(8,128)S(1)}, f32[6,24,128]{2,1,0:T(8,128)S(1)}, u32[]{:S(2)}, u32[]{:S(2)}) collective-permute-start(f32[6,24,128]{2,1,0:T(8,128)S(1)} %get-tuple-element.29), channel_id=1, source_target_pairs={{1,0},{2,1},{3,2},{4,3},{5,4},{6,5},{7,6},{9,8},{10,9},{11,10},{12... | collective-permute-start | bytes 221192 | tf_op jit(solution)/shard_map/ppermute | solution.py:598
  30.9 2.4 %collective-permute-start.2 = (f32[6,24,128]{2,1,0:T(8,128)S(1)}, f32[6,24,128]{2,1,0:T(8,128)S(1)}, u32[]{:S(2)}, u32[]{:S(2)}) collective-permute-start(f32[6,24,128]{2,1,0:T(8,128)S(1)} %get-tuple-element.29), channel_id=1, source_target_pairs={{0,1},{1,2},{2,3},{3,4},{4,5},{5,6},{6,7},{8,9},{9,10},{10,11},{11... | collective-permute-start | bytes 221192 | tf_op jit(solution)/shard_map/ppermute | solution.py:593
  33.4 3.2 %first_divergence.1.div = f32[10,16,24,128]{3,2,1,0:T(8,128)S(1)} custom-call(f32[10,16,24,128]{3,2,1,0:T(8,128)S(1)} %get-tuple-element.23.state, f32[10,16,128]{2,1,0:T(8,128)S(1)} %get-tuple-element.24.qx, f32[10,16,128]{2,1,0:T(8,128)S(1)} %get-tuple-element.25.qy), custom_call_target="tpu_custom_call" | custom-call | flops 20000000 | bytes 10000000 | tf_op jit(solution)/shard_map/first_divergence/pallas_call | solution.py:265
  38.0 9.9 %collective-permute-done.2.left.flow_left = f32[6,24,128]{2,1,0:T(8,128)S(1)} collective-permute-done((f32[6,24,128]{2,1,0:T(8,128)S(1)}, f32[6,24,128]{2,1,0:T(8,128)S(1)}, u32[]{:S(2)}, u32[]{:S(2)}) %collective-permute-start.2) | collective-permute-done | bytes 73760 | tf_op jit(solution)/shard_map/ppermute | solution.py:593
  47.9 5.1 %collective-permute-done.1.east = f32[10,2,24,128]{3,2,1,0:T(8,128)S(1)} collective-permute-done((f32[10,2,24,128]{3,2,1,0:T(8,128)S(1)}, f32[10,2,24,128]{3,2,1,0:T(8,128)S(1)}, u32[]{:S(2)}, u32[]{:S(2)}) %collective-permute-start.1) | collective-permute-done | bytes 245792 | tf_op jit(solution)/shard_map/ppermute | solution.py:598
  53.0 2.0 %collective-permute-done.west.flow_west = f32[11,2,24,128]{3,2,1,0:T(8,128)S(1)} collective-permute-done((f32[11,2,24,128]{3,2,1,0:T(8,128)S(1)}, f32[11,2,24,128]{3,2,1,0:T(8,128)S(1)}, u32[]{:S(2)}, u32[]{:S(2)}) %collective-permute-start) | collective-permute-done | bytes 270368 | tf_op jit(solution)/shard_map/ppermute | solution.py:593
  55.2 19.3 %aggregate_and_first_step.1 = (f32[10,16,24,128]{3,2,1,0:T(8,128)S(1)}, f32[10,2,24,128]{3,2,1,0:T(8,128)S(1)}, f32[10,2,24,128]{3,2,1,0:T(8,128)S(1)}, f32[10,2...) custom-call(f32[5376,128]{1,0:T(8,128)} %bitcast.3.slots, ...), custom_call_target="tpu_custom_call" | custom-call | flops 1000000000 | bytes 10000000 | tf_op jit(solution)/shard_map/aggregate_and_first_step/pallas_call | solution.py:491
  75.8 1.9 %collective-permute-start.4 = (f32[10,2,24,128]{3,2,1,0:T(8,128)S(1)}, f32[10,2,24,128]{3,2,1,0:T(8,128)S(1)}, u32[]{:S(2)}, u32[]{:S(2)}) collective-permute-start(f32[10,2,24,128]{3,2,1,0:T(8,128)S(1)} %get-tuple-element.31), channel_id=1, source_target_pairs={{0,8},{8,16},{16,24},{24,32},{32,40},{40,48},{48,56},{56,64},{64,7... | collective-permute-start | bytes 737288 | tf_op jit(solution)/shard_map/ppermute | solution.py:593
  77.7 6.0 %collective-permute-start.5 = (f32[10,2,24,128]{3,2,1,0:T(8,128)S(1)}, f32[10,2,24,128]{3,2,1,0:T(8,128)S(1)}, u32[]{:S(2)}, u32[]{:S(2)}) collective-permute-start(f32[10,2,24,128]{3,2,1,0:T(8,128)S(1)} %get-tuple-element.32), channel_id=1, source_target_pairs={{8,0},{16,8},{24,16},{32,24},{40,32},{48,40},{56,48},{64,56},{72,6... | collective-permute-start | bytes 737288 | tf_op jit(solution)/shard_map/ppermute | solution.py:598
  83.7 1.9 %collective-permute-start.7 = (f32[5,24,128]{2,1,0:T(8,128)S(1)}, f32[5,24,128]{2,1,0:T(8,128)S(1)}, u32[]{:S(2)}, u32[]{:S(2)}) collective-permute-start(f32[5,24,128]{2,1,0:T(8,128)S(1)} %get-tuple-element.34), channel_id=1, source_target_pairs={{1,0},{2,1},{3,2},{4,3},{5,4},{6,5},{7,6},{9,8},{10,9},{11,10},{12... | collective-permute-start | bytes 184328 | tf_op jit(solution)/shard_map/ppermute | solution.py:598
  85.6 2.4 %collective-permute-start.6 = (f32[5,24,128]{2,1,0:T(8,128)S(1)}, f32[5,24,128]{2,1,0:T(8,128)S(1)}, u32[]{:S(2)}, u32[]{:S(2)}) collective-permute-start(f32[5,24,128]{2,1,0:T(8,128)S(1)} %get-tuple-element.34), channel_id=1, source_target_pairs={{0,1},{1,2},{2,3},{3,4},{4,5},{5,6},{6,7},{8,9},{9,10},{10,11},{11... | collective-permute-start | bytes 184328 | tf_op jit(solution)/shard_map/ppermute | solution.py:593
  88.1 3.1 %collective-permute-done.6.left = f32[5,24,128]{2,1,0:T(8,128)S(1)} collective-permute-done((f32[5,24,128]{2,1,0:T(8,128)S(1)}, f32[5,24,128]{2,1,0:T(8,128)S(1)}, u32[]{:S(2)}, u32[]{:S(2)}) %collective-permute-start.6) | collective-permute-done | bytes 61472 | tf_op jit(solution)/shard_map/ppermute | solution.py:593
  91.2 8.5 %middle_step.1 = (f32[10,16,24,128]{3,2,1,0:T(8,128)S(1)}, f32[10,2,24,128]{3,2,1,0:T(8,128)S(1)}, f32[10,2,24,128]{3,2,1,0:T(8,128)S(1)}, f32[10,24,128]{2,1,0:T(8,128)S(1)}, f32[5,24,128]{2,1,0:T(8,128)S(1)}) custom-call(f32[10,16,24,128]{3,2,1,0:T(8,128)} %copy-done.2, f32[10,2,24,128]{3,2,1,0:T(8,128)S(1)} %collective-permute-done.4.west, ...), custom_call_target="tpu_custom_call" | custom-call | flops 30000000 | bytes 10000000 | tf_op jit(solution)/shard_map/middle_step/pallas_call | solution.py:579
  99.7 1.9 %collective-permute-start.8 = (f32[10,2,24,128]{3,2,1,0:T(8,128)S(1)}, f32[10,2,24,128]{3,2,1,0:T(8,128)S(1)}, u32[]{:S(2)}, u32[]{:S(2)}) collective-permute-start(f32[10,2,24,128]{3,2,1,0:T(8,128)S(1)} %get-tuple-element.37), channel_id=1, source_target_pairs={{0,8},{8,16},{16,24},{24,32},{32,40},{40,48},{48,56},{56,64},{64,7... | collective-permute-start | bytes 737288 | tf_op jit(solution)/shard_map/ppermute | solution.py:593
  101.6 6.0 %collective-permute-start.9 = (f32[10,2,24,128]{3,2,1,0:T(8,128)S(1)}, f32[10,2,24,128]{3,2,1,0:T(8,128)S(1)}, u32[]{:S(2)}, u32[]{:S(2)}) collective-permute-start(f32[10,2,24,128]{3,2,1,0:T(8,128)S(1)} %get-tuple-element.38), channel_id=1, source_target_pairs={{8,0},{16,8},{24,16},{32,24},{40,32},{48,40},{56,48},{64,56},{72,6... | collective-permute-start | bytes 737288 | tf_op jit(solution)/shard_map/ppermute | solution.py:598
  107.6 1.9 %collective-permute-start.11 = (f32[5,24,128]{2,1,0:T(8,128)S(1)}, f32[5,24,128]{2,1,0:T(8,128)S(1)}, u32[]{:S(2)}, u32[]{:S(2)}) collective-permute-start(f32[5,24,128]{2,1,0:T(8,128)S(1)} %get-tuple-element.40), channel_id=1, source_target_pairs={{1,0},{2,1},{3,2},{4,3},{5,4},{6,5},{7,6},{9,8},{10,9},{11,10},{12... | collective-permute-start | bytes 184328 | tf_op jit(solution)/shard_map/ppermute | solution.py:598
  109.6 2.4 %collective-permute-start.10 = (f32[5,24,128]{2,1,0:T(8,128)S(1)}, f32[5,24,128]{2,1,0:T(8,128)S(1)}, u32[]{:S(2)}, u32[]{:S(2)}) collective-permute-start(f32[5,24,128]{2,1,0:T(8,128)S(1)} %get-tuple-element.40), channel_id=1, source_target_pairs={{0,1},{1,2},{2,3},{3,4},{4,5},{5,6},{6,7},{8,9},{9,10},{10,11},{11... | collective-permute-start | bytes 184328 | tf_op jit(solution)/shard_map/ppermute | solution.py:593
  112.0 3.1 %collective-permute-done.10.left = f32[5,24,128]{2,1,0:T(8,128)S(1)} collective-permute-done((f32[5,24,128]{2,1,0:T(8,128)S(1)}, f32[5,24,128]{2,1,0:T(8,128)S(1)}, u32[]{:S(2)}, u32[]{:S(2)}) %collective-permute-start.10) | collective-permute-done | bytes 61472 | tf_op jit(solution)/shard_map/ppermute | solution.py:593
  115.1 8.5 %last_step.1 = f32[3840,128]{1,0:T(8,128)} custom-call(f32[10,16,24,128]{3,2,1,0:T(8,128)S(1)} %get-tuple-element.36.state, f32[10,2,24,128]{3,2,1,0:T(8,128)S(1)} %collective-permute-done.8.west, f32[10,2,24,128]{3,2,1,0:T(8,128)S(1)} %collective-permute-done.9.east, f32[10,24,128]{2,1,0:T(8,128)S(1)} %get-tuple-element.39.edges_before, ...), custom_call_target="tpu_custom_call" | custom-call | flops 30000000 | bytes 10000000 | tf_op jit(solution)/shard_map/last_step/pallas_call | solution.py:579
  (36 shorter events, 4.6 us)
Async XLA Ops:
  6.3 10.6 %copy-start.4 = (f32[10,16,128]{2,1,0:T(8,128)S(1)}, f32[10,16,128]{2,1,0:T(8,128)}, u32[]{:S(2)}) copy-start(f32[10,16,128]{2,1,0:T(8,128)} %flow_x.1) | copy-start | bytes 245764
  6.3 10.6 %copy-start.5 = (f32[10,16,128]{2,1,0:T(8,128)S(1)}, f32[10,16,128]{2,1,0:T(8,128)}, u32[]{:S(2)}) copy-start(f32[10,16,128]{2,1,0:T(8,128)} %flow_y.1) | copy-start | bytes 245764
  6.3 10.6 %copy-start.6 = (s32[10,16,128]{2,1,0:T(8,128)S(1)}, s32[10,16,128]{2,1,0:T(8,128)}, u32[]{:S(2)}) copy-start(s32[10,16,128]{2,1,0:T(8,128)} %wet_x.1) | copy-start | bytes 245764
  6.3 10.6 %copy-start.7 = (s32[10,16,128]{2,1,0:T(8,128)S(1)}, s32[10,16,128]{2,1,0:T(8,128)}, u32[]{:S(2)}) copy-start(s32[10,16,128]{2,1,0:T(8,128)} %wet_y.1) | copy-start | bytes 245764
  6.3 48.7 %all-to-all-start = ((f32[128,1,5376]{2,1,0:T(1,128)}), f32[128,1,5376]{2,1,0:T(1,128)}, u32[]{:S(2)}, u32[]{:S(2)}) async-start(f32[128,1,5376]{2,1,0:T(1,128)} %bitcast.10), calls=%async_computation | async-start | bytes 5505024 | tf_op jit(solution)/shard_map/all_to_all | solution.py:628
  16.9 1.5 %copy-start.1 = (f32[24,10,16,128]{3,2,1,0:T(8,128)S(1)}, f32[24,10,16,128]{3,2,1,0:T(8,128)}, u32[]{:S(2)}) copy-start(f32[24,10,16,128]{3,2,1,0:T(8,128)} %param.13) | copy-start | bytes 5898244
  21.0 34.0 %collective-permute-start = (f32[11,2,24,128]{3,2,1,0:T(8,128)S(1)}, f32[11,2,24,128]{3,2,1,0:T(8,128)S(1)}, u32[]{:S(2)}, u32[]{:S(2)}) collective-permute-start(f32[11,2,24,128]{3,2,1,0:T(8,128)S(1)} %get-tuple-element.26), channel_id=1, source_target_pairs={{0,8},{8,16},{16,24},{24,32},{32,40},{40,48},{48,56},{56,64},{64,7... | collective-permute-start | bytes 811016 | tf_op jit(solution)/shard_map/ppermute | solution.py:593
  24.4 28.6 %collective-permute-start.1 = (f32[10,2,24,128]{3,2,1,0:T(8,128)S(1)}, f32[10,2,24,128]{3,2,1,0:T(8,128)S(1)}, u32[]{:S(2)}, u32[]{:S(2)}) collective-permute-start(f32[10,2,24,128]{3,2,1,0:T(8,128)S(1)} %get-tuple-element.27), channel_id=1, source_target_pairs={{8,0},{16,8},{24,16},{32,24},{40,32},{48,40},{56,48},{64,56},{72,6... | collective-permute-start | bytes 737288 | tf_op jit(solution)/shard_map/ppermute | solution.py:598
  29.0 9.0 %collective-permute-start.3 = (f32[6,24,128]{2,1,0:T(8,128)S(1)}, f32[6,24,128]{2,1,0:T(8,128)S(1)}, u32[]{:S(2)}, u32[]{:S(2)}) collective-permute-start(f32[6,24,128]{2,1,0:T(8,128)S(1)} %get-tuple-element.29), channel_id=1, source_target_pairs={{1,0},{2,1},{3,2},{4,3},{5,4},{6,5},{7,6},{9,8},{10,9},{11,10},{12... | collective-permute-start | bytes 221192 | tf_op jit(solution)/shard_map/ppermute | solution.py:598
  30.9 17.0 %collective-permute-start.2 = (f32[6,24,128]{2,1,0:T(8,128)S(1)}, f32[6,24,128]{2,1,0:T(8,128)S(1)}, u32[]{:S(2)}, u32[]{:S(2)}) collective-permute-start(f32[6,24,128]{2,1,0:T(8,128)S(1)} %get-tuple-element.29), channel_id=1, source_target_pairs={{0,1},{1,2},{2,3},{3,4},{4,5},{5,6},{6,7},{8,9},{9,10},{10,11},{11... | collective-permute-start | bytes 221192 | tf_op jit(solution)/shard_map/ppermute | solution.py:593
  33.3 4.5 %copy-start.10 = (f32[23]{0:T(128)S(1)}, f32[23]{0:T(128)}, u32[]{:S(2)}) copy-start(f32[23]{0:T(128)} %param.20) | copy-start | bytes 280
  33.3 21.8 %copy-start.9 = (f32[24]{0:T(128)S(1)}, f32[24]{0:T(128)}, u32[]{:S(2)}) copy-start(f32[24]{0:T(128)} %param.21) | copy-start | bytes 292
  33.3 21.9 %copy-start.3 = (f32[10,16,128]{2,1,0:T(8,128)S(1)}, f32[10,16,128]{2,1,0:T(8,128)}, u32[]{:S(2)}) copy-start(f32[10,16,128]{2,1,0:T(8,128)} %base_volume.1) | copy-start | bytes 245764
  33.4 21.9 %copy-start.8 = (f32[9,16,128]{2,1,0:T(8,128)S(1)}, f32[9,16,128]{2,1,0:T(8,128)}, u32[]{:S(2)}) copy-start(f32[9,16,128]{2,1,0:T(8,128)} %diffusivity.1) | copy-start | bytes 221188
  36.6 1.3 %copy-start = (f32[10,16,24,128]{3,2,1,0:T(8,128)}, f32[10,16,24,128]{3,2,1,0:T(8,128)S(1)}, u32[]{:S(2)}) copy-start(f32[10,16,24,128]{3,2,1,0:T(8,128)S(1)} %first_divergence.1.div) | copy-start | bytes 5898244
  74.5 1.3 %copy-start.2 = (f32[10,16,24,128]{3,2,1,0:T(8,128)}, f32[10,16,24,128]{3,2,1,0:T(8,128)S(1)}, u32[]{:S(2)}) copy-start(f32[10,16,24,128]{3,2,1,0:T(8,128)S(1)} %get-tuple-element.30.state) | copy-start | bytes 5898244
  75.8 15.4 %collective-permute-start.4 = (f32[10,2,24,128]{3,2,1,0:T(8,128)S(1)}, f32[10,2,24,128]{3,2,1,0:T(8,128)S(1)}, u32[]{:S(2)}, u32[]{:S(2)}) collective-permute-start(f32[10,2,24,128]{3,2,1,0:T(8,128)S(1)} %get-tuple-element.31), channel_id=1, source_target_pairs={{0,8},{8,16},{16,24},{24,32},{32,40},{40,48},{48,56},{56,64},{64,7... | collective-permute-start | bytes 737288 | tf_op jit(solution)/shard_map/ppermute | solution.py:593
  77.7 13.5 %collective-permute-start.5 = (f32[10,2,24,128]{3,2,1,0:T(8,128)S(1)}, f32[10,2,24,128]{3,2,1,0:T(8,128)S(1)}, u32[]{:S(2)}, u32[]{:S(2)}) collective-permute-start(f32[10,2,24,128]{3,2,1,0:T(8,128)S(1)} %get-tuple-element.32), channel_id=1, source_target_pairs={{8,0},{16,8},{24,16},{32,24},{40,32},{48,40},{56,48},{64,56},{72,6... | collective-permute-start | bytes 737288 | tf_op jit(solution)/shard_map/ppermute | solution.py:598
  83.7 4.3 %collective-permute-start.7 = (f32[5,24,128]{2,1,0:T(8,128)S(1)}, f32[5,24,128]{2,1,0:T(8,128)S(1)}, u32[]{:S(2)}, u32[]{:S(2)}) collective-permute-start(f32[5,24,128]{2,1,0:T(8,128)S(1)} %get-tuple-element.34), channel_id=1, source_target_pairs={{1,0},{2,1},{3,2},{4,3},{5,4},{6,5},{7,6},{9,8},{10,9},{11,10},{12... | collective-permute-start | bytes 184328 | tf_op jit(solution)/shard_map/ppermute | solution.py:598
  85.6 5.5 %collective-permute-start.6 = (f32[5,24,128]{2,1,0:T(8,128)S(1)}, f32[5,24,128]{2,1,0:T(8,128)S(1)}, u32[]{:S(2)}, u32[]{:S(2)}) collective-permute-start(f32[5,24,128]{2,1,0:T(8,128)S(1)} %get-tuple-element.34), channel_id=1, source_target_pairs={{0,1},{1,2},{2,3},{3,4},{4,5},{5,6},{6,7},{8,9},{9,10},{10,11},{11... | collective-permute-start | bytes 184328 | tf_op jit(solution)/shard_map/ppermute | solution.py:593
  99.7 15.4 %collective-permute-start.8 = (f32[10,2,24,128]{3,2,1,0:T(8,128)S(1)}, f32[10,2,24,128]{3,2,1,0:T(8,128)S(1)}, u32[]{:S(2)}, u32[]{:S(2)}) collective-permute-start(f32[10,2,24,128]{3,2,1,0:T(8,128)S(1)} %get-tuple-element.37), channel_id=1, source_target_pairs={{0,8},{8,16},{16,24},{24,32},{32,40},{40,48},{48,56},{56,64},{64,7... | collective-permute-start | bytes 737288 | tf_op jit(solution)/shard_map/ppermute | solution.py:593
  101.6 13.5 %collective-permute-start.9 = (f32[10,2,24,128]{3,2,1,0:T(8,128)S(1)}, f32[10,2,24,128]{3,2,1,0:T(8,128)S(1)}, u32[]{:S(2)}, u32[]{:S(2)}) collective-permute-start(f32[10,2,24,128]{3,2,1,0:T(8,128)S(1)} %get-tuple-element.38), channel_id=1, source_target_pairs={{8,0},{16,8},{24,16},{32,24},{40,32},{48,40},{56,48},{64,56},{72,6... | collective-permute-start | bytes 737288 | tf_op jit(solution)/shard_map/ppermute | solution.py:598
  107.6 4.3 %collective-permute-start.11 = (f32[5,24,128]{2,1,0:T(8,128)S(1)}, f32[5,24,128]{2,1,0:T(8,128)S(1)}, u32[]{:S(2)}, u32[]{:S(2)}) collective-permute-start(f32[5,24,128]{2,1,0:T(8,128)S(1)} %get-tuple-element.40), channel_id=1, source_target_pairs={{1,0},{2,1},{3,2},{4,3},{5,4},{6,5},{7,6},{9,8},{10,9},{11,10},{12... | collective-permute-start | bytes 184328 | tf_op jit(solution)/shard_map/ppermute | solution.py:598
  109.6 5.5 %collective-permute-start.10 = (f32[5,24,128]{2,1,0:T(8,128)S(1)}, f32[5,24,128]{2,1,0:T(8,128)S(1)}, u32[]{:S(2)}, u32[]{:S(2)}) collective-permute-start(f32[5,24,128]{2,1,0:T(8,128)S(1)} %get-tuple-element.40), channel_id=1, source_target_pairs={{0,1},{1,2},{2,3},{3,4},{4,5},{5,6},{6,7},{8,9},{9,10},{10,11},{11... | collective-permute-start | bytes 184328 | tf_op jit(solution)/shard_map/ppermute | solution.py:593

commit v2 on v1

--- a/solution.py
+++ b/solution.py
@@ -9,7 +9,7 @@
 
 SUBSTEPS = 3
 STEP = 1.0 / SUBSTEPS
-VMEM_BYTES = 48 * 1024 * 1024
+VMEM_BYTES = 24 * 1024 * 1024
 PACK_VMEM_BYTES = 62 * 1024 * 1024
 F32 = jnp.float32
 BF16 = jnp.bfloat16
@@ -48,7 +48,7 @@
     layers, fine = volume.shape
     groups = fine // 128
     rows = 2 * layers + 1
-    step = 32 if groups % 32 == 0 else 8
+    step = 128 if groups % 128 == 0 else groups
     return pl.pallas_call(
         pack_kernel,
         grid=(groups // step,),
@@ -84,8 +84,7 @@
     return jnp.where((place >= 2) & (place < 6), even, roll(odd, 4))
 
 
-def widen(sent, layer):
-    tile = sent[layer // 2]
+def widen(tile, layer):
     return tile if layer % 2 == 0 else roll(tile, -4)
 
 
@@ -108,24 +107,34 @@
     return jnp.where(place < 4, last, first)
 
 
-def edge_pass(edges, left, right, flow_edges, flow_left, fixes):
+def edge_pass(place, edges, edges_swapped, flow_edges, flow_swapped, fixes):
     layers = fixes.shape[0]
-    flows_sent = layers // 2
+    odd = place[3] == 1
     for l in range(layers):
         flow = flow_edges[layers, l : l + 1, :]
-        other = flow_left[flows_sent, l // 2 : l // 2 + 1, :]
+        tile = [ref[l // 2] for ref in edges_swapped]
+        other = jnp.where(
+            odd, *[ref[layers // 2, l // 2 : l // 2 + 1, :] for ref in flow_swapped]
+        )
         fixes[l] = edge_divergence(
             edges[l],
-            widen(left, l),
-            widen(right, l),
+            widen(jnp.where(odd, tile[0], tile[1]), l),
+            widen(jnp.where(odd, tile[1], tile[0]), l),
             flow,
-            other if l % 2 == 0 else roll(other, -4),
+            widen(other, l),
         )
 
 
 def at_edges(shape):
     lane = lanes(shape)
     return (lane < 2) | (lane >= 126)
+
+
+def emit_swaps(place, state, swap_a, swap_b):
+    layers, rows = state.shape[0], state.shape[1]
+    low = place[2] * (rows - 2)
+    swap_b[:layers] = state[:, pl.ds(low, 2)]
+    swap_a[:layers] = state[:, pl.ds(rows - 2 - low, 2)]
 
 
 def emit_sent(edges, sent, with_flows):
@@ -142,17 +151,18 @@
 
 
 def start_kernel(
-    last, conc, flow_x, flow_y, wet_x, wet_y, state, low_x, high_x, edges, sent, qx, qy
+    place, conc, flow_x, flow_y, wet_x, wet_y, state, swap_a, swap_b, edges, sent, qx, qy
 ):
     layers, rows = flow_x.shape[0], flow_x.shape[1]
     subs = conc.shape[0] // (layers * rows)
     row = lax.broadcasted_iota(jnp.int32, flow_x.shape, 1)
     col = lax.broadcasted_iota(jnp.int32, flow_x.shape, 2)
-    keep_x = jnp.where((row == rows - 1) & (last[0] == 1), 0.0, 1.0)
-    keep_y = jnp.where((col == 127) & (last[1] == 1), 0.0, 1.0)
+    keep_x = jnp.where((row == rows - 1) & (place[0] == 1), 0.0, 1.0)
+    keep_y = jnp.where((col == 127) & (place[1] == 1), 0.0, 1.0)
     qx[...] = flow_x[...] * wet_x[...].astype(F32) * keep_x
     qy[...] = flow_y[...] * wet_y[...].astype(F32) * keep_y
-    high_x[layers] = jnp.zeros_like(high_x[layers])
+    for swap in (swap_a, swap_b):
+        swap[layers] = jnp.zeros_like(swap[layers])
     edges[layers] = jnp.zeros_like(edges[layers])
     sent[layers // 2] = jnp.zeros_like(sent[layers // 2])
 
@@ -162,20 +172,18 @@
             c = conc[pl.ds(l * rows + i, subs, stride=layers * rows), :]
             values.append(c)
             state[l, i] = c
-            if i < 2:
-                low_x[l, i] = c
-            if i >= rows - 2:
-                high_x[l, i - rows + 2] = c
         edges[l] = pack_layer(values)
         edges[layers, pl.ds(l, 1), :] = pack_layer([qy[l, i : i + 1, :] for i in range(rows)])
-        high_x[layers, 0, pl.ds(l, 1), :] = qx[l, rows - 1 :, :]
+        for swap in (swap_a, swap_b):
+            swap[layers, 0, pl.ds(l, 1), :] = qx[l, rows - 1 :, :]
         return carry
 
     lax.fori_loop(0, layers, layer, 0)
+    emit_swaps(place, state, swap_a, swap_b)
     emit_sent(edges, sent, True)
 
 
-def start(last, conc, flow_x, flow_y, wet_x, wet_y):
+def start(place, conc, flow_x, flow_y, wet_x, wet_y):
     subs, layers, rows, cols = conc.shape
     flows = jax.ShapeDtypeStruct(flow_x.shape, F32)
     return pl.pallas_call(
@@ -184,7 +192,7 @@
         out_specs=[VMEM] * 7,
         out_shape=[
             jax.ShapeDtypeStruct((layers, rows, subs, cols), F32),
-            jax.ShapeDtypeStruct((layers, 2, subs, cols), F32),
+            jax.ShapeDtypeStruct((layers + 1, 2, subs, cols), F32),
             jax.ShapeDtypeStruct((layers + 1, 2, subs, cols), F32),
             jax.ShapeDtypeStruct((layers + 1, subs, cols), F32),
             jax.ShapeDtypeStruct((layers // 2 + 1, subs, cols), F32),
@@ -194,7 +202,7 @@
         compiler_params=pltpu.CompilerParams(vmem_limit_bytes=VMEM_BYTES),
         cost_estimate=pl.CostEstimate(flops=10**6, bytes_accessed=8 * 10**6, transcendentals=0),
         name="start_state",
-    )(last, conc.reshape(subs * layers * rows, cols), flow_x, flow_y, wet_x, wet_y)
+    )(place, conc.reshape(subs * layers * rows, cols), flow_x, flow_y, wet_x, wet_y)
 
 
 def y_divergence(c, flows):
@@ -228,19 +236,23 @@
     return fluxes
 
 
-def x_rows(state, west, east, l, rows):
+def x_rows(state, place, swapped, l, rows):
     def get(i):
-        if i < 0:
-            return west[l, i + 2]
-        if i >= rows:
-            return east[l, i - rows]
-        return state[l, i]
+        if 0 <= i < rows:
+            return state[l, i]
+        j = i + 2 if i < 0 else i - rows
+        pair = [ref[l, j] for ref in (swapped if i < 0 else swapped[::-1])]
+        return jnp.where(place[2] == 1, *pair)
 
     return get
 
 
 def x_flows(qx, qx_west, l):
     return lambda i: qx_west if i < 0 else qx[l, i : i + 1, :]
+
+
+def west_flow(place, flow_swapped, layers, l):
+    return jnp.where(place[2] == 1, *[ref[layers, 0, pl.ds(l, 1), :] for ref in flow_swapped])
 
 
 def first_divergence_kernel(state, qx, qy, div):
@@ -310,10 +322,9 @@
     lax.fori_loop(0, rows // batch, some, 0)
 
 
-def emit_edges(state, low_x, high_x, edges, sent):
+def emit_edges(place, state, swap_a, swap_b, edges, sent):
     layers, rows = state.shape[0], state.shape[1]
-    low_x[...] = state[:, :2]
-    high_x[...] = state[:, rows - 2 :]
+    emit_swaps(place, state, swap_a, swap_b)
 
     def layer(l, carry):
         edges[l] = pack_layer([state[l, i] for i in range(rows)])
@@ -408,23 +419,24 @@
 
 
 def first_step_kernel(
+    place,
     slots,
     base_volume,
     diffusivity,
     state,
     div,
-    west,
-    east,
+    received_a,
+    received_b,
     edges_before,
-    left,
-    right,
+    edges_a,
+    edges_b,
     qx,
     rates,
     rates_before,
     inflow,
     new,
-    low_x,
-    high_x,
+    swap_a,
+    swap_b,
     edges,
     sent,
     coef,
@@ -438,12 +450,14 @@
     layers, rows = base_volume.shape[0], base_volume.shape[1]
     aggregate(slots, terms, spread, hot, total)
     factorize(total, base_volume, diffusivity, coef)
-    edge_pass(edges_before, left, right, edges_before, left, fixes)
+    received = (received_a, received_b)
+    edges_swapped = (edges_a, edges_b)
+    edge_pass(place, edges_before, edges_swapped, edges_before, edges_swapped, fixes)
     edge = at_edges(state.shape[2:])
 
     def explicit(l, carry):
-        get = x_rows(state, west, east, l, rows)
-        flow = x_flows(qx, west[layers, 0, pl.ds(l, 1), :], l)
+        get = x_rows(state, place, received, l, rows)
+        flow = x_flows(qx, west_flow(place, received, layers, l), l)
         low = x_faces(get, flow, -1, 1)
         high = x_faces(get, flow, rows - 3, rows - 1)
         fix = [roll(fixes[l], 124 - 8 * i) for i in range(rows)]
@@ -471,7 +485,7 @@
         new[l, i] = value
 
     solve(star, coef, emit)
-    emit_edges(new, low_x, high_x, edges, sent)
+    emit_edges(place, new, swap_a, swap_b, edges, sent)
 
 
 def state_shapes(shape):
@@ -485,12 +499,12 @@
     ]
 
 
-def first_step(slots, base_volume, diffusivity, state, *args):
+def first_step(place, slots, base_volume, diffusivity, state, *args):
     layers, rows, subs, cols = state.shape
     depth = min(2048, slots.shape[0] // 21 * 128)
     return pl.pallas_call(
         first_step_kernel,
-        in_specs=[VMEM] * 14,
+        in_specs=[SMEM] + [VMEM] * 14,
         out_specs=[VMEM] * 6,
         out_shape=state_shapes(state.shape)
         + [jax.ShapeDtypeStruct((5, layers, rows, cols), F32)],
@@ -505,20 +519,23 @@
         compiler_params=pltpu.CompilerParams(vmem_limit_bytes=VMEM_BYTES),
         cost_estimate=pl.CostEstimate(flops=10**9, bytes_accessed=10**7, transcendentals=0),
         name="aggregate_and_first_step",
-    )(slots, base_volume, diffusivity, state, *args)
+    )(place, slots, base_volume, diffusivity, state, *args)
 
 
 def later_step_kernel(
     final,
+    place,
     state,
-    west,
-    east,
+    received_a,
+    received_b,
     edges_before,
-    left,
-    right,
-    flow_west,
+    edges_a,
+    edges_b,
+    flow_a,
+    flow_b,
     flow_edges,
-    flow_left,
+    flow_edges_a,
+    flow_edges_b,
     qx,
     qy,
     coef,
@@ -532,8 +549,10 @@
         out, fixes, star = refs
         subs = out.shape[0] // (layers * rows)
     else:
-        new, low_x, high_x, edges, sent, fixes, star = refs
-    edge_pass(edges_before, left, right, flow_edges, flow_left, fixes)
+        new, swap_a, swap_b, edges, sent, fixes, star = refs
+    edge_pass(
+        place, edges_before, (edges_a, edges_b), flow_edges, (flow_edges_a, flow_edges_b), fixes
+    )
     edge = at_edges(state.shape[2:])
 
     def layer(l, carry):
@@ -541,8 +560,9 @@
         fix = [roll(fixes[l], 124 - 8 * i) for i in range(rows)]
         parts = y_divergence(c, [qy[l, i : i + 1, :] for i in range(rows)])
         parts = [jnp.where(edge, f, p) for f, p in zip(fix, parts)]
-        flow = x_flows(qx, flow_west[layers, 0, pl.ds(l, 1), :], l)
-        faces = x_faces(x_rows(state, west, east, l, rows), flow, -1, rows - 1)
+        flow = x_flows(qx, west_flow(place, (flow_a, flow_b), layers, l), l)
+        get = x_rows(state, place, (received_a, received_b), l, rows)
+        faces = x_faces(get, flow, -1, rows - 1)
         for i in range(rows):
             star[l, i] = explicit_value(
                 state[l, i],
@@ -565,10 +585,10 @@
 
     solve(star, coef, emit)
     if not final:
-        emit_edges(new, low_x, high_x, edges, sent)
-
-
-def later_step(final, state, *args):
+        emit_edges(place, new, swap_a, swap_b, edges, sent)
+
+
+def later_step(final, place, state, *args):
     layers, rows, subs, cols = state.shape
     if final:
         shapes = jax.ShapeDtypeStruct((subs * layers * rows, cols), F32)
@@ -578,32 +598,25 @@
         specs = [VMEM] * 5
     return pl.pallas_call(
         functools.partial(later_step_kernel, final),
-        in_specs=[VMEM] * 15,
+        in_specs=[SMEM] + [VMEM] * 17,
         out_specs=specs,
         out_shape=shapes,
         scratch_shapes=[pltpu.VMEM((layers, subs, cols), F32), pltpu.VMEM(state.shape, F32)],
         compiler_params=pltpu.CompilerParams(vmem_limit_bytes=VMEM_BYTES),
         cost_estimate=pl.CostEstimate(flops=3 * 10**7, bytes_accessed=10**7, transcendentals=0),
         name="last_step" if final else "middle_step",
-    )(state, *args)
-
-
-def to_next(values, axis):
-    size = lax.axis_size(axis)
-    return lax.ppermute(values, axis, [(i, i + 1) for i in range(size - 1)])
-
-
-def to_previous(values, axis):
-    size = lax.axis_size(axis)
-    return lax.ppermute(values, axis, [(i + 1, i) for i in range(size - 1)])
-
-
-def exchange(low_x, high_x, sent):
-    west = to_next(high_x, "gx")
-    east = to_previous(low_x, "gx")
-    left = to_next(sent, "gy")
-    right = to_previous(sent, "gy")
-    return (west, east, left, right)
+    )(place, state, *args)
+
+
+def swap(values, axis, first):
+    pairs = [(i, i + 1) for i in range(first, lax.axis_size(axis) - 1, 2)]
+    return lax.ppermute(values, axis, pairs + [(j, i) for i, j in pairs])
+
+
+def exchange(swap_a, swap_b, sent):
+    rows = (swap(swap_a, "gx", 0), swap(swap_b, "gx", 1))
+    columns = (swap(sent, "gy", 0), swap(sent, "gy", 1))
+    return (rows, columns)
 
 
 def local(
@@ -629,10 +642,13 @@
         slots.reshape(owners, 1, -1), ("gx", "gy"), split_axis=0, concat_axis=0, tiled=True
     ).reshape(slots.shape)
 
-    last = jnp.stack(
+    at_x, at_y = (lax.axis_index("gx"), lax.axis_index("gy"))
+    place = jnp.stack(
         [
-            (lax.axis_index("gx") == size_x - 1).astype(jnp.int32),
-            (lax.axis_index("gy") == size_y - 1).astype(jnp.int32),
+            (at_x == size_x - 1).astype(jnp.int32),
+            (at_y == size_y - 1).astype(jnp.int32),
+            at_x.astype(jnp.int32) % 2,
+            at_y.astype(jnp.int32) % 2,
         ]
     )
     rates = jnp.concatenate([jnp.zeros((1,), F32), decay_rates]) * STEP
@@ -640,23 +656,34 @@
     rates, rates_before, inflow = (
         jnp.broadcast_to(v[:, None], (subs, cols)) for v in (rates, rates_before, inflow)
     )
-    state, low_x, high_x, edges, sent, qx, qy = start(
-        last, concentration, flow_x, flow_y, face_wet_x, face_wet_y
-    )
-    west, east, left, right = exchange(low_x, high_x, sent)
-    flow_west, flow_edges, flow_left = (west, edges, left)
+    state, swap_a, swap_b, edges, sent, qx, qy = start(
+        place, concentration, flow_x, flow_y, face_wet_x, face_wet_y
+    )
+    rows_in, columns_in = exchange(swap_a, swap_b, sent)
+    flows = (*rows_in, edges, *columns_in, qx, qy)
     div = first_divergence(state, qx, qy)
     constants = (rates, rates_before, inflow)
-    state, low_x, high_x, edges, sent, coef = first_step(
-        arrived, base_volume, diffusivity, state, div, west, east, edges, left, right, qx, *constants
+    state, swap_a, swap_b, edges, sent, coef = first_step(
+        place,
+        arrived,
+        base_volume,
+        diffusivity,
+        state,
+        div,
+        *rows_in,
+        edges,
+        *columns_in,
+        qx,
+        *constants,
     )
     for step in range(1, SUBSTEPS):
         final = step == SUBSTEPS - 1
-        west, east, left, right = exchange(low_x, high_x, sent)
-        flows = (flow_west, flow_edges, flow_left, qx, qy, coef)
-        result = later_step(final, state, west, east, edges, left, right, *flows, *constants)
+        rows_in, columns_in = exchange(swap_a, swap_b, sent)
+        result = later_step(
+            final, place, state, *rows_in, edges, *columns_in, *flows, coef, *constants
+        )
         if not final:
-            state, low_x, high_x, edges, sent = result
+            state, swap_a, swap_b, edges, sent = result
     return result.reshape(concentration.shape)
 
 

time: 124 us -> 118 us (0.952)
  the two profiles are of different devices: /device:TPU:56 before, /device:TPU:16 now
where the time goes in v2:
time: 118 us; the launch traced here: 117 us
  Pallas kernels  43.2 us (37%)
  starting transfers between devices  35.3 us (30%)
  waiting for transfers between devices  27.1 us (23%)
  local copies, waits for them, and re-layouts  11 us (9%)
    ppermute x12, waiting for transfers between devices, swap(): return lax.ppermute(values, axis, pairs + [(j, i) for i, j in pairs])  27.1 us
    ppermute x12, starting transfers between devices, swap(): return lax.ppermute(values, axis, pairs + [(j, i) for i, j in pairs])  25 us
    pallas_call x1, Pallas kernels, first_step(): pl.pallas_call(first_step_kernel, in_specs=[SMEM] + [VMEM] * 14, out_spec...  17.4 us
    pallas_call x2, Pallas kernels, later_step(): pl.pallas_call(functools.partial(later_step_kernel, final), in_specs=[SME...  16.6 us
    unnamed x38, local copies, waits for them, and re-layouts  10.8 us
    all_to_all x1, starting transfers between devices, local(): lax.all_to_all(slots.reshape(owners, 1, -1), ('gx', 'gy'), split_axis=0,...  10.3 us
    pallas_call x1, Pallas kernels, pack_slots(): pl.pallas_call(pack_kernel, grid=(groups // step,), in_specs=[pl.BlockSpe...  3.48 us
    pallas_call x1, Pallas kernels, first_divergence(): pl.pallas_call(first_divergence_kernel, in_specs=[VMEM] * 3, out_specs=VM...  3.19 us
  transfers between devices with their start and end apart: 13, of which 6 were waited for; matrix products, arithmetic and copies ran while one was open for 0% of the time, Pallas kernels for 5%

profile of v2, /device:TPU:16, one launch (start us, length us, event | category | flops | bytes accessed | tf_op | source)
XLA Modules:
  0.0 117.0 jit_solution(1623849547693164530)
XLA Ops:
  0.0 3.5 %pack_slots.1 = f32[5376,128]{1,0:T(8,128)} custom-call(f32[10,32768]{1,0:T(8,128)} %volume.1, f32[10,32768]{1,0:T(8,128)} %discharge.1, s32[256,128]{1,0:T(8,128)} %bitcast.14, s32[256,128]{1,0:T(8,128)} %bitcast.15), custom_call_target="tpu_custom_call" | custom-call | bytes 8000000 | tf_op jit(solution)/shard_map/pack_slots/pallas_call | solution.py:52
  3.5 10.3 %all-to-all-start = ((f32[128,1,5376]{2,1,0:T(1,128)}), f32[128,1,5376]{2,1,0:T(1,128)S(1)}, u32[]{:S(2)}, u32[]{:S(2)}) async-start(f32[128,1,5376]{2,1,0:T(1,128)} %bitcast.13), calls=%async_computation | async-start | bytes 5505024 | tf_op jit(solution)/shard_map/all_to_all | solution.py:641
  14.0 1.5 %copy-done.4 = f32[24,10,16,128]{3,2,1,0:T(8,128)S(1)} copy-done((f32[24,10,16,128]{3,2,1,0:T(8,128)S(1)}, f32[24,10,16,128]{3,2,1,0:T(8,128)}, u32[]{:S(2)}) %copy-start.4) | copy-done | bytes 1966104
  15.5 2.5 %start_state.1 = (f32[10,16,24,128]{3,2,1,0:T(8,128)S(1)}, f32[11,2,24,128]{3,2,1,0:T(8,128)S(1)}, f32[11,2,24,128]{3,2,1,0:T(8,128)S(1)}, f32[11,24,128]{2,1,0:...) custom-call(s32[4]{0:T(128)S(1)} %pad_add_fusion.place, ...), custom_call_target="tpu_custom_call" | custom-call | flops 1000000 | bytes 8000000 | tf_op jit(solution)/shard_map/start_state/pallas_call | solution.py:189
  18.1 1.5 %collective-permute-start = (f32[11,2,24,128]{3,2,1,0:T(8,128)S(1)}, f32[11,2,24,128]{3,2,1,0:T(8,128)S(1)}, u32[]{:S(2)}, u32[]{:S(2)}) collective-permute-start(f32[11,2,24,128]{3,2,1,0:T(8,128)S(1)} %get-tuple-element.26), channel_id=1, source_target_pairs={{0,8},{16,24},{32,40},{48,56},{64,72},{80,88},{96,104},{112,120},{... | collective-permute-start | bytes 811016 | tf_op jit(solution)/shard_map/ppermute | solution.py:613
  19.6 4.0 %collective-permute-start.1 = (f32[11,2,24,128]{3,2,1,0:T(8,128)S(1)}, f32[11,2,24,128]{3,2,1,0:T(8,128)S(1)}, u32[]{:S(2)}, u32[]{:S(2)}) collective-permute-start(f32[11,2,24,128]{3,2,1,0:T(8,128)S(1)} %get-tuple-element.27), channel_id=1, source_target_pairs={{8,16},{24,32},{40,48},{56,64},{72,80},{88,96},{104,112},{16,8},{3... | collective-permute-start | bytes 811016 | tf_op jit(solution)/shard_map/ppermute | solution.py:613
  24.3 3.1 %collective-permute-start.2 = (f32[6,24,128]{2,1,0:T(8,128)S(1)}, f32[6,24,128]{2,1,0:T(8,128)S(1)}, u32[]{:S(2)}, u32[]{:S(2)}) collective-permute-start(f32[6,24,128]{2,1,0:T(8,128)S(1)} %get-tuple-element.29), channel_id=1, source_target_pairs={{0,1},{2,3},{4,5},{6,7},{1,0},{3,2},{5,4},{7,6},{8,9},{10,11},{12,... | collective-permute-start | bytes 221192 | tf_op jit(solution)/shard_map/ppermute | solution.py:613
  27.4 3.2 %first_divergence.1.div = f32[10,16,24,128]{3,2,1,0:T(8,128)S(1)} custom-call(f32[10,16,24,128]{3,2,1,0:T(8,128)S(1)} %get-tuple-element.23.state, f32[10,16,128]{2,1,0:T(8,128)S(1)} %get-tuple-element.24.qx, f32[10,16,128]{2,1,0:T(8,128)S(1)} %get-tuple-element.25.qy), custom_call_target="tpu_custom_call" | custom-call | flops 20000000 | bytes 10000000 | tf_op jit(solution)/shard_map/first_divergence/pallas_call | solution.py:277
  30.6 1.3 %copy-done.2 = f32[10,16,24,128]{3,2,1,0:T(8,128)} copy-done((f32[10,16,24,128]{3,2,1,0:T(8,128)}, f32[10,16,24,128]{3,2,1,0:T(8,128)S(1)}, u32[]{:S(2)}) %copy-start.2) | copy-done | bytes 1966104
  33.3 17.6 %collective-permute-done.received_a.flow_a = f32[11,2,24,128]{3,2,1,0:T(8,128)S(1)} collective-permute-done((f32[11,2,24,128]{3,2,1,0:T(8,128)S(1)}, f32[11,2,24,128]{3,2,1,0:T(8,128)S(1)}, u32[]{:S(2)}, u32[]{:S(2)}) %collective-permute-start) | collective-permute-done | bytes 270368 | tf_op jit(solution)/shard_map/ppermute | solution.py:613
  50.9 1.2 %collective-permute-done.1.received_b.flow_b = f32[11,2,24,128]{3,2,1,0:T(8,128)S(1)} collective-permute-done((f32[11,2,24,128]{3,2,1,0:T(8,128)S(1)}, f32[11,2,24,128]{3,2,1,0:T(8,128)S(1)}, u32[]{:S(2)}, u32[]{:S(2)}) %collective-permute-start.1) | collective-permute-done | bytes 270368 | tf_op jit(solution)/shard_map/ppermute | solution.py:613
  52.4 1.6 %copy-done.1 = f32[10,16,24,128]{3,2,1,0:T(8,128)S(1)} copy-done((f32[10,16,24,128]{3,2,1,0:T(8,128)S(1)}, f32[10,16,24,128]{3,2,1,0:T(8,128)}, u32[]{:S(2)}) %copy-start.1) | copy-done | bytes 1966104
  53.9 1.5 %copy-done.3 = f32[10,16,24,128]{3,2,1,0:T(8,128)S(1)} copy-done((f32[10,16,24,128]{3,2,1,0:T(8,128)S(1)}, f32[10,16,24,128]{3,2,1,0:T(8,128)}, u32[]{:S(2)}) %copy-start.3) | copy-done | bytes 1966104
  59.0 17.4 %aggregate_and_first_step.1 = (f32[10,16,24,128]{3,2,1,0:T(8,128)S(1)}, f32[10,2,24,128]{3,2,1,0:T(8,128)S(1)}, f32[10,2,24,128]{3,2,1,0:T(8,128)S(1)}, f32[10,2...) custom-call(s32[4]{0:T(128)S(1)} %pad_add_fusion.place, f32[5376,128]{1,0:T(8,128)S(1)} %bitcast.11, ...), custom_call_target="tpu_custom_call" | custom-call | flops 1000000000 | bytes 10000000 | tf_op jit(solution)/shard_map/aggregate_and_first_step/pallas_call | solution.py:505
  76.7 3.7 %collective-permute-start.5 = (f32[10,2,24,128]{3,2,1,0:T(8,128)S(1)}, f32[10,2,24,128]{3,2,1,0:T(8,128)S(1)}, u32[]{:S(2)}, u32[]{:S(2)}) collective-permute-start(f32[10,2,24,128]{3,2,1,0:T(8,128)S(1)} %get-tuple-element.32), channel_id=1, source_target_pairs={{8,16},{24,32},{40,48},{56,64},{72,80},{88,96},{104,112},{16,8},{3... | collective-permute-start | bytes 737288 | tf_op jit(solution)/shard_map/ppermute | solution.py:613
  81.1 3.3 %collective-permute-start.6 = (f32[5,24,128]{2,1,0:T(8,128)S(1)}, f32[5,24,128]{2,1,0:T(8,128)S(1)}, u32[]{:S(2)}, u32[]{:S(2)}) collective-permute-start(f32[5,24,128]{2,1,0:T(8,128)S(1)} %get-tuple-element.34), channel_id=1, source_target_pairs={{0,1},{2,3},{4,5},{6,7},{1,0},{3,2},{5,4},{7,6},{8,9},{10,11},{12,... | collective-permute-start | bytes 184328 | tf_op jit(solution)/shard_map/ppermute | solution.py:613
  84.4 0.9 collective-permute-done.6.edges_a
  85.3 2.9 %collective-permute-done.5.received_b = f32[10,2,24,128]{3,2,1,0:T(8,128)S(1)} collective-permute-done((f32[10,2,24,128]{3,2,1,0:T(8,128)S(1)}, f32[10,2,24,128]{3,2,1,0:T(8,128)S(1)}, u32[]{:S(2)}, u32[]{:S(2)}) %collective-permute-start.5) | collective-permute-done | bytes 245792 | tf_op jit(solution)/shard_map/ppermute | solution.py:613
  88.1 7.5 %middle_step.1 = (f32[10,16,24,128]{3,2,1,0:T(8,128)S(1)}, f32[10,2,24,128]{3,2,1,0:T(8,128)S(1)}, f32[10,2,24,128]{3,2,1,0:T(8,128)S(1)}, f32[10,24,128]{2,1,0:T(8,128)S(1)}, f32[5,24,128]{2,1,0:T(8,128)S(1)}) custom-call(s32[4]{0:T(128)S(1)} %pad_add_fusion.place, f32[10,16,24,128]{3,2,1,0:T(8,128)S(1)} %get-tuple-element.30.state, ...), custom_call_target="tpu_custom_call" | custom-call | flops 30000000 | bytes 10000000 | tf_op jit(solution)/shard_map/middle_step/pallas_call | solution.py:599
  95.7 3.7 %collective-permute-start.9 = (f32[10,2,24,128]{3,2,1,0:T(8,128)S(1)}, f32[10,2,24,128]{3,2,1,0:T(8,128)S(1)}, u32[]{:S(2)}, u32[]{:S(2)}) collective-permute-start(f32[10,2,24,128]{3,2,1,0:T(8,128)S(1)} %get-tuple-element.38), channel_id=1, source_target_pairs={{8,16},{24,32},{40,48},{56,64},{72,80},{88,96},{104,112},{16,8},{3... | collective-permute-start | bytes 737288 | tf_op jit(solution)/shard_map/ppermute | solution.py:613
  100.1 3.3 %collective-permute-start.10 = (f32[5,24,128]{2,1,0:T(8,128)S(1)}, f32[5,24,128]{2,1,0:T(8,128)S(1)}, u32[]{:S(2)}, u32[]{:S(2)}) collective-permute-start(f32[5,24,128]{2,1,0:T(8,128)S(1)} %get-tuple-element.40), channel_id=1, source_target_pairs={{0,1},{2,3},{4,5},{6,7},{1,0},{3,2},{5,4},{7,6},{8,9},{10,11},{12,... | collective-permute-start | bytes 184328 | tf_op jit(solution)/shard_map/ppermute | solution.py:613
  103.4 0.9 collective-permute-done.10.edges_a
  104.3 3.6 %collective-permute-done.9.received_b = f32[10,2,24,128]{3,2,1,0:T(8,128)S(1)} collective-permute-done((f32[10,2,24,128]{3,2,1,0:T(8,128)S(1)}, f32[10,2,24,128]{3,2,1,0:T(8,128)S(1)}, u32[]{:S(2)}, u32[]{:S(2)}) %collective-permute-start.9) | collective-permute-done | bytes 245792 | tf_op jit(solution)/shard_map/ppermute | solution.py:613
  108.0 9.1 %last_step.1 = f32[3840,128]{1,0:T(8,128)} custom-call(s32[4]{0:T(128)S(1)} %pad_add_fusion.place, f32[10,16,24,128]{3,2,1,0:T(8,128)S(1)} %get-tuple-element.36.state, f32[10,2,24,128]{3,2,1,0:T(8,128)S(1)} %collective-permute-done.8.received_a, f32[10,2,24,128]{3,2,1,0:T(8,128)S(1)} %collective-permute-done.9.received_b, ...), custom_call_target="tpu_custom_call" | custom-call | flops 30000000 | bytes 10000000 | tf_op jit(solution)/shard_map/last_step/pallas_call | solution.py:599
  (52 shorter events, 7.7 us)
Async XLA Ops:
  3.5 10.5 %copy-start.12 = (f32[10,16,128]{2,1,0:T(8,128)S(1)}, f32[10,16,128]{2,1,0:T(8,128)}, u32[]{:S(2)}) copy-start(f32[10,16,128]{2,1,0:T(8,128)} %flow_x.1) | copy-start | bytes 245764
  3.5 10.5 %copy-start.13 = (f32[10,16,128]{2,1,0:T(8,128)S(1)}, f32[10,16,128]{2,1,0:T(8,128)}, u32[]{:S(2)}) copy-start(f32[10,16,128]{2,1,0:T(8,128)} %flow_y.1) | copy-start | bytes 245764
  3.5 10.5 %copy-start.14 = (s32[10,16,128]{2,1,0:T(8,128)S(1)}, s32[10,16,128]{2,1,0:T(8,128)}, u32[]{:S(2)}) copy-start(s32[10,16,128]{2,1,0:T(8,128)} %wet_x.1) | copy-start | bytes 245764
  3.5 10.5 %copy-start.15 = (s32[10,16,128]{2,1,0:T(8,128)S(1)}, s32[10,16,128]{2,1,0:T(8,128)}, u32[]{:S(2)}) copy-start(s32[10,16,128]{2,1,0:T(8,128)} %wet_y.1) | copy-start | bytes 245764
  3.5 48.6 %all-to-all-start = ((f32[128,1,5376]{2,1,0:T(1,128)}), f32[128,1,5376]{2,1,0:T(1,128)S(1)}, u32[]{:S(2)}, u32[]{:S(2)}) async-start(f32[128,1,5376]{2,1,0:T(1,128)} %bitcast.13), calls=%async_computation | async-start | bytes 5505024 | tf_op jit(solution)/shard_map/all_to_all | solution.py:641
  14.0 1.5 %copy-start.4 = (f32[24,10,16,128]{3,2,1,0:T(8,128)S(1)}, f32[24,10,16,128]{3,2,1,0:T(8,128)}, u32[]{:S(2)}) copy-start(f32[24,10,16,128]{3,2,1,0:T(8,128)} %param.13) | copy-start | bytes 5898244
  18.1 12.5 %copy-start = (f32[10,16,24,128]{3,2,1,0:T(8,128)}, f32[10,16,24,128]{3,2,1,0:T(8,128)S(1)}, u32[]{:S(2)}) copy-start(f32[10,16,24,128]{3,2,1,0:T(8,128)S(1)} %get-tuple-element.23.state) | copy-start | bytes 5898244
  18.1 12.5 %copy-start.5 = (f32[10,16,128]{2,1,0:T(8,128)}, f32[10,16,128]{2,1,0:T(8,128)S(1)}, u32[]{:S(2)}) copy-start(f32[10,16,128]{2,1,0:T(8,128)S(1)} %get-tuple-element.25.qy) | copy-start | bytes 245764
  18.1 32.8 %collective-permute-start = (f32[11,2,24,128]{3,2,1,0:T(8,128)S(1)}, f32[11,2,24,128]{3,2,1,0:T(8,128)S(1)}, u32[]{:S(2)}, u32[]{:S(2)}) collective-permute-start(f32[11,2,24,128]{3,2,1,0:T(8,128)S(1)} %get-tuple-element.26), channel_id=1, source_target_pairs={{0,8},{16,24},{32,40},{48,56},{64,72},{80,88},{96,104},{112,120},{... | collective-permute-start | bytes 811016 | tf_op jit(solution)/shard_map/ppermute | solution.py:613
  19.6 32.5 %collective-permute-start.1 = (f32[11,2,24,128]{3,2,1,0:T(8,128)S(1)}, f32[11,2,24,128]{3,2,1,0:T(8,128)S(1)}, u32[]{:S(2)}, u32[]{:S(2)}) collective-permute-start(f32[11,2,24,128]{3,2,1,0:T(8,128)S(1)} %get-tuple-element.27), channel_id=1, source_target_pairs={{8,16},{24,32},{40,48},{56,64},{72,80},{88,96},{104,112},{16,8},{3... | collective-permute-start | bytes 811016 | tf_op jit(solution)/shard_map/ppermute | solution.py:613
  23.6 8.5 %collective-permute-start.3 = (f32[6,24,128]{2,1,0:T(8,128)S(1)}, f32[6,24,128]{2,1,0:T(8,128)S(1)}, u32[]{:S(2)}, u32[]{:S(2)}) collective-permute-start(f32[6,24,128]{2,1,0:T(8,128)S(1)} %get-tuple-element.29), channel_id=1, source_target_pairs={{1,2},{3,4},{5,6},{2,1},{4,3},{6,5},{9,10},{11,12},{13,14},{10,9},... | collective-permute-start | bytes 221192 | tf_op jit(solution)/shard_map/ppermute | solution.py:613
  24.3 8.4 %collective-permute-start.2 = (f32[6,24,128]{2,1,0:T(8,128)S(1)}, f32[6,24,128]{2,1,0:T(8,128)S(1)}, u32[]{:S(2)}, u32[]{:S(2)}) collective-permute-start(f32[6,24,128]{2,1,0:T(8,128)S(1)} %get-tuple-element.29), channel_id=1, source_target_pairs={{0,1},{2,3},{4,5},{6,7},{1,0},{3,2},{5,4},{7,6},{8,9},{10,11},{12,... | collective-permute-start | bytes 221192 | tf_op jit(solution)/shard_map/ppermute | solution.py:613
  27.4 4.5 %copy-start.18 = (f32[23]{0:T(128)S(1)}, f32[23]{0:T(128)}, u32[]{:S(2)}) copy-start(f32[23]{0:T(128)} %param.20) | copy-start | bytes 280
  27.4 24.9 %copy-start.17 = (f32[24]{0:T(128)S(1)}, f32[24]{0:T(128)}, u32[]{:S(2)}) copy-start(f32[24]{0:T(128)} %param.21) | copy-start | bytes 292
  52.4 1.6 %copy-start.1 = (f32[10,16,24,128]{3,2,1,0:T(8,128)S(1)}, f32[10,16,24,128]{3,2,1,0:T(8,128)}, u32[]{:S(2)}) copy-start(f32[10,16,24,128]{3,2,1,0:T(8,128)} %copy-done) | copy-start | bytes 5898244
  59.0 29.1 %copy-start.6 = (f32[10,16,128]{2,1,0:T(8,128)S(1)}, f32[10,16,128]{2,1,0:T(8,128)}, u32[]{:S(2)}) copy-start(f32[10,16,128]{2,1,0:T(8,128)} %copy-done.5) | copy-start | bytes 245764
  76.4 8.9 %collective-permute-start.4 = (f32[10,2,24,128]{3,2,1,0:T(8,128)S(1)}, f32[10,2,24,128]{3,2,1,0:T(8,128)S(1)}, u32[]{:S(2)}, u32[]{:S(2)}) collective-permute-start(f32[10,2,24,128]{3,2,1,0:T(8,128)S(1)} %get-tuple-element.31), channel_id=1, source_target_pairs={{0,8},{16,24},{32,40},{48,56},{64,72},{80,88},{96,104},{112,120},{... | collective-permute-start | bytes 737288 | tf_op jit(solution)/shard_map/ppermute | solution.py:613
  76.7 11.4 %collective-permute-start.5 = (f32[10,2,24,128]{3,2,1,0:T(8,128)S(1)}, f32[10,2,24,128]{3,2,1,0:T(8,128)S(1)}, u32[]{:S(2)}, u32[]{:S(2)}) collective-permute-start(f32[10,2,24,128]{3,2,1,0:T(8,128)S(1)} %get-tuple-element.32), channel_id=1, source_target_pairs={{8,16},{24,32},{40,48},{56,64},{72,80},{88,96},{104,112},{16,8},{3... | collective-permute-start | bytes 737288 | tf_op jit(solution)/shard_map/ppermute | solution.py:613
  80.4 4.0 %collective-permute-start.7 = (f32[5,24,128]{2,1,0:T(8,128)S(1)}, f32[5,24,128]{2,1,0:T(8,128)S(1)}, u32[]{:S(2)}, u32[]{:S(2)}) collective-permute-start(f32[5,24,128]{2,1,0:T(8,128)S(1)} %get-tuple-element.34), channel_id=1, source_target_pairs={{1,2},{3,4},{5,6},{2,1},{4,3},{6,5},{9,10},{11,12},{13,14},{10,9},... | collective-permute-start | bytes 184328 | tf_op jit(solution)/shard_map/ppermute | solution.py:613
  81.1 4.2 %collective-permute-start.6 = (f32[5,24,128]{2,1,0:T(8,128)S(1)}, f32[5,24,128]{2,1,0:T(8,128)S(1)}, u32[]{:S(2)}, u32[]{:S(2)}) collective-permute-start(f32[5,24,128]{2,1,0:T(8,128)S(1)} %get-tuple-element.34), channel_id=1, source_target_pairs={{0,1},{2,3},{4,5},{6,7},{1,0},{3,2},{5,4},{7,6},{8,9},{10,11},{12,... | collective-permute-start | bytes 184328 | tf_op jit(solution)/shard_map/ppermute | solution.py:613
  95.6 8.7 %collective-permute-start.8 = (f32[10,2,24,128]{3,2,1,0:T(8,128)S(1)}, f32[10,2,24,128]{3,2,1,0:T(8,128)S(1)}, u32[]{:S(2)}, u32[]{:S(2)}) collective-permute-start(f32[10,2,24,128]{3,2,1,0:T(8,128)S(1)} %get-tuple-element.37), channel_id=1, source_target_pairs={{0,8},{16,24},{32,40},{48,56},{64,72},{80,88},{96,104},{112,120},{... | collective-permute-start | bytes 737288 | tf_op jit(solution)/shard_map/ppermute | solution.py:613
  95.7 12.2 %collective-permute-start.9 = (f32[10,2,24,128]{3,2,1,0:T(8,128)S(1)}, f32[10,2,24,128]{3,2,1,0:T(8,128)S(1)}, u32[]{:S(2)}, u32[]{:S(2)}) collective-permute-start(f32[10,2,24,128]{3,2,1,0:T(8,128)S(1)} %get-tuple-element.38), channel_id=1, source_target_pairs={{8,16},{24,32},{40,48},{56,64},{72,80},{88,96},{104,112},{16,8},{3... | collective-permute-start | bytes 737288 | tf_op jit(solution)/shard_map/ppermute | solution.py:613
  99.4 4.0 %collective-permute-start.11 = (f32[5,24,128]{2,1,0:T(8,128)S(1)}, f32[5,24,128]{2,1,0:T(8,128)S(1)}, u32[]{:S(2)}, u32[]{:S(2)}) collective-permute-start(f32[5,24,128]{2,1,0:T(8,128)S(1)} %get-tuple-element.40), channel_id=1, source_target_pairs={{1,2},{3,4},{5,6},{2,1},{4,3},{6,5},{9,10},{11,12},{13,14},{10,9},... | collective-permute-start | bytes 184328 | tf_op jit(solution)/shard_map/ppermute | solution.py:613
  100.1 4.2 %collective-permute-start.10 = (f32[5,24,128]{2,1,0:T(8,128)S(1)}, f32[5,24,128]{2,1,0:T(8,128)S(1)}, u32[]{:S(2)}, u32[]{:S(2)}) collective-permute-start(f32[5,24,128]{2,1,0:T(8,128)S(1)} %get-tuple-element.40), channel_id=1, source_target_pairs={{0,1},{2,3},{4,5},{6,7},{1,0},{3,2},{5,4},{7,6},{8,9},{10,11},{12,... | collective-permute-start | bytes 184328 | tf_op jit(solution)/shard_map/ppermute | solution.py:613
  (8 other events, 7.7 us)

commit v3 on v2

--- a/solution.py
+++ b/solution.py
@@ -383,6 +383,30 @@
         return carry
 
     lax.fori_loop(0, slots.shape[0] // terms.shape[1], chunk, 0)
+
+
+def totals_kernel(slots, total, terms, spread, hot):
+    aggregate(slots, terms, spread, hot, total)
+
+
+def totals(slots):
+    depth = min(2048, slots.shape[0] // 21 * 128)
+    return pl.pallas_call(
+        totals_kernel,
+        in_specs=[VMEM],
+        out_specs=VMEM,
+        out_shape=jax.ShapeDtypeStruct((320, 256), F32),
+        scratch_shapes=[
+            pltpu.VMEM((2, depth // 128 * 21, 128), F32),
+            pltpu.VMEM((320, depth), BF16),
+            pltpu.VMEM((256, depth), BF16),
+        ],
+        compiler_params=pltpu.CompilerParams(vmem_limit_bytes=VMEM_BYTES),
+        cost_estimate=pl.CostEstimate(
+            flops=12 * 10**9, bytes_accessed=4 * 10**6, transcendentals=0
+        ),
+        name="aggregate",
+    )(slots)
 
 
 def factorize(total, base_volume, diffusivity, coef):
@@ -420,7 +444,7 @@
 
 def first_step_kernel(
     place,
-    slots,
+    total,
     base_volume,
     diffusivity,
     state,
@@ -440,15 +464,10 @@
     edges,
     sent,
     coef,
-    terms,
-    spread,
-    hot,
-    total,
     fixes,
     star,
 ):
     layers, rows = base_volume.shape[0], base_volume.shape[1]
-    aggregate(slots, terms, spread, hot, total)
     factorize(total, base_volume, diffusivity, coef)
     received = (received_a, received_b)
     edges_swapped = (edges_a, edges_b)
@@ -499,9 +518,8 @@
     ]
 
 
-def first_step(place, slots, base_volume, diffusivity, state, *args):
+def first_step(place, total, base_volume, diffusivity, state, *args):
     layers, rows, subs, cols = state.shape
-    depth = min(2048, slots.shape[0] // 21 * 128)
     return pl.pallas_call(
         first_step_kernel,
         in_specs=[SMEM] + [VMEM] * 14,
@@ -509,17 +527,13 @@
         out_shape=state_shapes(state.shape)
         + [jax.ShapeDtypeStruct((5, layers, rows, cols), F32)],
         scratch_shapes=[
-            pltpu.VMEM((2, depth // 128 * 21, 128), F32),
-            pltpu.VMEM((2 * layers * 16, depth), BF16),
-            pltpu.VMEM((256, depth), BF16),
-            pltpu.VMEM((2 * layers * 16, 256), F32),
             pltpu.VMEM((layers, subs, cols), F32),
             pltpu.VMEM(state.shape, F32),
         ],
         compiler_params=pltpu.CompilerParams(vmem_limit_bytes=VMEM_BYTES),
-        cost_estimate=pl.CostEstimate(flops=10**9, bytes_accessed=10**7, transcendentals=0),
-        name="aggregate_and_first_step",
-    )(place, slots, base_volume, diffusivity, state, *args)
+        cost_estimate=pl.CostEstimate(flops=2 * 10**7, bytes_accessed=10**7, transcendentals=0),
+        name="first_step",
+    )(place, total, base_volume, diffusivity, state, *args)
 
 
 def later_step_kernel(
@@ -665,7 +679,7 @@
     constants = (rates, rates_before, inflow)
     state, swap_a, swap_b, edges, sent, coef = first_step(
         place,
-        arrived,
+        totals(arrived),
         base_volume,
         diffusivity,
         state,

time: 118 us -> 113 us (0.958)
  local copies, waits for them, and re-layouts: 11 us -> 3.05 us
  Pallas kernels: 43.2 us -> 45.9 us
    all_to_all x1, waiting for transfers between devices: 0.01 us -> 16.7 us  [local(): lax.all_to_all(slots.reshape(owners, 1, -1), ('gx', 'gy'), split_axis=0,...]
    ppermute x12, waiting for transfers between devices: 27.1 us -> 10.6 us  [swap(): return lax.ppermute(values, axis, pairs + [(j, i) for i, j in pairs])]
    pallas_call x0 -> x1, Pallas kernels: none -> 15.1 us  [totals(): pl.pallas_call(totals_kernel, in_specs=[VMEM], out_specs=VMEM, out_shape=...]
    pallas_call x1, Pallas kernels: 17.4 us -> 4.31 us  [first_step(): pl.pallas_call(first_step_kernel, in_specs=[SMEM] + [VMEM] * 14, out_spec...]
    unnamed x38 -> x22, local copies, waits for them, and re-layouts: 10.8 us -> 2.85 us
  transfers between devices with their start and end apart: 13 -> 13, of which waited for: 6 -> 5; matrix products, arithmetic and copies ran while one was open for 0% -> 0% of each run, Pallas kernels for 5% -> 19%
where the time goes in v3:
time: 113 us
  Pallas kernels  45.9 us (41%)
  starting transfers between devices  35.9 us (32%)
  waiting for transfers between devices  27.4 us (24%)
  local copies, waits for them, and re-layouts  3.05 us (3%)
    ppermute x12, starting transfers between devices, swap(): return lax.ppermute(values, axis, pairs + [(j, i) for i, j in pairs])  25.2 us
    all_to_all x1, waiting for transfers between devices, local(): lax.all_to_all(slots.reshape(owners, 1, -1), ('gx', 'gy'), split_axis=0,...  16.7 us
    pallas_call x2, Pallas kernels, later_step(): pl.pallas_call(functools.partial(later_step_kernel, final), in_specs=[SME...  16.6 us
    pallas_call x1, Pallas kernels, totals(): pl.pallas_call(totals_kernel, in_specs=[VMEM], out_specs=VMEM, out_shape=...  15.1 us
    all_to_all x1, starting transfers between devices, local(): lax.all_to_all(slots.reshape(owners, 1, -1), ('gx', 'gy'), split_axis=0,...  10.7 us
    ppermute x12, waiting for transfers between devices, swap(): return lax.ppermute(values, axis, pairs + [(j, i) for i, j in pairs])  10.6 us
    pallas_call x1, Pallas kernels, first_step(): pl.pallas_call(first_step_kernel, in_specs=[SMEM] + [VMEM] * 14, out_spec...  4.31 us
    pallas_call x1, Pallas kernels, pack_slots(): pl.pallas_call(pack_kernel, grid=(groups // step,), in_specs=[pl.BlockSpe...  3.5 us
  transfers between devices with their start and end apart: 13, of which 5 were waited for; matrix products, arithmetic and copies ran while one was open for 0% of the time, Pallas kernels for 19%

profile of v3, /device:TPU:16, one launch (start us, length us, event | category | flops | bytes accessed | tf_op | source)
XLA Modules:
  0.0 112.7 jit_solution(15668642866867863321)
XLA Ops:
  0.0 3.5 %pack_slots.1 = f32[5376,128]{1,0:T(8,128)} custom-call(f32[10,32768]{1,0:T(8,128)} %volume.1, f32[10,32768]{1,0:T(8,128)} %discharge.1, s32[256,128]{1,0:T(8,128)} %bitcast.13, s32[256,128]{1,0:T(8,128)} %bitcast.14), custom_call_target="tpu_custom_call" | custom-call | bytes 8000000 | tf_op jit(solution)/shard_map/pack_slots/pallas_call | solution.py:52
  3.5 10.7 %all-to-all-start = ((f32[128,1,5376]{2,1,0:T(1,128)}), f32[128,1,5376]{2,1,0:T(1,128)}, u32[]{:S(2)}, u32[]{:S(2)}) async-start(f32[128,1,5376]{2,1,0:T(1,128)} %bitcast.12), calls=%async_computation | async-start | bytes 5505024 | tf_op jit(solution)/shard_map/all_to_all | solution.py:655
  14.4 1.5 %copy-done.2 = f32[24,10,16,128]{3,2,1,0:T(8,128)S(1)} copy-done((f32[24,10,16,128]{3,2,1,0:T(8,128)S(1)}, f32[24,10,16,128]{3,2,1,0:T(8,128)}, u32[]{:S(2)}) %copy-start.2) | copy-done | bytes 1966104
  15.9 3.2 %start_state.1 = (f32[10,16,24,128]{3,2,1,0:T(8,128)S(1)}, f32[11,2,24,128]{3,2,1,0:T(8,128)S(1)}, f32[11,2,24,128]{3,2,1,0:T(8,128)S(1)}, f32[11,24,128]{2,1,0:...) custom-call(s32[4]{0:T(128)S(1)} %pad_add_fusion.place, ...), custom_call_target="tpu_custom_call" | custom-call | flops 1000000 | bytes 8000000 | tf_op jit(solution)/shard_map/start_state/pallas_call | solution.py:189
  19.8 3.1 %collective-permute-start.2 = (f32[6,24,128]{2,1,0:T(8,128)}, f32[6,24,128]{2,1,0:T(8,128)S(1)}, u32[]{:S(2)}, u32[]{:S(2)}) collective-permute-start(f32[6,24,128]{2,1,0:T(8,128)} %get-tuple-element.29), channel_id=1, source_target_pairs={{0,1},{2,3},{4,5},{6,7},{1,0},{3,2},{5,4},{7,6},{8,9},{10,11},{12,... | collective-permute-start | bytes 221192 | tf_op jit(solution)/shard_map/ppermute | solution.py:627
  22.9 1.5 %collective-permute-start = (f32[11,2,24,128]{3,2,1,0:T(8,128)S(1)}, f32[11,2,24,128]{3,2,1,0:T(8,128)S(1)}, u32[]{:S(2)}, u32[]{:S(2)}) collective-permute-start(f32[11,2,24,128]{3,2,1,0:T(8,128)S(1)} %get-tuple-element.26), channel_id=1, source_target_pairs={{0,8},{16,24},{32,40},{48,56},{64,72},{80,88},{96,104},{112,120},{... | collective-permute-start | bytes 811016 | tf_op jit(solution)/shard_map/ppermute | solution.py:627
  24.4 3.9 %collective-permute-start.1 = (f32[11,2,24,128]{3,2,1,0:T(8,128)S(1)}, f32[11,2,24,128]{3,2,1,0:T(8,128)S(1)}, u32[]{:S(2)}, u32[]{:S(2)}) collective-permute-start(f32[11,2,24,128]{3,2,1,0:T(8,128)S(1)} %get-tuple-element.27), channel_id=1, source_target_pairs={{8,16},{24,32},{40,48},{56,64},{72,80},{88,96},{104,112},{16,8},{3... | collective-permute-start | bytes 811016 | tf_op jit(solution)/shard_map/ppermute | solution.py:627
  28.3 3.2 %first_divergence.1.div = f32[10,16,24,128]{3,2,1,0:T(8,128)S(1)} custom-call(f32[10,16,24,128]{3,2,1,0:T(8,128)S(1)} %get-tuple-element.23.state, f32[10,16,128]{2,1,0:T(8,128)S(1)} %get-tuple-element.24.qx, f32[10,16,128]{2,1,0:T(8,128)S(1)} %get-tuple-element.25.qy), custom_call_target="tpu_custom_call" | custom-call | flops 20000000 | bytes 10000000 | tf_op jit(solution)/shard_map/first_divergence/pallas_call | solution.py:277
  31.5 1.3 %copy-done = f32[10,16,24,128]{3,2,1,0:T(8,128)} copy-done((f32[10,16,24,128]{3,2,1,0:T(8,128)}, f32[10,16,24,128]{3,2,1,0:T(8,128)S(1)}, u32[]{:S(2)}) %copy-start) | copy-done | bytes 1966104
  33.0 16.7 %all-to-all-done = f32[128,1,5376]{2,1,0:T(1,128)} async-done(((f32[128,1,5376]{2,1,0:T(1,128)}), f32[128,1,5376]{2,1,0:T(1,128)}, u32[]{:S(2)}, u32[]{:S(2)}) %all-to-all-start) | async-done | bytes 2752544 | tf_op jit(solution)/shard_map/all_to_all | solution.py:655
  49.7 15.1 %aggregate.1.total = f32[320,256]{1,0:T(8,128)S(1)} custom-call(f32[5376,128]{1,0:T(8,128)} %bitcast.7.slots), custom_call_target="tpu_custom_call" | custom-call | flops 12000000000 | bytes 4000000 | tf_op jit(solution)/shard_map/aggregate/pallas_call | solution.py:394
  65.1 4.3 %first_step.1 = (f32[10,16,24,128]{3,2,1,0:T(8,128)S(1)}, f32[10,2,24,128]{3,2,1,0:T(8,128)S(1)}, f32[10,2,24,128]{3,2,1,0:T(8,128)S(1)}, f32[10,24,128]{2,1,0:T...) custom-call(s32[4]{0:T(128)S(1)} %pad_add_fusion.place, f32[320,256]{1,0:T(8,128)S(1)} %aggregate.1.total, ...), custom_call_target="tpu_custom_call" | custom-call | flops 20000000 | bytes 10000000 | tf_op jit(solution)/shard_map/first_step/pallas_call | solution.py:523
  69.5 1.0 collective-permute-start.4
  70.5 3.2 %collective-permute-start.5 = (f32[10,2,24,128]{3,2,1,0:T(8,128)S(1)}, f32[10,2,24,128]{3,2,1,0:T(8,128)S(1)}, u32[]{:S(2)}, u32[]{:S(2)}) collective-permute-start(f32[10,2,24,128]{3,2,1,0:T(8,128)S(1)} %get-tuple-element.32), channel_id=1, source_target_pairs={{8,16},{24,32},{40,48},{56,64},{72,80},{88,96},{104,112},{16,8},{3... | collective-permute-start | bytes 737288 | tf_op jit(solution)/shard_map/ppermute | solution.py:627
  74.4 2.1 %collective-permute-start.6 = (f32[5,24,128]{2,1,0:T(8,128)S(1)}, f32[5,24,128]{2,1,0:T(8,128)S(1)}, u32[]{:S(2)}, u32[]{:S(2)}) collective-permute-start(f32[5,24,128]{2,1,0:T(8,128)S(1)} %get-tuple-element.34), channel_id=1, source_target_pairs={{0,1},{2,3},{4,5},{6,7},{1,0},{3,2},{5,4},{7,6},{8,9},{10,11},{12,... | collective-permute-start | bytes 184328 | tf_op jit(solution)/shard_map/ppermute | solution.py:627
  76.5 0.9 collective-permute-done.6.edges_a
  77.4 3.8 %collective-permute-done.5.received_b = f32[10,2,24,128]{3,2,1,0:T(8,128)S(1)} collective-permute-done((f32[10,2,24,128]{3,2,1,0:T(8,128)S(1)}, f32[10,2,24,128]{3,2,1,0:T(8,128)S(1)}, u32[]{:S(2)}, u32[]{:S(2)}) %collective-permute-start.5) | collective-permute-done | bytes 245792 | tf_op jit(solution)/shard_map/ppermute | solution.py:627
  81.2 7.5 %middle_step.1 = (f32[10,16,24,128]{3,2,1,0:T(8,128)S(1)}, f32[10,2,24,128]{3,2,1,0:T(8,128)S(1)}, f32[10,2,24,128]{3,2,1,0:T(8,128)S(1)}, f32[10,24,128]{2,1,0:T(8,128)S(1)}, f32[5,24,128]{2,1,0:T(8,128)S(1)}) custom-call(s32[4]{0:T(128)S(1)} %pad_add_fusion.place, f32[10,16,24,128]{3,2,1,0:T(8,128)S(1)} %get-tuple-element.30.state, ...), custom_call_target="tpu_custom_call" | custom-call | flops 30000000 | bytes 10000000 | tf_op jit(solution)/shard_map/middle_step/pallas_call | solution.py:613
  88.7 2.4 %collective-permute-start.8 = (f32[10,2,24,128]{3,2,1,0:T(8,128)S(1)}, f32[10,2,24,128]{3,2,1,0:T(8,128)S(1)}, u32[]{:S(2)}, u32[]{:S(2)}) collective-permute-start(f32[10,2,24,128]{3,2,1,0:T(8,128)S(1)} %get-tuple-element.37), channel_id=1, source_target_pairs={{0,8},{16,24},{32,40},{48,56},{64,72},{80,88},{96,104},{112,120},{... | collective-permute-start | bytes 737288 | tf_op jit(solution)/shard_map/ppermute | solution.py:627
  91.1 1.9 %collective-permute-start.9 = (f32[10,2,24,128]{3,2,1,0:T(8,128)S(1)}, f32[10,2,24,128]{3,2,1,0:T(8,128)S(1)}, u32[]{:S(2)}, u32[]{:S(2)}) collective-permute-start(f32[10,2,24,128]{3,2,1,0:T(8,128)S(1)} %get-tuple-element.38), channel_id=1, source_target_pairs={{8,16},{24,32},{40,48},{56,64},{72,80},{88,96},{104,112},{16,8},{3... | collective-permute-start | bytes 737288 | tf_op jit(solution)/shard_map/ppermute | solution.py:627
  93.7 4.0 %collective-permute-start.10 = (f32[5,24,128]{2,1,0:T(8,128)S(1)}, f32[5,24,128]{2,1,0:T(8,128)S(1)}, u32[]{:S(2)}, u32[]{:S(2)}) collective-permute-start(f32[5,24,128]{2,1,0:T(8,128)S(1)} %get-tuple-element.40), channel_id=1, source_target_pairs={{0,1},{2,3},{4,5},{6,7},{1,0},{3,2},{5,4},{7,6},{8,9},{10,11},{12,... | collective-permute-start | bytes 184328 | tf_op jit(solution)/shard_map/ppermute | solution.py:627
  97.7 0.9 collective-permute-done.10.edges_a
  98.6 5.0 %collective-permute-done.9.received_b = f32[10,2,24,128]{3,2,1,0:T(8,128)S(1)} collective-permute-done((f32[10,2,24,128]{3,2,1,0:T(8,128)S(1)}, f32[10,2,24,128]{3,2,1,0:T(8,128)S(1)}, u32[]{:S(2)}, u32[]{:S(2)}) %collective-permute-start.9) | collective-permute-done | bytes 245792 | tf_op jit(solution)/shard_map/ppermute | solution.py:627
  103.6 9.1 %last_step.1 = f32[3840,128]{1,0:T(8,128)} custom-call(s32[4]{0:T(128)S(1)} %pad_add_fusion.place, f32[10,16,24,128]{3,2,1,0:T(8,128)S(1)} %get-tuple-element.36.state, f32[10,2,24,128]{3,2,1,0:T(8,128)S(1)} %collective-permute-done.8.received_a, f32[10,2,24,128]{3,2,1,0:T(8,128)S(1)} %collective-permute-done.9.received_b, ...), custom_call_target="tpu_custom_call" | custom-call | flops 30000000 | bytes 10000000 | tf_op jit(solution)/shard_map/last_step/pallas_call | solution.py:613
  (37 shorter events, 2.5 us)
Async XLA Ops:
  3.5 10.9 %copy-start.3 = (f32[10,16,128]{2,1,0:T(8,128)S(1)}, f32[10,16,128]{2,1,0:T(8,128)}, u32[]{:S(2)}) copy-start(f32[10,16,128]{2,1,0:T(8,128)} %flow_x.1) | copy-start | bytes 245764
  3.5 10.9 %copy-start.4 = (f32[10,16,128]{2,1,0:T(8,128)S(1)}, f32[10,16,128]{2,1,0:T(8,128)}, u32[]{:S(2)}) copy-start(f32[10,16,128]{2,1,0:T(8,128)} %flow_y.1) | copy-start | bytes 245764
  3.5 10.9 %copy-start.5 = (s32[10,16,128]{2,1,0:T(8,128)S(1)}, s32[10,16,128]{2,1,0:T(8,128)}, u32[]{:S(2)}) copy-start(s32[10,16,128]{2,1,0:T(8,128)} %wet_x.1) | copy-start | bytes 245764
  3.5 10.9 %copy-start.6 = (s32[10,16,128]{2,1,0:T(8,128)S(1)}, s32[10,16,128]{2,1,0:T(8,128)}, u32[]{:S(2)}) copy-start(s32[10,16,128]{2,1,0:T(8,128)} %wet_y.1) | copy-start | bytes 245764
  3.5 46.2 %all-to-all-start = ((f32[128,1,5376]{2,1,0:T(1,128)}), f32[128,1,5376]{2,1,0:T(1,128)}, u32[]{:S(2)}, u32[]{:S(2)}) async-start(f32[128,1,5376]{2,1,0:T(1,128)} %bitcast.12), calls=%async_computation | async-start | bytes 5505024 | tf_op jit(solution)/shard_map/all_to_all | solution.py:655
  14.4 1.5 %copy-start.2 = (f32[24,10,16,128]{3,2,1,0:T(8,128)S(1)}, f32[24,10,16,128]{3,2,1,0:T(8,128)}, u32[]{:S(2)}) copy-start(f32[24,10,16,128]{3,2,1,0:T(8,128)} %param.13) | copy-start | bytes 5898244
  19.1 45.8 %collective-permute-start.3 = (f32[6,24,128]{2,1,0:T(8,128)}, f32[6,24,128]{2,1,0:T(8,128)S(1)}, u32[]{:S(2)}, u32[]{:S(2)}) collective-permute-start(f32[6,24,128]{2,1,0:T(8,128)} %get-tuple-element.29), channel_id=1, source_target_pairs={{1,2},{3,4},{5,6},{2,1},{4,3},{6,5},{9,10},{11,12},{13,14},{10,9},... | collective-permute-start | bytes 221192 | tf_op jit(solution)/shard_map/ppermute | solution.py:627
  19.8 45.1 %collective-permute-start.2 = (f32[6,24,128]{2,1,0:T(8,128)}, f32[6,24,128]{2,1,0:T(8,128)S(1)}, u32[]{:S(2)}, u32[]{:S(2)}) collective-permute-start(f32[6,24,128]{2,1,0:T(8,128)} %get-tuple-element.29), channel_id=1, source_target_pairs={{0,1},{2,3},{4,5},{6,7},{1,0},{3,2},{5,4},{7,6},{8,9},{10,11},{12,... | collective-permute-start | bytes 221192 | tf_op jit(solution)/shard_map/ppermute | solution.py:627
  22.9 42.0 %collective-permute-start = (f32[11,2,24,128]{3,2,1,0:T(8,128)S(1)}, f32[11,2,24,128]{3,2,1,0:T(8,128)S(1)}, u32[]{:S(2)}, u32[]{:S(2)}) collective-permute-start(f32[11,2,24,128]{3,2,1,0:T(8,128)S(1)} %get-tuple-element.26), channel_id=1, source_target_pairs={{0,8},{16,24},{32,40},{48,56},{64,72},{80,88},{96,104},{112,120},{... | collective-permute-start | bytes 811016 | tf_op jit(solution)/shard_map/ppermute | solution.py:627
  24.4 40.5 %collective-permute-start.1 = (f32[11,2,24,128]{3,2,1,0:T(8,128)S(1)}, f32[11,2,24,128]{3,2,1,0:T(8,128)S(1)}, u32[]{:S(2)}, u32[]{:S(2)}) collective-permute-start(f32[11,2,24,128]{3,2,1,0:T(8,128)S(1)} %get-tuple-element.27), channel_id=1, source_target_pairs={{8,16},{24,32},{40,48},{56,64},{72,80},{88,96},{104,112},{16,8},{3... | collective-permute-start | bytes 811016 | tf_op jit(solution)/shard_map/ppermute | solution.py:627
  28.3 4.5 %copy-start.10 = (f32[23]{0:T(128)S(1)}, f32[23]{0:T(128)}, u32[]{:S(2)}) copy-start(f32[23]{0:T(128)} %param.20) | copy-start | bytes 280
  31.5 1.3 %copy-start = (f32[10,16,24,128]{3,2,1,0:T(8,128)}, f32[10,16,24,128]{3,2,1,0:T(8,128)S(1)}, u32[]{:S(2)}) copy-start(f32[10,16,24,128]{3,2,1,0:T(8,128)S(1)} %first_divergence.1.div) | copy-start | bytes 5898244
  49.7 15.4 %copy-start.9 = (f32[24]{0:T(128)S(1)}, f32[24]{0:T(128)}, u32[]{:S(2)}) copy-start(f32[24]{0:T(128)} %param.21) | copy-start | bytes 292
  49.7 15.4 %copy-start.1 = (f32[10,16,24,128]{3,2,1,0:T(8,128)S(1)}, f32[10,16,24,128]{3,2,1,0:T(8,128)}, u32[]{:S(2)}) copy-start(f32[10,16,24,128]{3,2,1,0:T(8,128)} %copy-done) | copy-start | bytes 5898244
  49.7 15.4 %copy-start.7 = (f32[10,16,128]{2,1,0:T(8,128)S(1)}, f32[10,16,128]{2,1,0:T(8,128)}, u32[]{:S(2)}) copy-start(f32[10,16,128]{2,1,0:T(8,128)} %base_volume.1) | copy-start | bytes 245764
  49.7 15.4 %copy-start.8 = (f32[9,16,128]{2,1,0:T(8,128)S(1)}, f32[9,16,128]{2,1,0:T(8,128)}, u32[]{:S(2)}) copy-start(f32[9,16,128]{2,1,0:T(8,128)} %diffusivity.1) | copy-start | bytes 221188
  69.5 7.9 %collective-permute-start.4 = (f32[10,2,24,128]{3,2,1,0:T(8,128)S(1)}, f32[10,2,24,128]{3,2,1,0:T(8,128)S(1)}, u32[]{:S(2)}, u32[]{:S(2)}) collective-permute-start(f32[10,2,24,128]{3,2,1,0:T(8,128)S(1)} %get-tuple-element.31), channel_id=1, source_target_pairs={{0,8},{16,24},{32,40},{48,56},{64,72},{80,88},{96,104},{112,120},{... | collective-permute-start | bytes 737288 | tf_op jit(solution)/shard_map/ppermute | solution.py:627
  70.5 10.7 %collective-permute-start.5 = (f32[10,2,24,128]{3,2,1,0:T(8,128)S(1)}, f32[10,2,24,128]{3,2,1,0:T(8,128)S(1)}, u32[]{:S(2)}, u32[]{:S(2)}) collective-permute-start(f32[10,2,24,128]{3,2,1,0:T(8,128)S(1)} %get-tuple-element.32), channel_id=1, source_target_pairs={{8,16},{24,32},{40,48},{56,64},{72,80},{88,96},{104,112},{16,8},{3... | collective-permute-start | bytes 737288 | tf_op jit(solution)/shard_map/ppermute | solution.py:627
  73.7 2.8 %collective-permute-start.7 = (f32[5,24,128]{2,1,0:T(8,128)S(1)}, f32[5,24,128]{2,1,0:T(8,128)S(1)}, u32[]{:S(2)}, u32[]{:S(2)}) collective-permute-start(f32[5,24,128]{2,1,0:T(8,128)S(1)} %get-tuple-element.34), channel_id=1, source_target_pairs={{1,2},{3,4},{5,6},{2,1},{4,3},{6,5},{9,10},{11,12},{13,14},{10,9},... | collective-permute-start | bytes 184328 | tf_op jit(solution)/shard_map/ppermute | solution.py:627
  74.4 3.0 %collective-permute-start.6 = (f32[5,24,128]{2,1,0:T(8,128)S(1)}, f32[5,24,128]{2,1,0:T(8,128)S(1)}, u32[]{:S(2)}, u32[]{:S(2)}) collective-permute-start(f32[5,24,128]{2,1,0:T(8,128)S(1)} %get-tuple-element.34), channel_id=1, source_target_pairs={{0,1},{2,3},{4,5},{6,7},{1,0},{3,2},{5,4},{7,6},{8,9},{10,11},{12,... | collective-permute-start | bytes 184328 | tf_op jit(solution)/shard_map/ppermute | solution.py:627
  88.7 9.9 %collective-permute-start.8 = (f32[10,2,24,128]{3,2,1,0:T(8,128)S(1)}, f32[10,2,24,128]{3,2,1,0:T(8,128)S(1)}, u32[]{:S(2)}, u32[]{:S(2)}) collective-permute-start(f32[10,2,24,128]{3,2,1,0:T(8,128)S(1)} %get-tuple-element.37), channel_id=1, source_target_pairs={{0,8},{16,24},{32,40},{48,56},{64,72},{80,88},{96,104},{112,120},{... | collective-permute-start | bytes 737288 | tf_op jit(solution)/shard_map/ppermute | solution.py:627
  91.1 12.5 %collective-permute-start.9 = (f32[10,2,24,128]{3,2,1,0:T(8,128)S(1)}, f32[10,2,24,128]{3,2,1,0:T(8,128)S(1)}, u32[]{:S(2)}, u32[]{:S(2)}) collective-permute-start(f32[10,2,24,128]{3,2,1,0:T(8,128)S(1)} %get-tuple-element.38), channel_id=1, source_target_pairs={{8,16},{24,32},{40,48},{56,64},{72,80},{88,96},{104,112},{16,8},{3... | collective-permute-start | bytes 737288 | tf_op jit(solution)/shard_map/ppermute | solution.py:627
  93.0 4.7 %collective-permute-start.11 = (f32[5,24,128]{2,1,0:T(8,128)S(1)}, f32[5,24,128]{2,1,0:T(8,128)S(1)}, u32[]{:S(2)}, u32[]{:S(2)}) collective-permute-start(f32[5,24,128]{2,1,0:T(8,128)S(1)} %get-tuple-element.40), channel_id=1, source_target_pairs={{1,2},{3,4},{5,6},{2,1},{4,3},{6,5},{9,10},{11,12},{13,14},{10,9},... | collective-permute-start | bytes 184328 | tf_op jit(solution)/shard_map/ppermute | solution.py:627
  93.7 4.9 %collective-permute-start.10 = (f32[5,24,128]{2,1,0:T(8,128)S(1)}, f32[5,24,128]{2,1,0:T(8,128)S(1)}, u32[]{:S(2)}, u32[]{:S(2)}) collective-permute-start(f32[5,24,128]{2,1,0:T(8,128)S(1)} %get-tuple-element.40), channel_id=1, source_target_pairs={{0,1},{2,3},{4,5},{6,7},{1,0},{3,2},{5,4},{7,6},{8,9},{10,11},{12,... | collective-permute-start | bytes 184328 | tf_op jit(solution)/shard_map/ppermute | solution.py:627

commit v4 on v3

--- a/solution.py
+++ b/solution.py
@@ -326,11 +326,13 @@
     layers, rows = state.shape[0], state.shape[1]
     emit_swaps(place, state, swap_a, swap_b)
 
-    def layer(l, carry):
-        edges[l] = pack_layer([state[l, i] for i in range(rows)])
+    def some(t, carry):
+        for l in range(5):
+            l = t * 5 + l
+            edges[l] = pack_layer([state[l, i] for i in range(rows)])
         return carry
 
-    lax.fori_loop(0, layers, layer, 0)
+    lax.fori_loop(0, layers // 5, some, 0)
     emit_sent(edges, sent, False)
 
 
@@ -570,26 +572,40 @@
     edge = at_edges(state.shape[2:])
 
     def layer(l, carry):
-        c = [state[l, i] for i in range(rows)]
-        fix = [roll(fixes[l], 124 - 8 * i) for i in range(rows)]
-        parts = y_divergence(c, [qy[l, i : i + 1, :] for i in range(rows)])
-        parts = [jnp.where(edge, f, p) for f, p in zip(fix, parts)]
         flow = x_flows(qx, west_flow(place, (flow_a, flow_b), layers, l), l)
         get = x_rows(state, place, (received_a, received_b), l, rows)
+        rolled = [(roll(state[l, i], 1), roll(state[l, i], -1)) for i in range(rows)]
         faces = x_faces(get, flow, -1, rows - 1)
+        x_part = [faces[i + 1] - faces[i] for i in range(rows)]
+        shifted = []
         for i in range(rows):
-            star[l, i] = explicit_value(
+            c, (before, after) = (state[l, i], rolled[i])
+            slope = 0.5 * half_minmod(c - before, after - c)
+            shifted.append((c + slope, roll(c - slope, -1)))
+        base = [
+            explicit_value(
                 state[l, i],
-                parts[i] + (faces[i + 1] - faces[i]),
+                x_part[i],
                 rates[...],
                 rates_before[...],
                 inflow[...],
                 coef[4, l, i : i + 1, :],
                 coef[3, l, i : i + 1, :],
             )
+            for i in range(rows)
+        ]
+        fluxes = []
+        for i in range(rows):
+            q = qy[l, i : i + 1, :]
+            flux = jnp.maximum(q, 0.0) * shifted[i][0] + jnp.minimum(q, 0.0) * shifted[i][1]
+            fluxes.append((flux, roll(flux, 1), roll(fixes[l], 124 - 8 * i)))
+        for i in range(rows):
+            flux, before, fix = fluxes[i]
+            y_part = jnp.where(edge, fix, flux - before)
+            star[l, i] = base[i] - coef[3, l, i : i + 1, :] * y_part
         return carry
 
-    lax.fori_loop(0, layers, layer, 0)
+    lax.fori_loop(0, layers, layer, 0, unroll=5)
 
     def emit(l, i, value):
         if final:

time: 113 us -> 109 us (0.965)
  Pallas kernels: 45.9 us -> 41.9 us
    pallas_call x2, Pallas kernels: 16.6 us -> 13.1 us  [later_step(): pl.pallas_call(functools.partial(later_step_kernel, final), in_specs=[SME...]
  transfers between devices with their start and end apart: 13 -> 13, of which waited for: 5 -> 5; matrix products, arithmetic and copies ran while one was open for 0% -> 0% of each run, Pallas kernels for 19% -> 20%
where the time goes in v4:
time: 109 us
  Pallas kernels  41.9 us (38%)
  starting transfers between devices  35.9 us (33%)
  waiting for transfers between devices  27.4 us (25%)
  local copies, waits for them, and re-layouts  3.05 us (3%)
    ppermute x12, starting transfers between devices, swap(): return lax.ppermute(values, axis, pairs + [(j, i) for i, j in pairs])  25.2 us
    all_to_all x1, waiting for transfers between devices, local(): lax.all_to_all(slots.reshape(owners, 1, -1), ('gx', 'gy'), split_axis=0,...  16.7 us
    pallas_call x1, Pallas kernels, totals(): pl.pallas_call(totals_kernel, in_specs=[VMEM], out_specs=VMEM, out_shape=...  15.1 us
    pallas_call x2, Pallas kernels, later_step(): pl.pallas_call(functools.partial(later_step_kernel, final), in_specs=[SME...  13.1 us
    all_to_all x1, starting transfers between devices, local(): lax.all_to_all(slots.reshape(owners, 1, -1), ('gx', 'gy'), split_axis=0,...  10.7 us
    ppermute x12, waiting for transfers between devices, swap(): return lax.ppermute(values, axis, pairs + [(j, i) for i, j in pairs])  10.6 us
    pallas_call x1, Pallas kernels, first_step(): pl.pallas_call(first_step_kernel, in_specs=[SMEM] + [VMEM] * 14, out_spec...  3.76 us
    pallas_call x1, Pallas kernels, pack_slots(): pl.pallas_call(pack_kernel, grid=(groups // step,), in_specs=[pl.BlockSpe...  3.5 us
  transfers between devices with their start and end apart: 13, of which 5 were waited for; matrix products, arithmetic and copies ran while one was open for 0% of the time, Pallas kernels for 20%

profile of v4, /device:TPU:16, one launch (start us, length us, event | category | flops | bytes accessed | tf_op | source)
XLA Modules:
  0.0 108.6 jit_solution(13805771723102230174)
XLA Ops:
  0.0 3.5 %pack_slots.1 = f32[5376,128]{1,0:T(8,128)} custom-call(f32[10,32768]{1,0:T(8,128)} %volume.1, f32[10,32768]{1,0:T(8,128)} %discharge.1, s32[256,128]{1,0:T(8,128)} %bitcast.13, s32[256,128]{1,0:T(8,128)} %bitcast.14), custom_call_target="tpu_custom_call" | custom-call | bytes 8000000 | tf_op jit(solution)/shard_map/pack_slots/pallas_call | solution.py:52
  3.5 10.7 %all-to-all-start = ((f32[128,1,5376]{2,1,0:T(1,128)}), f32[128,1,5376]{2,1,0:T(1,128)}, u32[]{:S(2)}, u32[]{:S(2)}) async-start(f32[128,1,5376]{2,1,0:T(1,128)} %bitcast.12), calls=%async_computation | async-start | bytes 5505024 | tf_op jit(solution)/shard_map/all_to_all | solution.py:671
  14.4 1.5 %copy-done.2 = f32[24,10,16,128]{3,2,1,0:T(8,128)S(1)} copy-done((f32[24,10,16,128]{3,2,1,0:T(8,128)S(1)}, f32[24,10,16,128]{3,2,1,0:T(8,128)}, u32[]{:S(2)}) %copy-start.2) | copy-done | bytes 1966104
  15.9 3.2 %start_state.1 = (f32[10,16,24,128]{3,2,1,0:T(8,128)S(1)}, f32[11,2,24,128]{3,2,1,0:T(8,128)S(1)}, f32[11,2,24,128]{3,2,1,0:T(8,128)S(1)}, f32[11,24,128]{2,1,0:...) custom-call(s32[4]{0:T(128)S(1)} %pad_add_fusion.place, ...), custom_call_target="tpu_custom_call" | custom-call | flops 1000000 | bytes 8000000 | tf_op jit(solution)/shard_map/start_state/pallas_call | solution.py:189
  19.8 3.1 %collective-permute-start.2 = (f32[6,24,128]{2,1,0:T(8,128)}, f32[6,24,128]{2,1,0:T(8,128)S(1)}, u32[]{:S(2)}, u32[]{:S(2)}) collective-permute-start(f32[6,24,128]{2,1,0:T(8,128)} %get-tuple-element.29), channel_id=1, source_target_pairs={{0,1},{2,3},{4,5},{6,7},{1,0},{3,2},{5,4},{7,6},{8,9},{10,11},{12,... | collective-permute-start | bytes 221192 | tf_op jit(solution)/shard_map/ppermute | solution.py:643
  22.9 1.5 %collective-permute-start = (f32[11,2,24,128]{3,2,1,0:T(8,128)S(1)}, f32[11,2,24,128]{3,2,1,0:T(8,128)S(1)}, u32[]{:S(2)}, u32[]{:S(2)}) collective-permute-start(f32[11,2,24,128]{3,2,1,0:T(8,128)S(1)} %get-tuple-element.26), channel_id=1, source_target_pairs={{0,8},{16,24},{32,40},{48,56},{64,72},{80,88},{96,104},{112,120},{... | collective-permute-start | bytes 811016 | tf_op jit(solution)/shard_map/ppermute | solution.py:643
  24.4 3.9 %collective-permute-start.1 = (f32[11,2,24,128]{3,2,1,0:T(8,128)S(1)}, f32[11,2,24,128]{3,2,1,0:T(8,128)S(1)}, u32[]{:S(2)}, u32[]{:S(2)}) collective-permute-start(f32[11,2,24,128]{3,2,1,0:T(8,128)S(1)} %get-tuple-element.27), channel_id=1, source_target_pairs={{8,16},{24,32},{40,48},{56,64},{72,80},{88,96},{104,112},{16,8},{3... | collective-permute-start | bytes 811016 | tf_op jit(solution)/shard_map/ppermute | solution.py:643
  28.3 3.2 %first_divergence.1.div = f32[10,16,24,128]{3,2,1,0:T(8,128)S(1)} custom-call(f32[10,16,24,128]{3,2,1,0:T(8,128)S(1)} %get-tuple-element.23.state, f32[10,16,128]{2,1,0:T(8,128)S(1)} %get-tuple-element.24.qx, f32[10,16,128]{2,1,0:T(8,128)S(1)} %get-tuple-element.25.qy), custom_call_target="tpu_custom_call" | custom-call | flops 20000000 | bytes 10000000 | tf_op jit(solution)/shard_map/first_divergence/pallas_call | solution.py:277
  31.5 1.3 %copy-done = f32[10,16,24,128]{3,2,1,0:T(8,128)} copy-done((f32[10,16,24,128]{3,2,1,0:T(8,128)}, f32[10,16,24,128]{3,2,1,0:T(8,128)S(1)}, u32[]{:S(2)}) %copy-start) | copy-done | bytes 1966104
  33.0 16.7 %all-to-all-done = f32[128,1,5376]{2,1,0:T(1,128)} async-done(((f32[128,1,5376]{2,1,0:T(1,128)}), f32[128,1,5376]{2,1,0:T(1,128)}, u32[]{:S(2)}, u32[]{:S(2)}) %all-to-all-start) | async-done | bytes 2752544 | tf_op jit(solution)/shard_map/all_to_all | solution.py:671
  49.7 15.1 %aggregate.1.total = f32[320,256]{1,0:T(8,128)S(1)} custom-call(f32[5376,128]{1,0:T(8,128)} %bitcast.7.slots), custom_call_target="tpu_custom_call" | custom-call | flops 12000000000 | bytes 4000000 | tf_op jit(solution)/shard_map/aggregate/pallas_call | solution.py:396
  65.1 3.8 %first_step.1 = (f32[10,16,24,128]{3,2,1,0:T(8,128)S(1)}, f32[10,2,24,128]{3,2,1,0:T(8,128)S(1)}, f32[10,2,24,128]{3,2,1,0:T(8,128)S(1)}, f32[10,24,128]{2,1,0:T...) custom-call(s32[4]{0:T(128)S(1)} %pad_add_fusion.place, f32[320,256]{1,0:T(8,128)S(1)} %aggregate.1.total, ...), custom_call_target="tpu_custom_call" | custom-call | flops 20000000 | bytes 10000000 | tf_op jit(solution)/shard_map/first_step/pallas_call | solution.py:525
  68.9 1.0 collective-permute-start.4
  69.9 3.2 %collective-permute-start.5 = (f32[10,2,24,128]{3,2,1,0:T(8,128)S(1)}, f32[10,2,24,128]{3,2,1,0:T(8,128)S(1)}, u32[]{:S(2)}, u32[]{:S(2)}) collective-permute-start(f32[10,2,24,128]{3,2,1,0:T(8,128)S(1)} %get-tuple-element.32), channel_id=1, source_target_pairs={{8,16},{24,32},{40,48},{56,64},{72,80},{88,96},{104,112},{16,8},{3... | collective-permute-start | bytes 737288 | tf_op jit(solution)/shard_map/ppermute | solution.py:643
  73.8 2.1 %collective-permute-start.6 = (f32[5,24,128]{2,1,0:T(8,128)S(1)}, f32[5,24,128]{2,1,0:T(8,128)S(1)}, u32[]{:S(2)}, u32[]{:S(2)}) collective-permute-start(f32[5,24,128]{2,1,0:T(8,128)S(1)} %get-tuple-element.34), channel_id=1, source_target_pairs={{0,1},{2,3},{4,5},{6,7},{1,0},{3,2},{5,4},{7,6},{8,9},{10,11},{12,... | collective-permute-start | bytes 184328 | tf_op jit(solution)/shard_map/ppermute | solution.py:643
  76.0 0.9 collective-permute-done.6.edges_a
  76.9 3.8 %collective-permute-done.5.received_b = f32[10,2,24,128]{3,2,1,0:T(8,128)S(1)} collective-permute-done((f32[10,2,24,128]{3,2,1,0:T(8,128)S(1)}, f32[10,2,24,128]{3,2,1,0:T(8,128)S(1)}, u32[]{:S(2)}, u32[]{:S(2)}) %collective-permute-start.5) | collective-permute-done | bytes 245792 | tf_op jit(solution)/shard_map/ppermute | solution.py:643
  80.7 5.5 %middle_step.1 = (f32[10,16,24,128]{3,2,1,0:T(8,128)S(1)}, f32[10,2,24,128]{3,2,1,0:T(8,128)S(1)}, f32[10,2,24,128]{3,2,1,0:T(8,128)S(1)}, f32[10,24,128]{2,1,0:T(8,128)S(1)}, f32[5,24,128]{2,1,0:T(8,128)S(1)}) custom-call(s32[4]{0:T(128)S(1)} %pad_add_fusion.place, f32[10,16,24,128]{3,2,1,0:T(8,128)S(1)} %get-tuple-element.30.state, ...), custom_call_target="tpu_custom_call" | custom-call | flops 30000000 | bytes 10000000 | tf_op jit(solution)/shard_map/middle_step/pallas_call | solution.py:629
  86.1 2.4 %collective-permute-start.8 = (f32[10,2,24,128]{3,2,1,0:T(8,128)S(1)}, f32[10,2,24,128]{3,2,1,0:T(8,128)S(1)}, u32[]{:S(2)}, u32[]{:S(2)}) collective-permute-start(f32[10,2,24,128]{3,2,1,0:T(8,128)S(1)} %get-tuple-element.37), channel_id=1, source_target_pairs={{0,8},{16,24},{32,40},{48,56},{64,72},{80,88},{96,104},{112,120},{... | collective-permute-start | bytes 737288 | tf_op jit(solution)/shard_map/ppermute | solution.py:643
  88.5 1.9 %collective-permute-start.9 = (f32[10,2,24,128]{3,2,1,0:T(8,128)S(1)}, f32[10,2,24,128]{3,2,1,0:T(8,128)S(1)}, u32[]{:S(2)}, u32[]{:S(2)}) collective-permute-start(f32[10,2,24,128]{3,2,1,0:T(8,128)S(1)} %get-tuple-element.38), channel_id=1, source_target_pairs={{8,16},{24,32},{40,48},{56,64},{72,80},{88,96},{104,112},{16,8},{3... | collective-permute-start | bytes 737288 | tf_op jit(solution)/shard_map/ppermute | solution.py:643
  91.1 4.0 %collective-permute-start.10 = (f32[5,24,128]{2,1,0:T(8,128)S(1)}, f32[5,24,128]{2,1,0:T(8,128)S(1)}, u32[]{:S(2)}, u32[]{:S(2)}) collective-permute-start(f32[5,24,128]{2,1,0:T(8,128)S(1)} %get-tuple-element.40), channel_id=1, source_target_pairs={{0,1},{2,3},{4,5},{6,7},{1,0},{3,2},{5,4},{7,6},{8,9},{10,11},{12,... | collective-permute-start | bytes 184328 | tf_op jit(solution)/shard_map/ppermute | solution.py:643
  95.1 0.9 collective-permute-done.10.edges_a
  96.0 5.0 %collective-permute-done.9.received_b = f32[10,2,24,128]{3,2,1,0:T(8,128)S(1)} collective-permute-done((f32[10,2,24,128]{3,2,1,0:T(8,128)S(1)}, f32[10,2,24,128]{3,2,1,0:T(8,128)S(1)}, u32[]{:S(2)}, u32[]{:S(2)}) %collective-permute-start.9) | collective-permute-done | bytes 245792 | tf_op jit(solution)/shard_map/ppermute | solution.py:643
  101.0 7.6 %last_step.1 = f32[3840,128]{1,0:T(8,128)} custom-call(s32[4]{0:T(128)S(1)} %pad_add_fusion.place, f32[10,16,24,128]{3,2,1,0:T(8,128)S(1)} %get-tuple-element.36.state, f32[10,2,24,128]{3,2,1,0:T(8,128)S(1)} %collective-permute-done.8.received_a, f32[10,2,24,128]{3,2,1,0:T(8,128)S(1)} %collective-permute-done.9.received_b, ...), custom_call_target="tpu_custom_call" | custom-call | flops 30000000 | bytes 10000000 | tf_op jit(solution)/shard_map/last_step/pallas_call | solution.py:629
  (37 shorter events, 2.5 us)
Async XLA Ops:
  3.5 10.9 %copy-start.3 = (f32[10,16,128]{2,1,0:T(8,128)S(1)}, f32[10,16,128]{2,1,0:T(8,128)}, u32[]{:S(2)}) copy-start(f32[10,16,128]{2,1,0:T(8,128)} %flow_x.1) | copy-start | bytes 245764
  3.5 10.9 %copy-start.4 = (f32[10,16,128]{2,1,0:T(8,128)S(1)}, f32[10,16,128]{2,1,0:T(8,128)}, u32[]{:S(2)}) copy-start(f32[10,16,128]{2,1,0:T(8,128)} %flow_y.1) | copy-start | bytes 245764
  3.5 10.9 %copy-start.5 = (s32[10,16,128]{2,1,0:T(8,128)S(1)}, s32[10,16,128]{2,1,0:T(8,128)}, u32[]{:S(2)}) copy-start(s32[10,16,128]{2,1,0:T(8,128)} %wet_x.1) | copy-start | bytes 245764
  3.5 10.9 %copy-start.6 = (s32[10,16,128]{2,1,0:T(8,128)S(1)}, s32[10,16,128]{2,1,0:T(8,128)}, u32[]{:S(2)}) copy-start(s32[10,16,128]{2,1,0:T(8,128)} %wet_y.1) | copy-start | bytes 245764
  3.5 46.2 %all-to-all-start = ((f32[128,1,5376]{2,1,0:T(1,128)}), f32[128,1,5376]{2,1,0:T(1,128)}, u32[]{:S(2)}, u32[]{:S(2)}) async-start(f32[128,1,5376]{2,1,0:T(1,128)} %bitcast.12), calls=%async_computation | async-start | bytes 5505024 | tf_op jit(solution)/shard_map/all_to_all | solution.py:671
  14.4 1.5 %copy-start.2 = (f32[24,10,16,128]{3,2,1,0:T(8,128)S(1)}, f32[24,10,16,128]{3,2,1,0:T(8,128)}, u32[]{:S(2)}) copy-start(f32[24,10,16,128]{3,2,1,0:T(8,128)} %param.13) | copy-start | bytes 5898244
  19.1 45.8 %collective-permute-start.3 = (f32[6,24,128]{2,1,0:T(8,128)}, f32[6,24,128]{2,1,0:T(8,128)S(1)}, u32[]{:S(2)}, u32[]{:S(2)}) collective-permute-start(f32[6,24,128]{2,1,0:T(8,128)} %get-tuple-element.29), channel_id=1, source_target_pairs={{1,2},{3,4},{5,6},{2,1},{4,3},{6,5},{9,10},{11,12},{13,14},{10,9},... | collective-permute-start | bytes 221192 | tf_op jit(solution)/shard_map/ppermute | solution.py:643
  19.8 45.1 %collective-permute-start.2 = (f32[6,24,128]{2,1,0:T(8,128)}, f32[6,24,128]{2,1,0:T(8,128)S(1)}, u32[]{:S(2)}, u32[]{:S(2)}) collective-permute-start(f32[6,24,128]{2,1,0:T(8,128)} %get-tuple-element.29), channel_id=1, source_target_pairs={{0,1},{2,3},{4,5},{6,7},{1,0},{3,2},{5,4},{7,6},{8,9},{10,11},{12,... | collective-permute-start | bytes 221192 | tf_op jit(solution)/shard_map/ppermute | solution.py:643
  22.9 42.0 %collective-permute-start = (f32[11,2,24,128]{3,2,1,0:T(8,128)S(1)}, f32[11,2,24,128]{3,2,1,0:T(8,128)S(1)}, u32[]{:S(2)}, u32[]{:S(2)}) collective-permute-start(f32[11,2,24,128]{3,2,1,0:T(8,128)S(1)} %get-tuple-element.26), channel_id=1, source_target_pairs={{0,8},{16,24},{32,40},{48,56},{64,72},{80,88},{96,104},{112,120},{... | collective-permute-start | bytes 811016 | tf_op jit(solution)/shard_map/ppermute | solution.py:643
  24.4 40.5 %collective-permute-start.1 = (f32[11,2,24,128]{3,2,1,0:T(8,128)S(1)}, f32[11,2,24,128]{3,2,1,0:T(8,128)S(1)}, u32[]{:S(2)}, u32[]{:S(2)}) collective-permute-start(f32[11,2,24,128]{3,2,1,0:T(8,128)S(1)} %get-tuple-element.27), channel_id=1, source_target_pairs={{8,16},{24,32},{40,48},{56,64},{72,80},{88,96},{104,112},{16,8},{3... | collective-permute-start | bytes 811016 | tf_op jit(solution)/shard_map/ppermute | solution.py:643
  28.3 4.5 %copy-start.10 = (f32[23]{0:T(128)S(1)}, f32[23]{0:T(128)}, u32[]{:S(2)}) copy-start(f32[23]{0:T(128)} %param.20) | copy-start | bytes 280
  31.5 1.3 %copy-start = (f32[10,16,24,128]{3,2,1,0:T(8,128)}, f32[10,16,24,128]{3,2,1,0:T(8,128)S(1)}, u32[]{:S(2)}) copy-start(f32[10,16,24,128]{3,2,1,0:T(8,128)S(1)} %first_divergence.1.div) | copy-start | bytes 5898244
  49.7 15.4 %copy-start.9 = (f32[24]{0:T(128)S(1)}, f32[24]{0:T(128)}, u32[]{:S(2)}) copy-start(f32[24]{0:T(128)} %param.21) | copy-start | bytes 292
  49.7 15.4 %copy-start.1 = (f32[10,16,24,128]{3,2,1,0:T(8,128)S(1)}, f32[10,16,24,128]{3,2,1,0:T(8,128)}, u32[]{:S(2)}) copy-start(f32[10,16,24,128]{3,2,1,0:T(8,128)} %copy-done) | copy-start | bytes 5898244
  49.7 15.4 %copy-start.7 = (f32[10,16,128]{2,1,0:T(8,128)S(1)}, f32[10,16,128]{2,1,0:T(8,128)}, u32[]{:S(2)}) copy-start(f32[10,16,128]{2,1,0:T(8,128)} %base_volume.1) | copy-start | bytes 245764
  49.7 15.4 %copy-start.8 = (f32[9,16,128]{2,1,0:T(8,128)S(1)}, f32[9,16,128]{2,1,0:T(8,128)}, u32[]{:S(2)}) copy-start(f32[9,16,128]{2,1,0:T(8,128)} %diffusivity.1) | copy-start | bytes 221188
  68.9 7.9 %collective-permute-start.4 = (f32[10,2,24,128]{3,2,1,0:T(8,128)S(1)}, f32[10,2,24,128]{3,2,1,0:T(8,128)S(1)}, u32[]{:S(2)}, u32[]{:S(2)}) collective-permute-start(f32[10,2,24,128]{3,2,1,0:T(8,128)S(1)} %get-tuple-element.31), channel_id=1, source_target_pairs={{0,8},{16,24},{32,40},{48,56},{64,72},{80,88},{96,104},{112,120},{... | collective-permute-start | bytes 737288 | tf_op jit(solution)/shard_map/ppermute | solution.py:643
  69.9 10.7 %collective-permute-start.5 = (f32[10,2,24,128]{3,2,1,0:T(8,128)S(1)}, f32[10,2,24,128]{3,2,1,0:T(8,128)S(1)}, u32[]{:S(2)}, u32[]{:S(2)}) collective-permute-start(f32[10,2,24,128]{3,2,1,0:T(8,128)S(1)} %get-tuple-element.32), channel_id=1, source_target_pairs={{8,16},{24,32},{40,48},{56,64},{72,80},{88,96},{104,112},{16,8},{3... | collective-permute-start | bytes 737288 | tf_op jit(solution)/shard_map/ppermute | solution.py:643
  73.1 2.8 %collective-permute-start.7 = (f32[5,24,128]{2,1,0:T(8,128)S(1)}, f32[5,24,128]{2,1,0:T(8,128)S(1)}, u32[]{:S(2)}, u32[]{:S(2)}) collective-permute-start(f32[5,24,128]{2,1,0:T(8,128)S(1)} %get-tuple-element.34), channel_id=1, source_target_pairs={{1,2},{3,4},{5,6},{2,1},{4,3},{6,5},{9,10},{11,12},{13,14},{10,9},... | collective-permute-start | bytes 184328 | tf_op jit(solution)/shard_map/ppermute | solution.py:643
  73.8 3.0 %collective-permute-start.6 = (f32[5,24,128]{2,1,0:T(8,128)S(1)}, f32[5,24,128]{2,1,0:T(8,128)S(1)}, u32[]{:S(2)}, u32[]{:S(2)}) collective-permute-start(f32[5,24,128]{2,1,0:T(8,128)S(1)} %get-tuple-element.34), channel_id=1, source_target_pairs={{0,1},{2,3},{4,5},{6,7},{1,0},{3,2},{5,4},{7,6},{8,9},{10,11},{12,... | collective-permute-start | bytes 184328 | tf_op jit(solution)/shard_map/ppermute | solution.py:643
  86.1 9.9 %collective-permute-start.8 = (f32[10,2,24,128]{3,2,1,0:T(8,128)S(1)}, f32[10,2,24,128]{3,2,1,0:T(8,128)S(1)}, u32[]{:S(2)}, u32[]{:S(2)}) collective-permute-start(f32[10,2,24,128]{3,2,1,0:T(8,128)S(1)} %get-tuple-element.37), channel_id=1, source_target_pairs={{0,8},{16,24},{32,40},{48,56},{64,72},{80,88},{96,104},{112,120},{... | collective-permute-start | bytes 737288 | tf_op jit(solution)/shard_map/ppermute | solution.py:643
  88.5 12.5 %collective-permute-start.9 = (f32[10,2,24,128]{3,2,1,0:T(8,128)S(1)}, f32[10,2,24,128]{3,2,1,0:T(8,128)S(1)}, u32[]{:S(2)}, u32[]{:S(2)}) collective-permute-start(f32[10,2,24,128]{3,2,1,0:T(8,128)S(1)} %get-tuple-element.38), channel_id=1, source_target_pairs={{8,16},{24,32},{40,48},{56,64},{72,80},{88,96},{104,112},{16,8},{3... | collective-permute-start | bytes 737288 | tf_op jit(solution)/shard_map/ppermute | solution.py:643
  90.4 4.7 %collective-permute-start.11 = (f32[5,24,128]{2,1,0:T(8,128)S(1)}, f32[5,24,128]{2,1,0:T(8,128)S(1)}, u32[]{:S(2)}, u32[]{:S(2)}) collective-permute-start(f32[5,24,128]{2,1,0:T(8,128)S(1)} %get-tuple-element.40), channel_id=1, source_target_pairs={{1,2},{3,4},{5,6},{2,1},{4,3},{6,5},{9,10},{11,12},{13,14},{10,9},... | collective-permute-start | bytes 184328 | tf_op jit(solution)/shard_map/ppermute | solution.py:643
  91.1 4.9 %collective-permute-start.10 = (f32[5,24,128]{2,1,0:T(8,128)S(1)}, f32[5,24,128]{2,1,0:T(8,128)S(1)}, u32[]{:S(2)}, u32[]{:S(2)}) collective-permute-start(f32[5,24,128]{2,1,0:T(8,128)S(1)} %get-tuple-element.40), channel_id=1, source_target_pairs={{0,1},{2,3},{4,5},{6,7},{1,0},{3,2},{5,4},{7,6},{8,9},{10,11},{12,... | collective-permute-start | bytes 184328 | tf_op jit(solution)/shard_map/ppermute | solution.py:643

commit v5 on v4

--- a/solution.py
+++ b/solution.py
@@ -336,27 +336,33 @@
     emit_sent(edges, sent, False)
 
 
-def spread_slots(slots, chunk, terms, spread, hot):
-    rows = 21
-    halves = spread.shape[1] // 128
-    sub8 = lax.broadcasted_iota(jnp.int32, (8, 128), 0)
-    column = lax.broadcasted_iota(jnp.int32, (128, 128), 0).astype(F32).astype(BF16)
-    base = pl.multiple_of(chunk * (halves * rows), 8)
-    values = slots[pl.ds(base, halves * rows), :]
+ROWS = 21
+PIECES = 2
+
+
+def split_values(slots, chunk, halves, terms):
+    base = pl.multiple_of(chunk * (halves * ROWS), 8)
+    values = slots[pl.ds(base, halves * ROWS), :]
     high = values.astype(BF16).astype(F32)
     terms[0] = high
     terms[1] = values - high
-    for j in range(halves):
+
+
+def spread_slots(terms, spread, hot, halves):
+    sub8 = lax.broadcasted_iota(jnp.int32, (8, 128), 0)
+    column = lax.broadcasted_iota(jnp.int32, (128, 128), 0).astype(F32).astype(BF16)
+    zero = jnp.zeros((16, 128), BF16)
+    for j in halves:
         to = slice(j * 128, (j + 1) * 128)
 
         def term(which, ch):
-            at = j * rows + ch
+            at = j * ROWS + ch
             return terms[which, at : at + 1, :]
 
-        label = (term(0, 20) + term(1, 20)).astype(jnp.int32)
+        label = (term(0, ROWS - 1) + term(1, ROWS - 1)).astype(jnp.int32)
         mask = jnp.where(jnp.broadcast_to((label >> 7) & 7, (8, 128)) == sub8, 1.0, 0.0)
         mask = jnp.concatenate([mask, mask], axis=0).astype(BF16)
-        for ch in range(20):
+        for ch in range(ROWS - 1):
             both = [jnp.broadcast_to(term(which, ch), (8, 128)) for which in range(2)]
             both = jnp.concatenate(both, axis=0).astype(BF16)
             spread[ch * 16 : (ch + 1) * 16, to] = both * mask
@@ -366,7 +372,6 @@
             jnp.broadcast_to(jnp.where(half == h, 1.0, 0.0), (16, 128)).astype(BF16)
             for h in range(2)
         ]
-        zero = jnp.zeros((16, 128), BF16)
         for g in range(8):
             same = column[g * 16 : (g + 1) * 16] == place
             for h in range(2):
@@ -374,35 +379,51 @@
                 hot[at : at + 16, to] = jnp.where(same, hits[h], zero)
 
 
-def aggregate(slots, terms, spread, hot, total):
+def totals_kernel(slots, total, *scratch):
+    sets = (scratch[:3], scratch[3:])
+    halves = scratch[1].shape[1] // 128
+    chunks = slots.shape[0] // ROWS // halves
+    piece = halves // PIECES
     total[...] = jnp.zeros_like(total)
-
-    def chunk(i, carry):
-        spread_slots(slots, i, terms, spread, hot)
-        total[...] += lax.dot_general(
-            spread[...], hot[...], (((1,), (1,)), ((), ())), preferred_element_type=F32
-        )
+    split_values(slots, 0, halves, sets[0][0])
+    spread_slots(*sets[0], range(halves))
+
+    def pair(i, carry):
+        added = None
+        for now in range(2):
+            _, spread, hot = sets[now]
+            filled = sets[1 - now]
+            later = jnp.minimum(2 * i + 1 + now, chunks - 1)
+            split_values(slots, later, halves, filled[0])
+            for p in range(PIECES):
+                some = slice(p * piece * 128, (p + 1) * piece * 128)
+                product = lax.dot_general(
+                    spread[:, some],
+                    hot[:, some],
+                    (((1,), (1,)), ((), ())),
+                    preferred_element_type=F32,
+                )
+                added = product if added is None else added + product
+                spread_slots(*filled, range(p * piece, (p + 1) * piece))
+        total[...] += added
         return carry
 
-    lax.fori_loop(0, slots.shape[0] // terms.shape[1], chunk, 0)
-
-
-def totals_kernel(slots, total, terms, spread, hot):
-    aggregate(slots, terms, spread, hot, total)
+    lax.fori_loop(0, chunks // 2, pair, 0)
 
 
 def totals(slots):
-    depth = min(2048, slots.shape[0] // 21 * 128)
+    depth = min(2048, slots.shape[0] // ROWS * 64)
     return pl.pallas_call(
         totals_kernel,
         in_specs=[VMEM],
         out_specs=VMEM,
         out_shape=jax.ShapeDtypeStruct((320, 256), F32),
         scratch_shapes=[
-            pltpu.VMEM((2, depth // 128 * 21, 128), F32),
+            pltpu.VMEM((2, depth // 128 * ROWS, 128), F32),
             pltpu.VMEM((320, depth), BF16),
             pltpu.VMEM((256, depth), BF16),
-        ],
+        ]
+        * 2,
         compiler_params=pltpu.CompilerParams(vmem_limit_bytes=VMEM_BYTES),
         cost_estimate=pl.CostEstimate(
             flops=12 * 10**9, bytes_accessed=4 * 10**6, transcendentals=0

time: 109 us -> 108 us (level)
  transfers between devices with their start and end apart: 13 -> 13, of which waited for: 5 -> 5; matrix products, arithmetic and copies ran while one was open for 0% -> 0% of each run, Pallas kernels for 20% -> 19%
where the time goes in v5:
time: 108 us
  Pallas kernels  41.2 us (38%)
  starting transfers between devices  35.9 us (33%)
  waiting for transfers between devices  27.4 us (25%)
  local copies, waits for them, and re-layouts  3.05 us (3%)
    ppermute x12, starting transfers between devices, swap(): return lax.ppermute(values, axis, pairs + [(j, i) for i, j in pairs])  25.1 us
    all_to_all x1, waiting for transfers between devices, local(): lax.all_to_all(slots.reshape(owners, 1, -1), ('gx', 'gy'), split_axis=0,...  16.7 us
    pallas_call x1, Pallas kernels, totals(): pl.pallas_call(totals_kernel, in_specs=[VMEM], out_specs=VMEM, out_shape=...  14.5 us
    pallas_call x2, Pallas kernels, later_step(): pl.pallas_call(functools.partial(later_step_kernel, final), in_specs=[SME...  13.1 us
    all_to_all x1, starting transfers between devices, local(): lax.all_to_all(slots.reshape(owners, 1, -1), ('gx', 'gy'), split_axis=0,...  10.7 us
    ppermute x12, waiting for transfers between devices, swap(): return lax.ppermute(values, axis, pairs + [(j, i) for i, j in pairs])  10.6 us
    pallas_call x1, Pallas kernels, first_step(): pl.pallas_call(first_step_kernel, in_specs=[SMEM] + [VMEM] * 14, out_spec...  3.76 us
    pallas_call x1, Pallas kernels, pack_slots(): pl.pallas_call(pack_kernel, grid=(groups // step,), in_specs=[pl.BlockSpe...  3.5 us
  transfers between devices with their start and end apart: 13, of which 5 were waited for; matrix products, arithmetic and copies ran while one was open for 0% of the time, Pallas kernels for 19%

profile of v5, /device:TPU:16, one launch (start us, length us, event | category | flops | bytes accessed | tf_op | source)
XLA Modules:
  0.0 108.0 jit_solution(10382113551660939548)
XLA Ops:
  0.0 3.5 %pack_slots.1 = f32[5376,128]{1,0:T(8,128)} custom-call(f32[10,32768]{1,0:T(8,128)} %volume.1, f32[10,32768]{1,0:T(8,128)} %discharge.1, s32[256,128]{1,0:T(8,128)} %bitcast.13, s32[256,128]{1,0:T(8,128)} %bitcast.14), custom_call_target="tpu_custom_call" | custom-call | bytes 8000000 | tf_op jit(solution)/shard_map/pack_slots/pallas_call | solution.py:52
  3.5 10.7 %all-to-all-start = ((f32[128,1,5376]{2,1,0:T(1,128)}), f32[128,1,5376]{2,1,0:T(1,128)}, u32[]{:S(2)}, u32[]{:S(2)}) async-start(f32[128,1,5376]{2,1,0:T(1,128)} %bitcast.12), calls=%async_computation | async-start | bytes 5505024 | tf_op jit(solution)/shard_map/all_to_all | solution.py:692
  14.4 1.5 %copy-done.2 = f32[24,10,16,128]{3,2,1,0:T(8,128)S(1)} copy-done((f32[24,10,16,128]{3,2,1,0:T(8,128)S(1)}, f32[24,10,16,128]{3,2,1,0:T(8,128)}, u32[]{:S(2)}) %copy-start.2) | copy-done | bytes 1966104
  15.9 3.2 %start_state.1 = (f32[10,16,24,128]{3,2,1,0:T(8,128)S(1)}, f32[11,2,24,128]{3,2,1,0:T(8,128)S(1)}, f32[11,2,24,128]{3,2,1,0:T(8,128)S(1)}, f32[11,24,128]{2,1,0:...) custom-call(s32[4]{0:T(128)S(1)} %pad_add_fusion.place, ...), custom_call_target="tpu_custom_call" | custom-call | flops 1000000 | bytes 8000000 | tf_op jit(solution)/shard_map/start_state/pallas_call | solution.py:189
  19.8 3.1 %collective-permute-start.2 = (f32[6,24,128]{2,1,0:T(8,128)}, f32[6,24,128]{2,1,0:T(8,128)S(1)}, u32[]{:S(2)}, u32[]{:S(2)}) collective-permute-start(f32[6,24,128]{2,1,0:T(8,128)} %get-tuple-element.29), channel_id=1, source_target_pairs={{0,1},{2,3},{4,5},{6,7},{1,0},{3,2},{5,4},{7,6},{8,9},{10,11},{12,... | collective-permute-start | bytes 221192 | tf_op jit(solution)/shard_map/ppermute | solution.py:664
  22.9 1.5 %collective-permute-start = (f32[11,2,24,128]{3,2,1,0:T(8,128)S(1)}, f32[11,2,24,128]{3,2,1,0:T(8,128)S(1)}, u32[]{:S(2)}, u32[]{:S(2)}) collective-permute-start(f32[11,2,24,128]{3,2,1,0:T(8,128)S(1)} %get-tuple-element.26), channel_id=1, source_target_pairs={{0,8},{16,24},{32,40},{48,56},{64,72},{80,88},{96,104},{112,120},{... | collective-permute-start | bytes 811016 | tf_op jit(solution)/shard_map/ppermute | solution.py:664
  24.4 3.9 %collective-permute-start.1 = (f32[11,2,24,128]{3,2,1,0:T(8,128)S(1)}, f32[11,2,24,128]{3,2,1,0:T(8,128)S(1)}, u32[]{:S(2)}, u32[]{:S(2)}) collective-permute-start(f32[11,2,24,128]{3,2,1,0:T(8,128)S(1)} %get-tuple-element.27), channel_id=1, source_target_pairs={{8,16},{24,32},{40,48},{56,64},{72,80},{88,96},{104,112},{16,8},{3... | collective-permute-start | bytes 811016 | tf_op jit(solution)/shard_map/ppermute | solution.py:664
  28.3 3.2 %first_divergence.1.div = f32[10,16,24,128]{3,2,1,0:T(8,128)S(1)} custom-call(f32[10,16,24,128]{3,2,1,0:T(8,128)S(1)} %get-tuple-element.23.state, f32[10,16,128]{2,1,0:T(8,128)S(1)} %get-tuple-element.24.qx, f32[10,16,128]{2,1,0:T(8,128)S(1)} %get-tuple-element.25.qy), custom_call_target="tpu_custom_call" | custom-call | flops 20000000 | bytes 10000000 | tf_op jit(solution)/shard_map/first_divergence/pallas_call | solution.py:277
  31.5 1.3 %copy-done = f32[10,16,24,128]{3,2,1,0:T(8,128)} copy-done((f32[10,16,24,128]{3,2,1,0:T(8,128)}, f32[10,16,24,128]{3,2,1,0:T(8,128)S(1)}, u32[]{:S(2)}) %copy-start) | copy-done | bytes 1966104
  33.0 16.7 %all-to-all-done = f32[128,1,5376]{2,1,0:T(1,128)} async-done(((f32[128,1,5376]{2,1,0:T(1,128)}), f32[128,1,5376]{2,1,0:T(1,128)}, u32[]{:S(2)}, u32[]{:S(2)}) %all-to-all-start) | async-done | bytes 2752544 | tf_op jit(solution)/shard_map/all_to_all | solution.py:692
  49.7 14.5 %aggregate.1.total = f32[320,256]{1,0:T(8,128)S(1)} custom-call(f32[5376,128]{1,0:T(8,128)} %bitcast.7.slots), custom_call_target="tpu_custom_call" | custom-call | flops 12000000000 | bytes 4000000 | tf_op jit(solution)/shard_map/aggregate/pallas_call | solution.py:416
  64.5 3.8 %first_step.1 = (f32[10,16,24,128]{3,2,1,0:T(8,128)S(1)}, f32[10,2,24,128]{3,2,1,0:T(8,128)S(1)}, f32[10,2,24,128]{3,2,1,0:T(8,128)S(1)}, f32[10,24,128]{2,1,0:T...) custom-call(s32[4]{0:T(128)S(1)} %pad_add_fusion.place, f32[320,256]{1,0:T(8,128)S(1)} %aggregate.1.total, ...), custom_call_target="tpu_custom_call" | custom-call | flops 20000000 | bytes 10000000 | tf_op jit(solution)/shard_map/first_step/pallas_call | solution.py:546
  68.3 1.0 collective-permute-start.4
  69.3 3.2 %collective-permute-start.5 = (f32[10,2,24,128]{3,2,1,0:T(8,128)S(1)}, f32[10,2,24,128]{3,2,1,0:T(8,128)S(1)}, u32[]{:S(2)}, u32[]{:S(2)}) collective-permute-start(f32[10,2,24,128]{3,2,1,0:T(8,128)S(1)} %get-tuple-element.32), channel_id=1, source_target_pairs={{8,16},{24,32},{40,48},{56,64},{72,80},{88,96},{104,112},{16,8},{3... | collective-permute-start | bytes 737288 | tf_op jit(solution)/shard_map/ppermute | solution.py:664
  73.2 2.1 %collective-permute-start.6 = (f32[5,24,128]{2,1,0:T(8,128)S(1)}, f32[5,24,128]{2,1,0:T(8,128)S(1)}, u32[]{:S(2)}, u32[]{:S(2)}) collective-permute-start(f32[5,24,128]{2,1,0:T(8,128)S(1)} %get-tuple-element.34), channel_id=1, source_target_pairs={{0,1},{2,3},{4,5},{6,7},{1,0},{3,2},{5,4},{7,6},{8,9},{10,11},{12,... | collective-permute-start | bytes 184328 | tf_op jit(solution)/shard_map/ppermute | solution.py:664
  75.3 0.9 collective-permute-done.6.edges_a
  76.2 3.8 %collective-permute-done.5.received_b = f32[10,2,24,128]{3,2,1,0:T(8,128)S(1)} collective-permute-done((f32[10,2,24,128]{3,2,1,0:T(8,128)S(1)}, f32[10,2,24,128]{3,2,1,0:T(8,128)S(1)}, u32[]{:S(2)}, u32[]{:S(2)}) %collective-permute-start.5) | collective-permute-done | bytes 245792 | tf_op jit(solution)/shard_map/ppermute | solution.py:664
  80.0 5.5 %middle_step.1 = (f32[10,16,24,128]{3,2,1,0:T(8,128)S(1)}, f32[10,2,24,128]{3,2,1,0:T(8,128)S(1)}, f32[10,2,24,128]{3,2,1,0:T(8,128)S(1)}, f32[10,24,128]{2,1,0:T(8,128)S(1)}, f32[5,24,128]{2,1,0:T(8,128)S(1)}) custom-call(s32[4]{0:T(128)S(1)} %pad_add_fusion.place, f32[10,16,24,128]{3,2,1,0:T(8,128)S(1)} %get-tuple-element.30.state, ...), custom_call_target="tpu_custom_call" | custom-call | flops 30000000 | bytes 10000000 | tf_op jit(solution)/shard_map/middle_step/pallas_call | solution.py:650
  85.5 2.4 %collective-permute-start.8 = (f32[10,2,24,128]{3,2,1,0:T(8,128)S(1)}, f32[10,2,24,128]{3,2,1,0:T(8,128)S(1)}, u32[]{:S(2)}, u32[]{:S(2)}) collective-permute-start(f32[10,2,24,128]{3,2,1,0:T(8,128)S(1)} %get-tuple-element.37), channel_id=1, source_target_pairs={{0,8},{16,24},{32,40},{48,56},{64,72},{80,88},{96,104},{112,120},{... | collective-permute-start | bytes 737288 | tf_op jit(solution)/shard_map/ppermute | solution.py:664
  87.9 1.9 %collective-permute-start.9 = (f32[10,2,24,128]{3,2,1,0:T(8,128)S(1)}, f32[10,2,24,128]{3,2,1,0:T(8,128)S(1)}, u32[]{:S(2)}, u32[]{:S(2)}) collective-permute-start(f32[10,2,24,128]{3,2,1,0:T(8,128)S(1)} %get-tuple-element.38), channel_id=1, source_target_pairs={{8,16},{24,32},{40,48},{56,64},{72,80},{88,96},{104,112},{16,8},{3... | collective-permute-start | bytes 737288 | tf_op jit(solution)/shard_map/ppermute | solution.py:664
  90.5 4.0 %collective-permute-start.10 = (f32[5,24,128]{2,1,0:T(8,128)S(1)}, f32[5,24,128]{2,1,0:T(8,128)S(1)}, u32[]{:S(2)}, u32[]{:S(2)}) collective-permute-start(f32[5,24,128]{2,1,0:T(8,128)S(1)} %get-tuple-element.40), channel_id=1, source_target_pairs={{0,1},{2,3},{4,5},{6,7},{1,0},{3,2},{5,4},{7,6},{8,9},{10,11},{12,... | collective-permute-start | bytes 184328 | tf_op jit(solution)/shard_map/ppermute | solution.py:664
  94.5 0.9 collective-permute-done.10.edges_a
  95.4 5.0 %collective-permute-done.9.received_b = f32[10,2,24,128]{3,2,1,0:T(8,128)S(1)} collective-permute-done((f32[10,2,24,128]{3,2,1,0:T(8,128)S(1)}, f32[10,2,24,128]{3,2,1,0:T(8,128)S(1)}, u32[]{:S(2)}, u32[]{:S(2)}) %collective-permute-start.9) | collective-permute-done | bytes 245792 | tf_op jit(solution)/shard_map/ppermute | solution.py:664
  100.4 7.6 %last_step.1 = f32[3840,128]{1,0:T(8,128)} custom-call(s32[4]{0:T(128)S(1)} %pad_add_fusion.place, f32[10,16,24,128]{3,2,1,0:T(8,128)S(1)} %get-tuple-element.36.state, f32[10,2,24,128]{3,2,1,0:T(8,128)S(1)} %collective-permute-done.8.received_a, f32[10,2,24,128]{3,2,1,0:T(8,128)S(1)} %collective-permute-done.9.received_b, ...), custom_call_target="tpu_custom_call" | custom-call | flops 30000000 | bytes 10000000 | tf_op jit(solution)/shard_map/last_step/pallas_call | solution.py:650
  (37 shorter events, 2.5 us)
Async XLA Ops:
  3.5 10.9 %copy-start.3 = (f32[10,16,128]{2,1,0:T(8,128)S(1)}, f32[10,16,128]{2,1,0:T(8,128)}, u32[]{:S(2)}) copy-start(f32[10,16,128]{2,1,0:T(8,128)} %flow_x.1) | copy-start | bytes 245764
  3.5 10.9 %copy-start.4 = (f32[10,16,128]{2,1,0:T(8,128)S(1)}, f32[10,16,128]{2,1,0:T(8,128)}, u32[]{:S(2)}) copy-start(f32[10,16,128]{2,1,0:T(8,128)} %flow_y.1) | copy-start | bytes 245764
  3.5 10.9 %copy-start.5 = (s32[10,16,128]{2,1,0:T(8,128)S(1)}, s32[10,16,128]{2,1,0:T(8,128)}, u32[]{:S(2)}) copy-start(s32[10,16,128]{2,1,0:T(8,128)} %wet_x.1) | copy-start | bytes 245764
  3.5 10.9 %copy-start.6 = (s32[10,16,128]{2,1,0:T(8,128)S(1)}, s32[10,16,128]{2,1,0:T(8,128)}, u32[]{:S(2)}) copy-start(s32[10,16,128]{2,1,0:T(8,128)} %wet_y.1) | copy-start | bytes 245764
  3.5 46.2 %all-to-all-start = ((f32[128,1,5376]{2,1,0:T(1,128)}), f32[128,1,5376]{2,1,0:T(1,128)}, u32[]{:S(2)}, u32[]{:S(2)}) async-start(f32[128,1,5376]{2,1,0:T(1,128)} %bitcast.12), calls=%async_computation | async-start | bytes 5505024 | tf_op jit(solution)/shard_map/all_to_all | solution.py:692
  14.4 1.5 %copy-start.2 = (f32[24,10,16,128]{3,2,1,0:T(8,128)S(1)}, f32[24,10,16,128]{3,2,1,0:T(8,128)}, u32[]{:S(2)}) copy-start(f32[24,10,16,128]{3,2,1,0:T(8,128)} %param.13) | copy-start | bytes 5898244
  19.1 45.1 %collective-permute-start.3 = (f32[6,24,128]{2,1,0:T(8,128)}, f32[6,24,128]{2,1,0:T(8,128)S(1)}, u32[]{:S(2)}, u32[]{:S(2)}) collective-permute-start(f32[6,24,128]{2,1,0:T(8,128)} %get-tuple-element.29), channel_id=1, source_target_pairs={{1,2},{3,4},{5,6},{2,1},{4,3},{6,5},{9,10},{11,12},{13,14},{10,9},... | collective-permute-start | bytes 221192 | tf_op jit(solution)/shard_map/ppermute | solution.py:664
  19.8 44.5 %collective-permute-start.2 = (f32[6,24,128]{2,1,0:T(8,128)}, f32[6,24,128]{2,1,0:T(8,128)S(1)}, u32[]{:S(2)}, u32[]{:S(2)}) collective-permute-start(f32[6,24,128]{2,1,0:T(8,128)} %get-tuple-element.29), channel_id=1, source_target_pairs={{0,1},{2,3},{4,5},{6,7},{1,0},{3,2},{5,4},{7,6},{8,9},{10,11},{12,... | collective-permute-start | bytes 221192 | tf_op jit(solution)/shard_map/ppermute | solution.py:664
  22.9 41.4 %collective-permute-start = (f32[11,2,24,128]{3,2,1,0:T(8,128)S(1)}, f32[11,2,24,128]{3,2,1,0:T(8,128)S(1)}, u32[]{:S(2)}, u32[]{:S(2)}) collective-permute-start(f32[11,2,24,128]{3,2,1,0:T(8,128)S(1)} %get-tuple-element.26), channel_id=1, source_target_pairs={{0,8},{16,24},{32,40},{48,56},{64,72},{80,88},{96,104},{112,120},{... | collective-permute-start | bytes 811016 | tf_op jit(solution)/shard_map/ppermute | solution.py:664
  24.4 39.9 %collective-permute-start.1 = (f32[11,2,24,128]{3,2,1,0:T(8,128)S(1)}, f32[11,2,24,128]{3,2,1,0:T(8,128)S(1)}, u32[]{:S(2)}, u32[]{:S(2)}) collective-permute-start(f32[11,2,24,128]{3,2,1,0:T(8,128)S(1)} %get-tuple-element.27), channel_id=1, source_target_pairs={{8,16},{24,32},{40,48},{56,64},{72,80},{88,96},{104,112},{16,8},{3... | collective-permute-start | bytes 811016 | tf_op jit(solution)/shard_map/ppermute | solution.py:664
  28.3 4.5 %copy-start.10 = (f32[23]{0:T(128)S(1)}, f32[23]{0:T(128)}, u32[]{:S(2)}) copy-start(f32[23]{0:T(128)} %param.20) | copy-start | bytes 280
  31.5 1.3 %copy-start = (f32[10,16,24,128]{3,2,1,0:T(8,128)}, f32[10,16,24,128]{3,2,1,0:T(8,128)S(1)}, u32[]{:S(2)}) copy-start(f32[10,16,24,128]{3,2,1,0:T(8,128)S(1)} %first_divergence.1.div) | copy-start | bytes 5898244
  49.7 14.7 %copy-start.9 = (f32[24]{0:T(128)S(1)}, f32[24]{0:T(128)}, u32[]{:S(2)}) copy-start(f32[24]{0:T(128)} %param.21) | copy-start | bytes 292
  49.7 14.8 %copy-start.1 = (f32[10,16,24,128]{3,2,1,0:T(8,128)S(1)}, f32[10,16,24,128]{3,2,1,0:T(8,128)}, u32[]{:S(2)}) copy-start(f32[10,16,24,128]{3,2,1,0:T(8,128)} %copy-done) | copy-start | bytes 5898244
  49.7 14.8 %copy-start.7 = (f32[10,16,128]{2,1,0:T(8,128)S(1)}, f32[10,16,128]{2,1,0:T(8,128)}, u32[]{:S(2)}) copy-start(f32[10,16,128]{2,1,0:T(8,128)} %base_volume.1) | copy-start | bytes 245764
  49.7 14.8 %copy-start.8 = (f32[9,16,128]{2,1,0:T(8,128)S(1)}, f32[9,16,128]{2,1,0:T(8,128)}, u32[]{:S(2)}) copy-start(f32[9,16,128]{2,1,0:T(8,128)} %diffusivity.1) | copy-start | bytes 221188
  68.3 7.9 %collective-permute-start.4 = (f32[10,2,24,128]{3,2,1,0:T(8,128)S(1)}, f32[10,2,24,128]{3,2,1,0:T(8,128)S(1)}, u32[]{:S(2)}, u32[]{:S(2)}) collective-permute-start(f32[10,2,24,128]{3,2,1,0:T(8,128)S(1)} %get-tuple-element.31), channel_id=1, source_target_pairs={{0,8},{16,24},{32,40},{48,56},{64,72},{80,88},{96,104},{112,120},{... | collective-permute-start | bytes 737288 | tf_op jit(solution)/shard_map/ppermute | solution.py:664
  69.3 10.7 %collective-permute-start.5 = (f32[10,2,24,128]{3,2,1,0:T(8,128)S(1)}, f32[10,2,24,128]{3,2,1,0:T(8,128)S(1)}, u32[]{:S(2)}, u32[]{:S(2)}) collective-permute-start(f32[10,2,24,128]{3,2,1,0:T(8,128)S(1)} %get-tuple-element.32), channel_id=1, source_target_pairs={{8,16},{24,32},{40,48},{56,64},{72,80},{88,96},{104,112},{16,8},{3... | collective-permute-start | bytes 737288 | tf_op jit(solution)/shard_map/ppermute | solution.py:664
  72.5 2.8 %collective-permute-start.7 = (f32[5,24,128]{2,1,0:T(8,128)S(1)}, f32[5,24,128]{2,1,0:T(8,128)S(1)}, u32[]{:S(2)}, u32[]{:S(2)}) collective-permute-start(f32[5,24,128]{2,1,0:T(8,128)S(1)} %get-tuple-element.34), channel_id=1, source_target_pairs={{1,2},{3,4},{5,6},{2,1},{4,3},{6,5},{9,10},{11,12},{13,14},{10,9},... | collective-permute-start | bytes 184328 | tf_op jit(solution)/shard_map/ppermute | solution.py:664
  73.2 3.0 %collective-permute-start.6 = (f32[5,24,128]{2,1,0:T(8,128)S(1)}, f32[5,24,128]{2,1,0:T(8,128)S(1)}, u32[]{:S(2)}, u32[]{:S(2)}) collective-permute-start(f32[5,24,128]{2,1,0:T(8,128)S(1)} %get-tuple-element.34), channel_id=1, source_target_pairs={{0,1},{2,3},{4,5},{6,7},{1,0},{3,2},{5,4},{7,6},{8,9},{10,11},{12,... | collective-permute-start | bytes 184328 | tf_op jit(solution)/shard_map/ppermute | solution.py:664
  85.5 9.9 %collective-permute-start.8 = (f32[10,2,24,128]{3,2,1,0:T(8,128)S(1)}, f32[10,2,24,128]{3,2,1,0:T(8,128)S(1)}, u32[]{:S(2)}, u32[]{:S(2)}) collective-permute-start(f32[10,2,24,128]{3,2,1,0:T(8,128)S(1)} %get-tuple-element.37), channel_id=1, source_target_pairs={{0,8},{16,24},{32,40},{48,56},{64,72},{80,88},{96,104},{112,120},{... | collective-permute-start | bytes 737288 | tf_op jit(solution)/shard_map/ppermute | solution.py:664
  87.9 12.5 %collective-permute-start.9 = (f32[10,2,24,128]{3,2,1,0:T(8,128)S(1)}, f32[10,2,24,128]{3,2,1,0:T(8,128)S(1)}, u32[]{:S(2)}, u32[]{:S(2)}) collective-permute-start(f32[10,2,24,128]{3,2,1,0:T(8,128)S(1)} %get-tuple-element.38), channel_id=1, source_target_pairs={{8,16},{24,32},{40,48},{56,64},{72,80},{88,96},{104,112},{16,8},{3... | collective-permute-start | bytes 737288 | tf_op jit(solution)/shard_map/ppermute | solution.py:664
  89.8 4.7 %collective-permute-start.11 = (f32[5,24,128]{2,1,0:T(8,128)S(1)}, f32[5,24,128]{2,1,0:T(8,128)S(1)}, u32[]{:S(2)}, u32[]{:S(2)}) collective-permute-start(f32[5,24,128]{2,1,0:T(8,128)S(1)} %get-tuple-element.40), channel_id=1, source_target_pairs={{1,2},{3,4},{5,6},{2,1},{4,3},{6,5},{9,10},{11,12},{13,14},{10,9},... | collective-permute-start | bytes 184328 | tf_op jit(solution)/shard_map/ppermute | solution.py:664
  90.5 4.9 %collective-permute-start.10 = (f32[5,24,128]{2,1,0:T(8,128)S(1)}, f32[5,24,128]{2,1,0:T(8,128)S(1)}, u32[]{:S(2)}, u32[]{:S(2)}) collective-permute-start(f32[5,24,128]{2,1,0:T(8,128)S(1)} %get-tuple-element.40), channel_id=1, source_target_pairs={{0,1},{2,3},{4,5},{6,7},{1,0},{3,2},{5,4},{7,6},{8,9},{10,11},{12,... | collective-permute-start | bytes 184328 | tf_op jit(solution)/shard_map/ppermute | solution.py:664

commit v6 on v5

--- a/solution.py
+++ b/solution.py
@@ -337,6 +337,7 @@
 
 
 ROWS = 21
+PITCH_PAD = 8
 PIECES = 2
 
 
@@ -583,8 +584,10 @@
 ):
     layers, rows = qx.shape[0], qx.shape[1]
     if final:
-        out, fixes, star = refs
-        subs = out.shape[0] // (layers * rows)
+        out, fixes, star, staged, sems = refs
+        segments = layers * rows
+        subs = out.shape[0] // segments
+        pitch = staged.shape[0] // subs
     else:
         new, swap_a, swap_b, edges, sent, fixes, star = refs
     edge_pass(
@@ -630,20 +633,38 @@
 
     def emit(l, i, value):
         if final:
-            out[pl.ds(l * rows + i, subs, stride=layers * rows), :] = value
+            staged[pl.ds(l * rows + i, subs, stride=pitch), :] = value
         else:
             new[l, i] = value
 
     solve(star, coef, emit)
-    if not final:
+    if final:
+        copies = [
+            pltpu.make_async_copy(
+                staged.at[pl.ds(k * pitch, segments)],
+                out.at[pl.ds(k * segments, segments)],
+                sems.at[k],
+            )
+            for k in range(subs)
+        ]
+        for copy in copies:
+            copy.start()
+        for copy in copies:
+            copy.wait()
+    else:
         emit_edges(place, new, swap_a, swap_b, edges, sent)
 
 
 def later_step(final, place, state, *args):
     layers, rows, subs, cols = state.shape
+    scratch = [pltpu.VMEM((layers, subs, cols), F32), pltpu.VMEM(state.shape, F32)]
     if final:
+        scratch += [
+            pltpu.VMEM((subs * (layers * rows + PITCH_PAD), cols), F32),
+            pltpu.SemaphoreType.DMA((subs,)),
+        ]
         shapes = jax.ShapeDtypeStruct((subs * layers * rows, cols), F32)
-        specs = VMEM
+        specs = pl.BlockSpec(memory_space=pl.ANY)
     else:
         shapes = state_shapes(state.shape)
         specs = [VMEM] * 5
@@ -652,7 +673,7 @@
         in_specs=[SMEM] + [VMEM] * 17,
         out_specs=specs,
         out_shape=shapes,
-        scratch_shapes=[pltpu.VMEM((layers, subs, cols), F32), pltpu.VMEM(state.shape, F32)],
+        scratch_shapes=scratch,
         compiler_params=pltpu.CompilerParams(vmem_limit_bytes=VMEM_BYTES),
         cost_estimate=pl.CostEstimate(flops=3 * 10**7, bytes_accessed=10**7, transcendentals=0),
         name="last_step" if final else "middle_step",

time: 108 us -> 107 us (level)
  Pallas kernels: 41.2 us -> 40 us
    pallas_call x2, Pallas kernels: 13.1 us -> 11.8 us  [later_step(): pl.pallas_call(functools.partial(later_step_kernel, final), in_specs=[SME...]
  transfers between devices with their start and end apart: 13 -> 13, of which waited for: 5 -> 5; matrix products, arithmetic and copies ran while one was open for 0% -> 0% of each run, Pallas kernels for 19% -> 20%
where the time goes in v6:
time: 107 us
  Pallas kernels  40 us (37%)
  starting transfers between devices  35.9 us (34%)
  waiting for transfers between devices  27.4 us (26%)
  local copies, waits for them, and re-layouts  3.05 us (3%)
    ppermute x12, starting transfers between devices, swap(): return lax.ppermute(values, axis, pairs + [(j, i) for i, j in pairs])  25.1 us
    all_to_all x1, waiting for transfers between devices, local(): lax.all_to_all(slots.reshape(owners, 1, -1), ('gx', 'gy'), split_axis=0,...  16.7 us
    pallas_call x1, Pallas kernels, totals(): pl.pallas_call(totals_kernel, in_specs=[VMEM], out_specs=VMEM, out_shape=...  14.5 us
    pallas_call x2, Pallas kernels, later_step(): pl.pallas_call(functools.partial(later_step_kernel, final), in_specs=[SME...  11.8 us
    all_to_all x1, starting transfers between devices, local(): lax.all_to_all(slots.reshape(owners, 1, -1), ('gx', 'gy'), split_axis=0,...  10.7 us
    ppermute x12, waiting for transfers between devices, swap(): return lax.ppermute(values, axis, pairs + [(j, i) for i, j in pairs])  10.6 us
    pallas_call x1, Pallas kernels, first_step(): pl.pallas_call(first_step_kernel, in_specs=[SMEM] + [VMEM] * 14, out_spec...  3.76 us
    pallas_call x1, Pallas kernels, pack_slots(): pl.pallas_call(pack_kernel, grid=(groups // step,), in_specs=[pl.BlockSpe...  3.5 us
  transfers between devices with their start and end apart: 13, of which 5 were waited for; matrix products, arithmetic and copies ran while one was open for 0% of the time, Pallas kernels for 20%

profile of v6, /device:TPU:16, one launch (start us, length us, event | category | flops | bytes accessed | tf_op | source)
XLA Modules:
  0.0 106.7 jit_solution(18013255637750480612)
XLA Ops:
  0.0 3.5 %pack_slots.1 = f32[5376,128]{1,0:T(8,128)} custom-call(f32[10,32768]{1,0:T(8,128)} %volume.1, f32[10,32768]{1,0:T(8,128)} %discharge.1, s32[256,128]{1,0:T(8,128)} %bitcast.13, s32[256,128]{1,0:T(8,128)} %bitcast.14), custom_call_target="tpu_custom_call" | custom-call | bytes 8000000 | tf_op jit(solution)/shard_map/pack_slots/pallas_call | solution.py:52
  3.5 10.7 %all-to-all-start = ((f32[128,1,5376]{2,1,0:T(1,128)}), f32[128,1,5376]{2,1,0:T(1,128)}, u32[]{:S(2)}, u32[]{:S(2)}) async-start(f32[128,1,5376]{2,1,0:T(1,128)} %bitcast.12), calls=%async_computation | async-start | bytes 5505024 | tf_op jit(solution)/shard_map/all_to_all | solution.py:713
  14.4 1.5 %copy-done.2 = f32[24,10,16,128]{3,2,1,0:T(8,128)S(1)} copy-done((f32[24,10,16,128]{3,2,1,0:T(8,128)S(1)}, f32[24,10,16,128]{3,2,1,0:T(8,128)}, u32[]{:S(2)}) %copy-start.2) | copy-done | bytes 1966104
  15.9 3.2 %start_state.1 = (f32[10,16,24,128]{3,2,1,0:T(8,128)S(1)}, f32[11,2,24,128]{3,2,1,0:T(8,128)S(1)}, f32[11,2,24,128]{3,2,1,0:T(8,128)S(1)}, f32[11,24,128]{2,1,0:...) custom-call(s32[4]{0:T(128)S(1)} %pad_add_fusion.place, ...), custom_call_target="tpu_custom_call" | custom-call | flops 1000000 | bytes 8000000 | tf_op jit(solution)/shard_map/start_state/pallas_call | solution.py:189
  19.8 3.1 %collective-permute-start.2 = (f32[6,24,128]{2,1,0:T(8,128)}, f32[6,24,128]{2,1,0:T(8,128)S(1)}, u32[]{:S(2)}, u32[]{:S(2)}) collective-permute-start(f32[6,24,128]{2,1,0:T(8,128)} %get-tuple-element.29), channel_id=1, source_target_pairs={{0,1},{2,3},{4,5},{6,7},{1,0},{3,2},{5,4},{7,6},{8,9},{10,11},{12,... | collective-permute-start | bytes 221192 | tf_op jit(solution)/shard_map/ppermute | solution.py:685
  22.9 1.5 %collective-permute-start = (f32[11,2,24,128]{3,2,1,0:T(8,128)S(1)}, f32[11,2,24,128]{3,2,1,0:T(8,128)S(1)}, u32[]{:S(2)}, u32[]{:S(2)}) collective-permute-start(f32[11,2,24,128]{3,2,1,0:T(8,128)S(1)} %get-tuple-element.26), channel_id=1, source_target_pairs={{0,8},{16,24},{32,40},{48,56},{64,72},{80,88},{96,104},{112,120},{... | collective-permute-start | bytes 811016 | tf_op jit(solution)/shard_map/ppermute | solution.py:685
  24.4 3.9 %collective-permute-start.1 = (f32[11,2,24,128]{3,2,1,0:T(8,128)S(1)}, f32[11,2,24,128]{3,2,1,0:T(8,128)S(1)}, u32[]{:S(2)}, u32[]{:S(2)}) collective-permute-start(f32[11,2,24,128]{3,2,1,0:T(8,128)S(1)} %get-tuple-element.27), channel_id=1, source_target_pairs={{8,16},{24,32},{40,48},{56,64},{72,80},{88,96},{104,112},{16,8},{3... | collective-permute-start | bytes 811016 | tf_op jit(solution)/shard_map/ppermute | solution.py:685
  28.3 3.2 %first_divergence.1.div = f32[10,16,24,128]{3,2,1,0:T(8,128)S(1)} custom-call(f32[10,16,24,128]{3,2,1,0:T(8,128)S(1)} %get-tuple-element.23.state, f32[10,16,128]{2,1,0:T(8,128)S(1)} %get-tuple-element.24.qx, f32[10,16,128]{2,1,0:T(8,128)S(1)} %get-tuple-element.25.qy), custom_call_target="tpu_custom_call" | custom-call | flops 20000000 | bytes 10000000 | tf_op jit(solution)/shard_map/first_divergence/pallas_call | solution.py:277
  31.5 1.3 %copy-done = f32[10,16,24,128]{3,2,1,0:T(8,128)} copy-done((f32[10,16,24,128]{3,2,1,0:T(8,128)}, f32[10,16,24,128]{3,2,1,0:T(8,128)S(1)}, u32[]{:S(2)}) %copy-start) | copy-done | bytes 1966104
  33.0 16.7 %all-to-all-done = f32[128,1,5376]{2,1,0:T(1,128)} async-done(((f32[128,1,5376]{2,1,0:T(1,128)}), f32[128,1,5376]{2,1,0:T(1,128)}, u32[]{:S(2)}, u32[]{:S(2)}) %all-to-all-start) | async-done | bytes 2752544 | tf_op jit(solution)/shard_map/all_to_all | solution.py:713
  49.7 14.5 %aggregate.1.total = f32[320,256]{1,0:T(8,128)S(1)} custom-call(f32[5376,128]{1,0:T(8,128)} %bitcast.7.slots), custom_call_target="tpu_custom_call" | custom-call | flops 12000000000 | bytes 4000000 | tf_op jit(solution)/shard_map/aggregate/pallas_call | solution.py:417
  64.5 3.8 %first_step.1 = (f32[10,16,24,128]{3,2,1,0:T(8,128)S(1)}, f32[10,2,24,128]{3,2,1,0:T(8,128)S(1)}, f32[10,2,24,128]{3,2,1,0:T(8,128)S(1)}, f32[10,24,128]{2,1,0:T...) custom-call(s32[4]{0:T(128)S(1)} %pad_add_fusion.place, f32[320,256]{1,0:T(8,128)S(1)} %aggregate.1.total, ...), custom_call_target="tpu_custom_call" | custom-call | flops 20000000 | bytes 10000000 | tf_op jit(solution)/shard_map/first_step/pallas_call | solution.py:547
  68.3 1.0 collective-permute-start.4
  69.3 3.2 %collective-permute-start.5 = (f32[10,2,24,128]{3,2,1,0:T(8,128)S(1)}, f32[10,2,24,128]{3,2,1,0:T(8,128)S(1)}, u32[]{:S(2)}, u32[]{:S(2)}) collective-permute-start(f32[10,2,24,128]{3,2,1,0:T(8,128)S(1)} %get-tuple-element.32), channel_id=1, source_target_pairs={{8,16},{24,32},{40,48},{56,64},{72,80},{88,96},{104,112},{16,8},{3... | collective-permute-start | bytes 737288 | tf_op jit(solution)/shard_map/ppermute | solution.py:685
  73.2 2.1 %collective-permute-start.6 = (f32[5,24,128]{2,1,0:T(8,128)S(1)}, f32[5,24,128]{2,1,0:T(8,128)S(1)}, u32[]{:S(2)}, u32[]{:S(2)}) collective-permute-start(f32[5,24,128]{2,1,0:T(8,128)S(1)} %get-tuple-element.34), channel_id=1, source_target_pairs={{0,1},{2,3},{4,5},{6,7},{1,0},{3,2},{5,4},{7,6},{8,9},{10,11},{12,... | collective-permute-start | bytes 184328 | tf_op jit(solution)/shard_map/ppermute | solution.py:685
  75.3 0.9 collective-permute-done.6.edges_a
  76.2 3.8 %collective-permute-done.5.received_b = f32[10,2,24,128]{3,2,1,0:T(8,128)S(1)} collective-permute-done((f32[10,2,24,128]{3,2,1,0:T(8,128)S(1)}, f32[10,2,24,128]{3,2,1,0:T(8,128)S(1)}, u32[]{:S(2)}, u32[]{:S(2)}) %collective-permute-start.5) | collective-permute-done | bytes 245792 | tf_op jit(solution)/shard_map/ppermute | solution.py:685
  80.0 5.5 %middle_step.1 = (f32[10,16,24,128]{3,2,1,0:T(8,128)S(1)}, f32[10,2,24,128]{3,2,1,0:T(8,128)S(1)}, f32[10,2,24,128]{3,2,1,0:T(8,128)S(1)}, f32[10,24,128]{2,1,0:T(8,128)S(1)}, f32[5,24,128]{2,1,0:T(8,128)S(1)}) custom-call(s32[4]{0:T(128)S(1)} %pad_add_fusion.place, f32[10,16,24,128]{3,2,1,0:T(8,128)S(1)} %get-tuple-element.30.state, ...), custom_call_target="tpu_custom_call" | custom-call | flops 30000000 | bytes 10000000 | tf_op jit(solution)/shard_map/middle_step/pallas_call | solution.py:671
  85.5 2.4 %collective-permute-start.8 = (f32[10,2,24,128]{3,2,1,0:T(8,128)S(1)}, f32[10,2,24,128]{3,2,1,0:T(8,128)S(1)}, u32[]{:S(2)}, u32[]{:S(2)}) collective-permute-start(f32[10,2,24,128]{3,2,1,0:T(8,128)S(1)} %get-tuple-element.37), channel_id=1, source_target_pairs={{0,8},{16,24},{32,40},{48,56},{64,72},{80,88},{96,104},{112,120},{... | collective-permute-start | bytes 737288 | tf_op jit(solution)/shard_map/ppermute | solution.py:685
  87.9 1.9 %collective-permute-start.9 = (f32[10,2,24,128]{3,2,1,0:T(8,128)S(1)}, f32[10,2,24,128]{3,2,1,0:T(8,128)S(1)}, u32[]{:S(2)}, u32[]{:S(2)}) collective-permute-start(f32[10,2,24,128]{3,2,1,0:T(8,128)S(1)} %get-tuple-element.38), channel_id=1, source_target_pairs={{8,16},{24,32},{40,48},{56,64},{72,80},{88,96},{104,112},{16,8},{3... | collective-permute-start | bytes 737288 | tf_op jit(solution)/shard_map/ppermute | solution.py:685
  90.5 4.0 %collective-permute-start.10 = (f32[5,24,128]{2,1,0:T(8,128)S(1)}, f32[5,24,128]{2,1,0:T(8,128)S(1)}, u32[]{:S(2)}, u32[]{:S(2)}) collective-permute-start(f32[5,24,128]{2,1,0:T(8,128)S(1)} %get-tuple-element.40), channel_id=1, source_target_pairs={{0,1},{2,3},{4,5},{6,7},{1,0},{3,2},{5,4},{7,6},{8,9},{10,11},{12,... | collective-permute-start | bytes 184328 | tf_op jit(solution)/shard_map/ppermute | solution.py:685
  94.5 0.9 collective-permute-done.10.edges_a
  95.4 5.0 %collective-permute-done.9.received_b = f32[10,2,24,128]{3,2,1,0:T(8,128)S(1)} collective-permute-done((f32[10,2,24,128]{3,2,1,0:T(8,128)S(1)}, f32[10,2,24,128]{3,2,1,0:T(8,128)S(1)}, u32[]{:S(2)}, u32[]{:S(2)}) %collective-permute-start.9) | collective-permute-done | bytes 245792 | tf_op jit(solution)/shard_map/ppermute | solution.py:685
  100.4 6.3 %last_step.1 = f32[3840,128]{1,0:T(8,128)} custom-call(s32[4]{0:T(128)S(1)} %pad_add_fusion.place, f32[10,16,24,128]{3,2,1,0:T(8,128)S(1)} %get-tuple-element.36.state, f32[10,2,24,128]{3,2,1,0:T(8,128)S(1)} %collective-permute-done.8.received_a, f32[10,2,24,128]{3,2,1,0:T(8,128)S(1)} %collective-permute-done.9.received_b, ...), custom_call_target="tpu_custom_call" | custom-call | flops 30000000 | bytes 10000000 | tf_op jit(solution)/shard_map/last_step/pallas_call | solution.py:671
  (37 shorter events, 2.5 us)
Async XLA Ops:
  3.5 10.9 %copy-start.3 = (f32[10,16,128]{2,1,0:T(8,128)S(1)}, f32[10,16,128]{2,1,0:T(8,128)}, u32[]{:S(2)}) copy-start(f32[10,16,128]{2,1,0:T(8,128)} %flow_x.1) | copy-start | bytes 245764
  3.5 10.9 %copy-start.4 = (f32[10,16,128]{2,1,0:T(8,128)S(1)}, f32[10,16,128]{2,1,0:T(8,128)}, u32[]{:S(2)}) copy-start(f32[10,16,128]{2,1,0:T(8,128)} %flow_y.1) | copy-start | bytes 245764
  3.5 10.9 %copy-start.5 = (s32[10,16,128]{2,1,0:T(8,128)S(1)}, s32[10,16,128]{2,1,0:T(8,128)}, u32[]{:S(2)}) copy-start(s32[10,16,128]{2,1,0:T(8,128)} %wet_x.1) | copy-start | bytes 245764
  3.5 10.9 %copy-start.6 = (s32[10,16,128]{2,1,0:T(8,128)S(1)}, s32[10,16,128]{2,1,0:T(8,128)}, u32[]{:S(2)}) copy-start(s32[10,16,128]{2,1,0:T(8,128)} %wet_y.1) | copy-start | bytes 245764
  3.5 46.2 %all-to-all-start = ((f32[128,1,5376]{2,1,0:T(1,128)}), f32[128,1,5376]{2,1,0:T(1,128)}, u32[]{:S(2)}, u32[]{:S(2)}) async-start(f32[128,1,5376]{2,1,0:T(1,128)} %bitcast.12), calls=%async_computation | async-start | bytes 5505024 | tf_op jit(solution)/shard_map/all_to_all | solution.py:713
  14.4 1.5 %copy-start.2 = (f32[24,10,16,128]{3,2,1,0:T(8,128)S(1)}, f32[24,10,16,128]{3,2,1,0:T(8,128)}, u32[]{:S(2)}) copy-start(f32[24,10,16,128]{3,2,1,0:T(8,128)} %param.13) | copy-start | bytes 5898244
  19.1 45.1 %collective-permute-start.3 = (f32[6,24,128]{2,1,0:T(8,128)}, f32[6,24,128]{2,1,0:T(8,128)S(1)}, u32[]{:S(2)}, u32[]{:S(2)}) collective-permute-start(f32[6,24,128]{2,1,0:T(8,128)} %get-tuple-element.29), channel_id=1, source_target_pairs={{1,2},{3,4},{5,6},{2,1},{4,3},{6,5},{9,10},{11,12},{13,14},{10,9},... | collective-permute-start | bytes 221192 | tf_op jit(solution)/shard_map/ppermute | solution.py:685
  19.8 44.5 %collective-permute-start.2 = (f32[6,24,128]{2,1,0:T(8,128)}, f32[6,24,128]{2,1,0:T(8,128)S(1)}, u32[]{:S(2)}, u32[]{:S(2)}) collective-permute-start(f32[6,24,128]{2,1,0:T(8,128)} %get-tuple-element.29), channel_id=1, source_target_pairs={{0,1},{2,3},{4,5},{6,7},{1,0},{3,2},{5,4},{7,6},{8,9},{10,11},{12,... | collective-permute-start | bytes 221192 | tf_op jit(solution)/shard_map/ppermute | solution.py:685
  22.9 41.4 %collective-permute-start = (f32[11,2,24,128]{3,2,1,0:T(8,128)S(1)}, f32[11,2,24,128]{3,2,1,0:T(8,128)S(1)}, u32[]{:S(2)}, u32[]{:S(2)}) collective-permute-start(f32[11,2,24,128]{3,2,1,0:T(8,128)S(1)} %get-tuple-element.26), channel_id=1, source_target_pairs={{0,8},{16,24},{32,40},{48,56},{64,72},{80,88},{96,104},{112,120},{... | collective-permute-start | bytes 811016 | tf_op jit(solution)/shard_map/ppermute | solution.py:685
  24.4 39.9 %collective-permute-start.1 = (f32[11,2,24,128]{3,2,1,0:T(8,128)S(1)}, f32[11,2,24,128]{3,2,1,0:T(8,128)S(1)}, u32[]{:S(2)}, u32[]{:S(2)}) collective-permute-start(f32[11,2,24,128]{3,2,1,0:T(8,128)S(1)} %get-tuple-element.27), channel_id=1, source_target_pairs={{8,16},{24,32},{40,48},{56,64},{72,80},{88,96},{104,112},{16,8},{3... | collective-permute-start | bytes 811016 | tf_op jit(solution)/shard_map/ppermute | solution.py:685
  28.3 4.5 %copy-start.10 = (f32[23]{0:T(128)S(1)}, f32[23]{0:T(128)}, u32[]{:S(2)}) copy-start(f32[23]{0:T(128)} %param.20) | copy-start | bytes 280
  31.5 1.3 %copy-start = (f32[10,16,24,128]{3,2,1,0:T(8,128)}, f32[10,16,24,128]{3,2,1,0:T(8,128)S(1)}, u32[]{:S(2)}) copy-start(f32[10,16,24,128]{3,2,1,0:T(8,128)S(1)} %first_divergence.1.div) | copy-start | bytes 5898244
  49.7 14.7 %copy-start.9 = (f32[24]{0:T(128)S(1)}, f32[24]{0:T(128)}, u32[]{:S(2)}) copy-start(f32[24]{0:T(128)} %param.21) | copy-start | bytes 292
  49.7 14.8 %copy-start.1 = (f32[10,16,24,128]{3,2,1,0:T(8,128)S(1)}, f32[10,16,24,128]{3,2,1,0:T(8,128)}, u32[]{:S(2)}) copy-start(f32[10,16,24,128]{3,2,1,0:T(8,128)} %copy-done) | copy-start | bytes 5898244
  49.7 14.8 %copy-start.7 = (f32[10,16,128]{2,1,0:T(8,128)S(1)}, f32[10,16,128]{2,1,0:T(8,128)}, u32[]{:S(2)}) copy-start(f32[10,16,128]{2,1,0:T(8,128)} %base_volume.1) | copy-start | bytes 245764
  49.7 14.8 %copy-start.8 = (f32[9,16,128]{2,1,0:T(8,128)S(1)}, f32[9,16,128]{2,1,0:T(8,128)}, u32[]{:S(2)}) copy-start(f32[9,16,128]{2,1,0:T(8,128)} %diffusivity.1) | copy-start | bytes 221188
  68.3 7.9 %collective-permute-start.4 = (f32[10,2,24,128]{3,2,1,0:T(8,128)S(1)}, f32[10,2,24,128]{3,2,1,0:T(8,128)S(1)}, u32[]{:S(2)}, u32[]{:S(2)}) collective-permute-start(f32[10,2,24,128]{3,2,1,0:T(8,128)S(1)} %get-tuple-element.31), channel_id=1, source_target_pairs={{0,8},{16,24},{32,40},{48,56},{64,72},{80,88},{96,104},{112,120},{... | collective-permute-start | bytes 737288 | tf_op jit(solution)/shard_map/ppermute | solution.py:685
  69.3 10.7 %collective-permute-start.5 = (f32[10,2,24,128]{3,2,1,0:T(8,128)S(1)}, f32[10,2,24,128]{3,2,1,0:T(8,128)S(1)}, u32[]{:S(2)}, u32[]{:S(2)}) collective-permute-start(f32[10,2,24,128]{3,2,1,0:T(8,128)S(1)} %get-tuple-element.32), channel_id=1, source_target_pairs={{8,16},{24,32},{40,48},{56,64},{72,80},{88,96},{104,112},{16,8},{3... | collective-permute-start | bytes 737288 | tf_op jit(solution)/shard_map/ppermute | solution.py:685
  72.5 2.8 %collective-permute-start.7 = (f32[5,24,128]{2,1,0:T(8,128)S(1)}, f32[5,24,128]{2,1,0:T(8,128)S(1)}, u32[]{:S(2)}, u32[]{:S(2)}) collective-permute-start(f32[5,24,128]{2,1,0:T(8,128)S(1)} %get-tuple-element.34), channel_id=1, source_target_pairs={{1,2},{3,4},{5,6},{2,1},{4,3},{6,5},{9,10},{11,12},{13,14},{10,9},... | collective-permute-start | bytes 184328 | tf_op jit(solution)/shard_map/ppermute | solution.py:685
  73.2 3.0 %collective-permute-start.6 = (f32[5,24,128]{2,1,0:T(8,128)S(1)}, f32[5,24,128]{2,1,0:T(8,128)S(1)}, u32[]{:S(2)}, u32[]{:S(2)}) collective-permute-start(f32[5,24,128]{2,1,0:T(8,128)S(1)} %get-tuple-element.34), channel_id=1, source_target_pairs={{0,1},{2,3},{4,5},{6,7},{1,0},{3,2},{5,4},{7,6},{8,9},{10,11},{12,... | collective-permute-start | bytes 184328 | tf_op jit(solution)/shard_map/ppermute | solution.py:685
  85.5 9.9 %collective-permute-start.8 = (f32[10,2,24,128]{3,2,1,0:T(8,128)S(1)}, f32[10,2,24,128]{3,2,1,0:T(8,128)S(1)}, u32[]{:S(2)}, u32[]{:S(2)}) collective-permute-start(f32[10,2,24,128]{3,2,1,0:T(8,128)S(1)} %get-tuple-element.37), channel_id=1, source_target_pairs={{0,8},{16,24},{32,40},{48,56},{64,72},{80,88},{96,104},{112,120},{... | collective-permute-start | bytes 737288 | tf_op jit(solution)/shard_map/ppermute | solution.py:685
  87.9 12.5 %collective-permute-start.9 = (f32[10,2,24,128]{3,2,1,0:T(8,128)S(1)}, f32[10,2,24,128]{3,2,1,0:T(8,128)S(1)}, u32[]{:S(2)}, u32[]{:S(2)}) collective-permute-start(f32[10,2,24,128]{3,2,1,0:T(8,128)S(1)} %get-tuple-element.38), channel_id=1, source_target_pairs={{8,16},{24,32},{40,48},{56,64},{72,80},{88,96},{104,112},{16,8},{3... | collective-permute-start | bytes 737288 | tf_op jit(solution)/shard_map/ppermute | solution.py:685
  89.8 4.7 %collective-permute-start.11 = (f32[5,24,128]{2,1,0:T(8,128)S(1)}, f32[5,24,128]{2,1,0:T(8,128)S(1)}, u32[]{:S(2)}, u32[]{:S(2)}) collective-permute-start(f32[5,24,128]{2,1,0:T(8,128)S(1)} %get-tuple-element.40), channel_id=1, source_target_pairs={{1,2},{3,4},{5,6},{2,1},{4,3},{6,5},{9,10},{11,12},{13,14},{10,9},... | collective-permute-start | bytes 184328 | tf_op jit(solution)/shard_map/ppermute | solution.py:685
  90.5 4.9 %collective-permute-start.10 = (f32[5,24,128]{2,1,0:T(8,128)S(1)}, f32[5,24,128]{2,1,0:T(8,128)S(1)}, u32[]{:S(2)}, u32[]{:S(2)}) collective-permute-start(f32[5,24,128]{2,1,0:T(8,128)S(1)} %get-tuple-element.40), channel_id=1, source_target_pairs={{0,1},{2,3},{4,5},{6,7},{1,0},{3,2},{5,4},{7,6},{8,9},{10,11},{12,... | collective-permute-start | bytes 184328 | tf_op jit(solution)/shard_map/ppermute | solution.py:685

commit v7 on v6

--- a/solution.py
+++ b/solution.py
@@ -413,7 +413,7 @@
 
 
 def totals(slots):
-    depth = min(2048, slots.shape[0] // ROWS * 64)
+    depth = min(4096, slots.shape[0] // ROWS * 64)
     return pl.pallas_call(
         totals_kernel,
         in_specs=[VMEM],

time: 107 us -> 107 us (level)
  no operation moved by 1% of the time
where the time goes in v7:
time: 107 us
  Pallas kernels  40 us (37%)
  starting transfers between devices  35.9 us (34%)
  waiting for transfers between devices  27.4 us (26%)
  local copies, waits for them, and re-layouts  3.05 us (3%)
    ppermute x12, starting transfers between devices, swap(): return lax.ppermute(values, axis, pairs + [(j, i) for i, j in pairs])  25.2 us
    all_to_all x1, waiting for transfers between devices, local(): lax.all_to_all(slots.reshape(owners, 1, -1), ('gx', 'gy'), split_axis=0,...  16.7 us
    pallas_call x1, Pallas kernels, totals(): pl.pallas_call(totals_kernel, in_specs=[VMEM], out_specs=VMEM, out_shape=...  14.5 us
    pallas_call x2, Pallas kernels, later_step(): pl.pallas_call(functools.partial(later_step_kernel, final), in_specs=[SME...  11.8 us
    all_to_all x1, starting transfers between devices, local(): lax.all_to_all(slots.reshape(owners, 1, -1), ('gx', 'gy'), split_axis=0,...  10.7 us
    ppermute x12, waiting for transfers between devices, swap(): return lax.ppermute(values, axis, pairs + [(j, i) for i, j in pairs])  10.6 us
    pallas_call x1, Pallas kernels, first_step(): pl.pallas_call(first_step_kernel, in_specs=[SMEM] + [VMEM] * 14, out_spec...  3.76 us
    pallas_call x1, Pallas kernels, pack_slots(): pl.pallas_call(pack_kernel, grid=(groups // step,), in_specs=[pl.BlockSpe...  3.5 us
  transfers between devices with their start and end apart: 13, of which 5 were waited for; matrix products, arithmetic and copies ran while one was open for 0% of the time, Pallas kernels for 20%

profile of v7, /device:TPU:16, one launch (start us, length us, event | category | flops | bytes accessed | tf_op | source)
XLA Modules:
  0.0 106.7 jit_solution(16199991274705098822)
XLA Ops:
  0.0 3.5 %pack_slots.1 = f32[5376,128]{1,0:T(8,128)} custom-call(f32[10,32768]{1,0:T(8,128)} %volume.1, f32[10,32768]{1,0:T(8,128)} %discharge.1, s32[256,128]{1,0:T(8,128)} %bitcast.13, s32[256,128]{1,0:T(8,128)} %bitcast.14), custom_call_target="tpu_custom_call" | custom-call | bytes 8000000 | tf_op jit(solution)/shard_map/pack_slots/pallas_call | solution.py:52
  3.5 10.7 %all-to-all-start = ((f32[128,1,5376]{2,1,0:T(1,128)}), f32[128,1,5376]{2,1,0:T(1,128)}, u32[]{:S(2)}, u32[]{:S(2)}) async-start(f32[128,1,5376]{2,1,0:T(1,128)} %bitcast.12), calls=%async_computation | async-start | bytes 5505024 | tf_op jit(solution)/shard_map/all_to_all | solution.py:713
  14.4 1.5 %copy-done.2 = f32[24,10,16,128]{3,2,1,0:T(8,128)S(1)} copy-done((f32[24,10,16,128]{3,2,1,0:T(8,128)S(1)}, f32[24,10,16,128]{3,2,1,0:T(8,128)}, u32[]{:S(2)}) %copy-start.2) | copy-done | bytes 1966104
  15.9 3.2 %start_state.1 = (f32[10,16,24,128]{3,2,1,0:T(8,128)S(1)}, f32[11,2,24,128]{3,2,1,0:T(8,128)S(1)}, f32[11,2,24,128]{3,2,1,0:T(8,128)S(1)}, f32[11,24,128]{2,1,0:...) custom-call(s32[4]{0:T(128)S(1)} %pad_add_fusion.place, ...), custom_call_target="tpu_custom_call" | custom-call | flops 1000000 | bytes 8000000 | tf_op jit(solution)/shard_map/start_state/pallas_call | solution.py:189
  19.8 3.1 %collective-permute-start.2 = (f32[6,24,128]{2,1,0:T(8,128)}, f32[6,24,128]{2,1,0:T(8,128)S(1)}, u32[]{:S(2)}, u32[]{:S(2)}) collective-permute-start(f32[6,24,128]{2,1,0:T(8,128)} %get-tuple-element.29), channel_id=1, source_target_pairs={{0,1},{2,3},{4,5},{6,7},{1,0},{3,2},{5,4},{7,6},{8,9},{10,11},{12,... | collective-permute-start | bytes 221192 | tf_op jit(solution)/shard_map/ppermute | solution.py:685
  22.9 1.5 %collective-permute-start = (f32[11,2,24,128]{3,2,1,0:T(8,128)S(1)}, f32[11,2,24,128]{3,2,1,0:T(8,128)S(1)}, u32[]{:S(2)}, u32[]{:S(2)}) collective-permute-start(f32[11,2,24,128]{3,2,1,0:T(8,128)S(1)} %get-tuple-element.26), channel_id=1, source_target_pairs={{0,8},{16,24},{32,40},{48,56},{64,72},{80,88},{96,104},{112,120},{... | collective-permute-start | bytes 811016 | tf_op jit(solution)/shard_map/ppermute | solution.py:685
  24.4 3.9 %collective-permute-start.1 = (f32[11,2,24,128]{3,2,1,0:T(8,128)S(1)}, f32[11,2,24,128]{3,2,1,0:T(8,128)S(1)}, u32[]{:S(2)}, u32[]{:S(2)}) collective-permute-start(f32[11,2,24,128]{3,2,1,0:T(8,128)S(1)} %get-tuple-element.27), channel_id=1, source_target_pairs={{8,16},{24,32},{40,48},{56,64},{72,80},{88,96},{104,112},{16,8},{3... | collective-permute-start | bytes 811016 | tf_op jit(solution)/shard_map/ppermute | solution.py:685
  28.3 3.2 %first_divergence.1.div = f32[10,16,24,128]{3,2,1,0:T(8,128)S(1)} custom-call(f32[10,16,24,128]{3,2,1,0:T(8,128)S(1)} %get-tuple-element.23.state, f32[10,16,128]{2,1,0:T(8,128)S(1)} %get-tuple-element.24.qx, f32[10,16,128]{2,1,0:T(8,128)S(1)} %get-tuple-element.25.qy), custom_call_target="tpu_custom_call" | custom-call | flops 20000000 | bytes 10000000 | tf_op jit(solution)/shard_map/first_divergence/pallas_call | solution.py:277
  31.5 1.3 %copy-done = f32[10,16,24,128]{3,2,1,0:T(8,128)} copy-done((f32[10,16,24,128]{3,2,1,0:T(8,128)}, f32[10,16,24,128]{3,2,1,0:T(8,128)S(1)}, u32[]{:S(2)}) %copy-start) | copy-done | bytes 1966104
  33.0 16.7 %all-to-all-done = f32[128,1,5376]{2,1,0:T(1,128)} async-done(((f32[128,1,5376]{2,1,0:T(1,128)}), f32[128,1,5376]{2,1,0:T(1,128)}, u32[]{:S(2)}, u32[]{:S(2)}) %all-to-all-start) | async-done | bytes 2752544 | tf_op jit(solution)/shard_map/all_to_all | solution.py:713
  49.7 14.5 %aggregate.1.total = f32[320,256]{1,0:T(8,128)S(1)} custom-call(f32[5376,128]{1,0:T(8,128)} %bitcast.7.slots), custom_call_target="tpu_custom_call" | custom-call | flops 12000000000 | bytes 4000000 | tf_op jit(solution)/shard_map/aggregate/pallas_call | solution.py:417
  64.5 3.8 %first_step.1 = (f32[10,16,24,128]{3,2,1,0:T(8,128)S(1)}, f32[10,2,24,128]{3,2,1,0:T(8,128)S(1)}, f32[10,2,24,128]{3,2,1,0:T(8,128)S(1)}, f32[10,24,128]{2,1,0:T...) custom-call(s32[4]{0:T(128)S(1)} %pad_add_fusion.place, f32[320,256]{1,0:T(8,128)S(1)} %aggregate.1.total, ...), custom_call_target="tpu_custom_call" | custom-call | flops 20000000 | bytes 10000000 | tf_op jit(solution)/shard_map/first_step/pallas_call | solution.py:547
  68.3 1.0 collective-permute-start.4
  69.3 3.2 %collective-permute-start.5 = (f32[10,2,24,128]{3,2,1,0:T(8,128)S(1)}, f32[10,2,24,128]{3,2,1,0:T(8,128)S(1)}, u32[]{:S(2)}, u32[]{:S(2)}) collective-permute-start(f32[10,2,24,128]{3,2,1,0:T(8,128)S(1)} %get-tuple-element.32), channel_id=1, source_target_pairs={{8,16},{24,32},{40,48},{56,64},{72,80},{88,96},{104,112},{16,8},{3... | collective-permute-start | bytes 737288 | tf_op jit(solution)/shard_map/ppermute | solution.py:685
  73.2 2.1 %collective-permute-start.6 = (f32[5,24,128]{2,1,0:T(8,128)S(1)}, f32[5,24,128]{2,1,0:T(8,128)S(1)}, u32[]{:S(2)}, u32[]{:S(2)}) collective-permute-start(f32[5,24,128]{2,1,0:T(8,128)S(1)} %get-tuple-element.34), channel_id=1, source_target_pairs={{0,1},{2,3},{4,5},{6,7},{1,0},{3,2},{5,4},{7,6},{8,9},{10,11},{12,... | collective-permute-start | bytes 184328 | tf_op jit(solution)/shard_map/ppermute | solution.py:685
  75.3 0.9 collective-permute-done.6.edges_a
  76.2 3.8 %collective-permute-done.5.received_b = f32[10,2,24,128]{3,2,1,0:T(8,128)S(1)} collective-permute-done((f32[10,2,24,128]{3,2,1,0:T(8,128)S(1)}, f32[10,2,24,128]{3,2,1,0:T(8,128)S(1)}, u32[]{:S(2)}, u32[]{:S(2)}) %collective-permute-start.5) | collective-permute-done | bytes 245792 | tf_op jit(solution)/shard_map/ppermute | solution.py:685
  80.0 5.5 %middle_step.1 = (f32[10,16,24,128]{3,2,1,0:T(8,128)S(1)}, f32[10,2,24,128]{3,2,1,0:T(8,128)S(1)}, f32[10,2,24,128]{3,2,1,0:T(8,128)S(1)}, f32[10,24,128]{2,1,0:T(8,128)S(1)}, f32[5,24,128]{2,1,0:T(8,128)S(1)}) custom-call(s32[4]{0:T(128)S(1)} %pad_add_fusion.place, f32[10,16,24,128]{3,2,1,0:T(8,128)S(1)} %get-tuple-element.30.state, ...), custom_call_target="tpu_custom_call" | custom-call | flops 30000000 | bytes 10000000 | tf_op jit(solution)/shard_map/middle_step/pallas_call | solution.py:671
  85.5 2.4 %collective-permute-start.8 = (f32[10,2,24,128]{3,2,1,0:T(8,128)S(1)}, f32[10,2,24,128]{3,2,1,0:T(8,128)S(1)}, u32[]{:S(2)}, u32[]{:S(2)}) collective-permute-start(f32[10,2,24,128]{3,2,1,0:T(8,128)S(1)} %get-tuple-element.37), channel_id=1, source_target_pairs={{0,8},{16,24},{32,40},{48,56},{64,72},{80,88},{96,104},{112,120},{... | collective-permute-start | bytes 737288 | tf_op jit(solution)/shard_map/ppermute | solution.py:685
  87.9 1.9 %collective-permute-start.9 = (f32[10,2,24,128]{3,2,1,0:T(8,128)S(1)}, f32[10,2,24,128]{3,2,1,0:T(8,128)S(1)}, u32[]{:S(2)}, u32[]{:S(2)}) collective-permute-start(f32[10,2,24,128]{3,2,1,0:T(8,128)S(1)} %get-tuple-element.38), channel_id=1, source_target_pairs={{8,16},{24,32},{40,48},{56,64},{72,80},{88,96},{104,112},{16,8},{3... | collective-permute-start | bytes 737288 | tf_op jit(solution)/shard_map/ppermute | solution.py:685
  90.5 4.0 %collective-permute-start.10 = (f32[5,24,128]{2,1,0:T(8,128)S(1)}, f32[5,24,128]{2,1,0:T(8,128)S(1)}, u32[]{:S(2)}, u32[]{:S(2)}) collective-permute-start(f32[5,24,128]{2,1,0:T(8,128)S(1)} %get-tuple-element.40), channel_id=1, source_target_pairs={{0,1},{2,3},{4,5},{6,7},{1,0},{3,2},{5,4},{7,6},{8,9},{10,11},{12,... | collective-permute-start | bytes 184328 | tf_op jit(solution)/shard_map/ppermute | solution.py:685
  94.5 0.9 collective-permute-done.10.edges_a
  95.4 5.0 %collective-permute-done.9.received_b = f32[10,2,24,128]{3,2,1,0:T(8,128)S(1)} collective-permute-done((f32[10,2,24,128]{3,2,1,0:T(8,128)S(1)}, f32[10,2,24,128]{3,2,1,0:T(8,128)S(1)}, u32[]{:S(2)}, u32[]{:S(2)}) %collective-permute-start.9) | collective-permute-done | bytes 245792 | tf_op jit(solution)/shard_map/ppermute | solution.py:685
  100.4 6.3 %last_step.1 = f32[3840,128]{1,0:T(8,128)} custom-call(s32[4]{0:T(128)S(1)} %pad_add_fusion.place, f32[10,16,24,128]{3,2,1,0:T(8,128)S(1)} %get-tuple-element.36.state, f32[10,2,24,128]{3,2,1,0:T(8,128)S(1)} %collective-permute-done.8.received_a, f32[10,2,24,128]{3,2,1,0:T(8,128)S(1)} %collective-permute-done.9.received_b, ...), custom_call_target="tpu_custom_call" | custom-call | flops 30000000 | bytes 10000000 | tf_op jit(solution)/shard_map/last_step/pallas_call | solution.py:671
  (37 shorter events, 2.5 us)
Async XLA Ops:
  3.5 10.9 %copy-start.3 = (f32[10,16,128]{2,1,0:T(8,128)S(1)}, f32[10,16,128]{2,1,0:T(8,128)}, u32[]{:S(2)}) copy-start(f32[10,16,128]{2,1,0:T(8,128)} %flow_x.1) | copy-start | bytes 245764
  3.5 10.9 %copy-start.4 = (f32[10,16,128]{2,1,0:T(8,128)S(1)}, f32[10,16,128]{2,1,0:T(8,128)}, u32[]{:S(2)}) copy-start(f32[10,16,128]{2,1,0:T(8,128)} %flow_y.1) | copy-start | bytes 245764
  3.5 10.9 %copy-start.5 = (s32[10,16,128]{2,1,0:T(8,128)S(1)}, s32[10,16,128]{2,1,0:T(8,128)}, u32[]{:S(2)}) copy-start(s32[10,16,128]{2,1,0:T(8,128)} %wet_x.1) | copy-start | bytes 245764
  3.5 10.9 %copy-start.6 = (s32[10,16,128]{2,1,0:T(8,128)S(1)}, s32[10,16,128]{2,1,0:T(8,128)}, u32[]{:S(2)}) copy-start(s32[10,16,128]{2,1,0:T(8,128)} %wet_y.1) | copy-start | bytes 245764
  3.5 46.2 %all-to-all-start = ((f32[128,1,5376]{2,1,0:T(1,128)}), f32[128,1,5376]{2,1,0:T(1,128)}, u32[]{:S(2)}, u32[]{:S(2)}) async-start(f32[128,1,5376]{2,1,0:T(1,128)} %bitcast.12), calls=%async_computation | async-start | bytes 5505024 | tf_op jit(solution)/shard_map/all_to_all | solution.py:713
  14.4 1.5 %copy-start.2 = (f32[24,10,16,128]{3,2,1,0:T(8,128)S(1)}, f32[24,10,16,128]{3,2,1,0:T(8,128)}, u32[]{:S(2)}) copy-start(f32[24,10,16,128]{3,2,1,0:T(8,128)} %param.13) | copy-start | bytes 5898244
  19.1 45.1 %collective-permute-start.3 = (f32[6,24,128]{2,1,0:T(8,128)}, f32[6,24,128]{2,1,0:T(8,128)S(1)}, u32[]{:S(2)}, u32[]{:S(2)}) collective-permute-start(f32[6,24,128]{2,1,0:T(8,128)} %get-tuple-element.29), channel_id=1, source_target_pairs={{1,2},{3,4},{5,6},{2,1},{4,3},{6,5},{9,10},{11,12},{13,14},{10,9},... | collective-permute-start | bytes 221192 | tf_op jit(solution)/shard_map/ppermute | solution.py:685
  19.8 44.5 %collective-permute-start.2 = (f32[6,24,128]{2,1,0:T(8,128)}, f32[6,24,128]{2,1,0:T(8,128)S(1)}, u32[]{:S(2)}, u32[]{:S(2)}) collective-permute-start(f32[6,24,128]{2,1,0:T(8,128)} %get-tuple-element.29), channel_id=1, source_target_pairs={{0,1},{2,3},{4,5},{6,7},{1,0},{3,2},{5,4},{7,6},{8,9},{10,11},{12,... | collective-permute-start | bytes 221192 | tf_op jit(solution)/shard_map/ppermute | solution.py:685
  22.9 41.4 %collective-permute-start = (f32[11,2,24,128]{3,2,1,0:T(8,128)S(1)}, f32[11,2,24,128]{3,2,1,0:T(8,128)S(1)}, u32[]{:S(2)}, u32[]{:S(2)}) collective-permute-start(f32[11,2,24,128]{3,2,1,0:T(8,128)S(1)} %get-tuple-element.26), channel_id=1, source_target_pairs={{0,8},{16,24},{32,40},{48,56},{64,72},{80,88},{96,104},{112,120},{... | collective-permute-start | bytes 811016 | tf_op jit(solution)/shard_map/ppermute | solution.py:685
  24.4 39.9 %collective-permute-start.1 = (f32[11,2,24,128]{3,2,1,0:T(8,128)S(1)}, f32[11,2,24,128]{3,2,1,0:T(8,128)S(1)}, u32[]{:S(2)}, u32[]{:S(2)}) collective-permute-start(f32[11,2,24,128]{3,2,1,0:T(8,128)S(1)} %get-tuple-element.27), channel_id=1, source_target_pairs={{8,16},{24,32},{40,48},{56,64},{72,80},{88,96},{104,112},{16,8},{3... | collective-permute-start | bytes 811016 | tf_op jit(solution)/shard_map/ppermute | solution.py:685
  28.3 4.5 %copy-start.10 = (f32[23]{0:T(128)S(1)}, f32[23]{0:T(128)}, u32[]{:S(2)}) copy-start(f32[23]{0:T(128)} %param.20) | copy-start | bytes 280
  31.5 1.3 %copy-start = (f32[10,16,24,128]{3,2,1,0:T(8,128)}, f32[10,16,24,128]{3,2,1,0:T(8,128)S(1)}, u32[]{:S(2)}) copy-start(f32[10,16,24,128]{3,2,1,0:T(8,128)S(1)} %first_divergence.1.div) | copy-start | bytes 5898244
  49.7 14.7 %copy-start.9 = (f32[24]{0:T(128)S(1)}, f32[24]{0:T(128)}, u32[]{:S(2)}) copy-start(f32[24]{0:T(128)} %param.21) | copy-start | bytes 292
  49.7 14.8 %copy-start.1 = (f32[10,16,24,128]{3,2,1,0:T(8,128)S(1)}, f32[10,16,24,128]{3,2,1,0:T(8,128)}, u32[]{:S(2)}) copy-start(f32[10,16,24,128]{3,2,1,0:T(8,128)} %copy-done) | copy-start | bytes 5898244
  49.7 14.8 %copy-start.7 = (f32[10,16,128]{2,1,0:T(8,128)S(1)}, f32[10,16,128]{2,1,0:T(8,128)}, u32[]{:S(2)}) copy-start(f32[10,16,128]{2,1,0:T(8,128)} %base_volume.1) | copy-start | bytes 245764
  49.7 14.8 %copy-start.8 = (f32[9,16,128]{2,1,0:T(8,128)S(1)}, f32[9,16,128]{2,1,0:T(8,128)}, u32[]{:S(2)}) copy-start(f32[9,16,128]{2,1,0:T(8,128)} %diffusivity.1) | copy-start | bytes 221188
  68.3 7.9 %collective-permute-start.4 = (f32[10,2,24,128]{3,2,1,0:T(8,128)S(1)}, f32[10,2,24,128]{3,2,1,0:T(8,128)S(1)}, u32[]{:S(2)}, u32[]{:S(2)}) collective-permute-start(f32[10,2,24,128]{3,2,1,0:T(8,128)S(1)} %get-tuple-element.31), channel_id=1, source_target_pairs={{0,8},{16,24},{32,40},{48,56},{64,72},{80,88},{96,104},{112,120},{... | collective-permute-start | bytes 737288 | tf_op jit(solution)/shard_map/ppermute | solution.py:685
  69.3 10.7 %collective-permute-start.5 = (f32[10,2,24,128]{3,2,1,0:T(8,128)S(1)}, f32[10,2,24,128]{3,2,1,0:T(8,128)S(1)}, u32[]{:S(2)}, u32[]{:S(2)}) collective-permute-start(f32[10,2,24,128]{3,2,1,0:T(8,128)S(1)} %get-tuple-element.32), channel_id=1, source_target_pairs={{8,16},{24,32},{40,48},{56,64},{72,80},{88,96},{104,112},{16,8},{3... | collective-permute-start | bytes 737288 | tf_op jit(solution)/shard_map/ppermute | solution.py:685
  72.5 2.8 %collective-permute-start.7 = (f32[5,24,128]{2,1,0:T(8,128)S(1)}, f32[5,24,128]{2,1,0:T(8,128)S(1)}, u32[]{:S(2)}, u32[]{:S(2)}) collective-permute-start(f32[5,24,128]{2,1,0:T(8,128)S(1)} %get-tuple-element.34), channel_id=1, source_target_pairs={{1,2},{3,4},{5,6},{2,1},{4,3},{6,5},{9,10},{11,12},{13,14},{10,9},... | collective-permute-start | bytes 184328 | tf_op jit(solution)/shard_map/ppermute | solution.py:685
  73.2 3.0 %collective-permute-start.6 = (f32[5,24,128]{2,1,0:T(8,128)S(1)}, f32[5,24,128]{2,1,0:T(8,128)S(1)}, u32[]{:S(2)}, u32[]{:S(2)}) collective-permute-start(f32[5,24,128]{2,1,0:T(8,128)S(1)} %get-tuple-element.34), channel_id=1, source_target_pairs={{0,1},{2,3},{4,5},{6,7},{1,0},{3,2},{5,4},{7,6},{8,9},{10,11},{12,... | collective-permute-start | bytes 184328 | tf_op jit(solution)/shard_map/ppermute | solution.py:685
  85.5 9.9 %collective-permute-start.8 = (f32[10,2,24,128]{3,2,1,0:T(8,128)S(1)}, f32[10,2,24,128]{3,2,1,0:T(8,128)S(1)}, u32[]{:S(2)}, u32[]{:S(2)}) collective-permute-start(f32[10,2,24,128]{3,2,1,0:T(8,128)S(1)} %get-tuple-element.37), channel_id=1, source_target_pairs={{0,8},{16,24},{32,40},{48,56},{64,72},{80,88},{96,104},{112,120},{... | collective-permute-start | bytes 737288 | tf_op jit(solution)/shard_map/ppermute | solution.py:685
  87.9 12.5 %collective-permute-start.9 = (f32[10,2,24,128]{3,2,1,0:T(8,128)S(1)}, f32[10,2,24,128]{3,2,1,0:T(8,128)S(1)}, u32[]{:S(2)}, u32[]{:S(2)}) collective-permute-start(f32[10,2,24,128]{3,2,1,0:T(8,128)S(1)} %get-tuple-element.38), channel_id=1, source_target_pairs={{8,16},{24,32},{40,48},{56,64},{72,80},{88,96},{104,112},{16,8},{3... | collective-permute-start | bytes 737288 | tf_op jit(solution)/shard_map/ppermute | solution.py:685
  89.8 4.7 %collective-permute-start.11 = (f32[5,24,128]{2,1,0:T(8,128)S(1)}, f32[5,24,128]{2,1,0:T(8,128)S(1)}, u32[]{:S(2)}, u32[]{:S(2)}) collective-permute-start(f32[5,24,128]{2,1,0:T(8,128)S(1)} %get-tuple-element.40), channel_id=1, source_target_pairs={{1,2},{3,4},{5,6},{2,1},{4,3},{6,5},{9,10},{11,12},{13,14},{10,9},... | collective-permute-start | bytes 184328 | tf_op jit(solution)/shard_map/ppermute | solution.py:685
  90.5 4.9 %collective-permute-start.10 = (f32[5,24,128]{2,1,0:T(8,128)S(1)}, f32[5,24,128]{2,1,0:T(8,128)S(1)}, u32[]{:S(2)}, u32[]{:S(2)}) collective-permute-start(f32[5,24,128]{2,1,0:T(8,128)S(1)} %get-tuple-element.40), channel_id=1, source_target_pairs={{0,1},{2,3},{4,5},{6,7},{1,0},{3,2},{5,4},{7,6},{8,9},{10,11},{12,... | collective-permute-start | bytes 184328 | tf_op jit(solution)/shard_map/ppermute | solution.py:685
